TPU v7x, 32 devices: a whole 2x2x4 slice. The times are simulated.
32 devices in a mesh: groups: 2 (over y), tgt: 4 (over z), src: 2 (over x), sub: 2 (over core).
Axes of the slice: x: 2, y: 2, z: 4, core: 2. Of those that a mesh axis runs over, the one named last changes fastest.
Arguments:
- points: float32 [3, 4096], P(None, ('groups', 'tgt', 'src', 'sub')), parts along dimension 1, may hold values from -1.4 to 1.4, as said below
- density: float32 [32, 4096], P(None, ('groups', 'tgt', 'src', 'sub')), parts along dimension 1, may hold values from 0.2 to 2
- incident: float32 [32, 4096], P(None, ('groups', 'tgt', 'src', 'sub')), parts along dimension 1, may hold values from -0.21 to 0.21
- precond: float32 [4096], P(('groups', 'tgt', 'src', 'sub')), parts along dimension 0, may hold values from 0.054414064 to 0.16324219
- receivers: int32 [4096], P('groups'), parts along dimension 0, may hold values from 0 to 65535
Outputs:
- density_out: float32 [32, 4096], P(None, ('groups', 'tgt', 'src', 'sub')), parts along dimension 1
- far_field: float32 [32, 4096], P(None, ('groups', 'tgt', 'src', 'sub')), parts along dimension 1
There are 2 independent parts, one for each index of `groups`. A program takes and returns all parts, laid end to end along the dimension named above; each array names one. Nothing has to cross between parts.
Inputs may be any that keep to these rules, and one draw needn't show every extreme that they name: Coordinates of points of a closed star-shaped surface around the anchor. `receivers`: numbers of directions in the receiver table.
All inputs are finite; a program needn't handle non-finite values.
Results may differ from a plain program's by a relative error of at most 0.0015.
Values may be sent and summed in bfloat16 or wider, within the bound.
No kernel may reach another device: no remote copies, remote signals or barrier semaphores. Data moves between devices by JAX's collectives and lax.ppermute only.
A program may use at most 64 MiB of HBM per device.

v0:
```python
import math

import jax
import jax.numpy as jnp
from jax import lax
from jax.sharding import PartitionSpec as P

ITERS = 4
NDIR = 65536


WAVENUMBER = 32.0
SMOOTHING = 0.02
FOUR_PI = 4.0 * math.pi


def single_layer(targets, sources):
    delta_x = targets[0][:, None] - sources[0][None, :]
    delta_y = targets[1][:, None] - sources[1][None, :]
    delta_z = targets[2][:, None] - sources[2][None, :]
    squared = delta_x * delta_x + delta_y * delta_y + delta_z * delta_z
    values = jnp.cos(WAVENUMBER * jnp.sqrt(squared)) / (
        FOUR_PI * jnp.sqrt(squared + SMOOTHING * SMOOTHING)
    )
    return values.astype(jnp.bfloat16)


def far_kernel(toward, sources):
    projection = toward[0][:, None] * sources[0][None, :] + toward[1][:, None] * sources[1][None, :]
    projection = projection + toward[2][:, None] * sources[2][None, :]
    return jnp.cos(WAVENUMBER * projection).astype(jnp.bfloat16)


def receiver_directions(direction_index):
    upper_part = direction_index // 256
    lower_part = direction_index % 256
    rotation = (upper_part * 14080 + lower_part * 40503) % 65536
    azimuth = rotation.astype(jnp.float32) * (2.0 * math.pi / 65536.0)
    height = 1.0 - (2 * direction_index + 1).astype(jnp.float32) / NDIR
    radial = jnp.sqrt(jnp.maximum(1.0 - height * height, 0.0))
    return jnp.stack([radial * jnp.cos(azimuth), radial * jnp.sin(azimuth), height])


def fold_blocks(running, incoming, coordinates, targets, maker):
    length = incoming.shape[1]
    block_width = math.gcd(length, 1024)

    def fold_one_block(number, accumulated):
        inside = number * block_width
        part_density = lax.dynamic_slice_in_dim(incoming, inside, block_width, 1)
        part_points = lax.dynamic_slice_in_dim(coordinates, inside, block_width, 1)
        kernel_table = maker(targets, part_points)
        return accumulated + lax.dot_general(
            part_density, kernel_table, (((1,), (1,)), ((), ())), preferred_element_type=jnp.float32
        )

    return lax.fori_loop(0, length // block_width, fold_one_block, running)


def build_table(targets, sources):
    source_count = sources.shape[1]
    block_width = math.gcd(source_count, 1024)
    table = jnp.zeros((targets.shape[1], source_count), jnp.bfloat16)

    def build_one_block(number, filled):
        inside = number * block_width
        part_points = lax.dynamic_slice_in_dim(sources, inside, block_width, 1)
        return lax.dynamic_update_slice_in_dim(
            filled, single_layer(targets, part_points), inside, 1
        )

    return lax.fori_loop(0, source_count // block_width, build_one_block, table)


def shards(points, density, incident, precond, receivers):
    count_tgt = lax.axis_size("tgt")
    count_src = lax.axis_size("src")
    count_sub = lax.axis_size("sub")
    point_count = points.shape[1] * count_tgt * count_src * count_sub
    cell_area = FOUR_PI / point_count
    row_points = lax.all_gather(points, "src", axis=1, tiled=True)
    column_points = lax.all_gather(points, ("tgt", "sub"), axis=1, tiled=True)
    columns_count = density.shape[0]
    stored_table = build_table(row_points, column_points)
    for iteration in range(ITERS):
        weighted = (density * cell_area).astype(jnp.bfloat16)
        partial_sum = lax.dot_general(
            lax.all_gather(weighted, ("tgt", "sub"), axis=1, tiled=True),
            stored_table,
            (((1,), (1,)), ((), ())),
            preferred_element_type=jnp.float32,
        )
        field = lax.psum_scatter(partial_sum, "src", scatter_dimension=1, tiled=True)
        density = density - (field + incident) / precond[None, :]
    weighted = (density * cell_area).astype(jnp.bfloat16)
    receiver_blocks = receivers.reshape(count_tgt, count_src, count_sub, -1)
    picked = lax.dynamic_index_in_dim(receiver_blocks, lax.axis_index("tgt"), 0, keepdims=False)
    picked = lax.dynamic_index_in_dim(picked, lax.axis_index("sub"), 1, keepdims=False)
    toward = receiver_directions(picked.reshape(-1))
    empty_far = jnp.zeros((columns_count, toward.shape[1]), jnp.float32)
    far_partial = fold_blocks(
        empty_far,
        lax.all_gather(weighted, ("tgt", "sub"), axis=1, tiled=True),
        column_points,
        toward,
        far_kernel,
    )
    far_field = lax.psum_scatter(far_partial, "src", scatter_dimension=1, tiled=True)
    return (density, far_field)


def solution(mesh):
    placed = (
        P(None, ("groups", "tgt", "src", "sub")),
        P(None, ("groups", "tgt", "src", "sub")),
        P(None, ("groups", "tgt", "src", "sub")),
        P(("groups", "tgt", "src", "sub")),
        P("groups"),
    )
    return jax.shard_map(
        shards,
        mesh=mesh,
        in_specs=placed,
        out_specs=(
            P(None, ("groups", "tgt", "src", "sub")),
            P(None, ("groups", "tgt", "src", "sub")),
        ),
        check_vma=False,
    )
```

profile of v0, /device:TPU:0, one launch (start us, length us, event | category | flops | bytes accessed | tf_op | source)
XLA Modules:
  0.0 169.7 jit_solution(17720902413788426603)
XLA Ops:
  7.2 0.0 copy-start
  7.2 0.0 copy-start.6
  7.2 0.0 reduce-scatter.6.cloned.1.call-start
  7.2 14.5 %all_gather.23 = f32[3,1024]{1,0:T(4,128)S(1)} all-gather(f32[3,128]{1,0:T(4,128)} %param.5), channel_id=1, replica_groups=mesh['groups'=2,'tgt'=4,'src'=2,'sub'=2] {'tgt','sub'}, dimensions={1}, use_global_device_ids=true | all-gather | bytes 13824 | tf_op jit(solution)/shard_map/all_gather | solution.py:82
  21.8 0.0 copy-done.6
  21.8 4.3 %all_gather.22 = f32[3,256]{1,0:T(4,128)S(1)} all-gather(f32[3,128]{1,0:T(4,128)S(1)} %copy-done.6), channel_id=1, replica_groups=mesh['groups'=2,'tgt'=4,'src'=2,'sub'=2] {'src'}, dimensions={1}, use_global_device_ids=true | all-gather | bytes 4608 | tf_op jit(solution)/shard_map/all_gather | solution.py:81
  26.1 0.0 copy-start.2
  26.1 0.7 copy-done.2
  26.8 12.7 %all_gather.21 = bf16[32,1024]{1,0:T(8,128)(2,1)S(1)} all-gather(bf16[32,128]{1,0:T(8,128)(2,1)S(1)} %multiply_convert_fusion.4), channel_id=1, replica_groups=mesh['groups'=2,'tgt'=4,'src'=2,'sub'=2] {'tgt','sub'}, dimensions={1}, use_global_device_ids=true | all-gather | bytes 73728 | tf_op jit(solution)/shard_map/all_gather | solution.py:88
  39.5 5.2 %fusion.10 = f32[32,256]{1,0:T(8,128)} fusion(bf16[32,1024]{1,0:T(8,128)(2,1)S(1)} %all_gather.21, f32[1024]{0:T(1024)S(1)} %bitcast.21, f32[256]{0:T(256)S(1)} %bitcast.35, f32[1024]{0:T(1024)S(1)} %bitcast.26, f32[256]{0:T(256)S(1)} %bitcast.39, f32[1024]{0:T(1024)S(1)} %bitcast.16, f32[256]{0:T(256)S(1)} %bitcast.31), kind=kOutput, calls=%fused_computation.34 | convolution fusion | flops 20185088 | bytes 113664 | tf_op jit(solution)/shard_map/dot_general | solution.py:87
  44.7 0.0 reduce-scatter.6.cloned.1.call-update
  44.7 0.0 copy-start.1
  44.7 0.0 reduce-scatter.8.cloned.1.call-start
  44.8 0.0 copy-start.5
  44.8 8.5 %reduce-scatter.6.cloned.1.call-done = f32[32,128]{1,0:T(8,128)} async-done(((f32[32,256]{1,0:T(8,128)}), f32[32,128]{1,0:T(8,128)}) %reduce-scatter.6.cloned.1.call-update) | async-done | bytes 16400 | tf_op jit(solution)/shard_map/reduce_scatter | solution.py:93
  53.3 0.0 copy-done.1
  53.3 0.0 copy-done.5
  53.3 0.7 multiply_convert_fusion.3
  54.0 12.7 %all_gather.24 = bf16[32,1024]{1,0:T(8,128)(2,1)S(1)} all-gather(bf16[32,128]{1,0:T(8,128)(2,1)S(1)} %multiply_convert_fusion.3), channel_id=1, replica_groups=mesh['groups'=2,'tgt'=4,'src'=2,'sub'=2] {'tgt','sub'}, dimensions={1}, use_global_device_ids=true | all-gather | bytes 73728 | tf_op jit(solution)/shard_map/all_gather | solution.py:88
  66.7 5.2 %fusion.9 = f32[32,256]{1,0:T(8,128)} fusion(bf16[32,1024]{1,0:T(8,128)(2,1)S(1)} %all_gather.24, f32[1024]{0:T(1024)S(1)} %bitcast.22, f32[256]{0:T(256)S(1)} %bitcast.36, f32[1024]{0:T(1024)S(1)} %bitcast.27, f32[256]{0:T(256)S(1)} %bitcast.40, f32[1024]{0:T(1024)S(1)} %bitcast.17, f32[256]{0:T(256)S(1)} %bitcast.32), kind=kOutput, calls=%fused_computation.33 | convolution fusion | flops 20185088 | bytes 113664 | tf_op jit(solution)/shard_map/dot_general | solution.py:87
  71.9 0.0 copy-start.3
  71.9 0.0 reduce-scatter.8.cloned.1.call-update
  72.0 0.0 reduce-scatter.10.cloned.1.call-start
  72.0 0.0 copy-done
  72.0 8.7 %reduce-scatter.8.cloned.1.call-done = f32[32,128]{1,0:T(8,128)} async-done(((f32[32,256]{1,0:T(8,128)}), f32[32,128]{1,0:T(8,128)}) %reduce-scatter.8.cloned.1.call-update) | async-done | bytes 16400 | tf_op jit(solution)/shard_map/reduce_scatter | solution.py:93
  80.7 0.0 copy-done.3
  80.7 0.7 multiply_convert_fusion.2
  81.5 12.9 %all_gather.25 = bf16[32,1024]{1,0:T(8,128)(2,1)S(1)} all-gather(bf16[32,128]{1,0:T(8,128)(2,1)S(1)} %get-tuple-element.37), channel_id=1, replica_groups=mesh['groups'=2,'tgt'=4,'src'=2,'sub'=2] {'tgt','sub'}, dimensions={1}, use_global_device_ids=true | all-gather | bytes 73728 | tf_op jit(solution)/shard_map/all_gather | solution.py:88
  94.4 5.2 %fusion.8 = f32[32,256]{1,0:T(8,128)} fusion(bf16[32,1024]{1,0:T(8,128)(2,1)S(1)} %all_gather.25, f32[1024]{0:T(1024)S(1)} %bitcast.23, f32[256]{0:T(256)S(1)} %bitcast.37, f32[1024]{0:T(1024)S(1)} %bitcast.28, f32[256]{0:T(256)S(1)} %bitcast.41, f32[1024]{0:T(1024)S(1)} %bitcast.18, f32[256]{0:T(256)S(1)} %bitcast.33), kind=kOutput, calls=%fused_computation.32 | convolution fusion | flops 20185088 | bytes 113664 | tf_op jit(solution)/shard_map/dot_general | solution.py:87
  99.6 0.0 reduce-scatter.10.cloned.1.call-update
  99.6 0.0 reduce-scatter.12.cloned.1.call-start
  99.7 0.1 cosine_multiply_fusion
  99.7 8.6 %reduce-scatter.10.cloned.1.call-done = f32[32,128]{1,0:T(8,128)} async-done(((f32[32,256]{1,0:T(8,128)}), f32[32,128]{1,0:T(8,128)}) %reduce-scatter.10.cloned.1.call-update) | async-done | bytes 16400 | tf_op jit(solution)/shard_map/reduce_scatter | solution.py:93
  108.3 0.7 multiply_convert_fusion.1
  109.1 12.7 %all_gather.26 = bf16[32,1024]{1,0:T(8,128)(2,1)S(1)} all-gather(bf16[32,128]{1,0:T(8,128)(2,1)S(1)} %multiply_convert_fusion.1), channel_id=1, replica_groups=mesh['groups'=2,'tgt'=4,'src'=2,'sub'=2] {'tgt','sub'}, dimensions={1}, use_global_device_ids=true | all-gather | bytes 73728 | tf_op jit(solution)/shard_map/all_gather | solution.py:88
  121.8 5.2 %fusion.7 = f32[32,256]{1,0:T(8,128)} fusion(bf16[32,1024]{1,0:T(8,128)(2,1)S(1)} %all_gather.26, f32[1024]{0:T(1024)S(1)} %bitcast.24, f32[256]{0:T(256)S(1)} %bitcast.38, f32[1024]{0:T(1024)S(1)} %bitcast.29, f32[256]{0:T(256)S(1)} %bitcast.42, f32[1024]{0:T(1024)S(1)} %bitcast.19, f32[256]{0:T(256)S(1)} %bitcast.34), kind=kOutput, calls=%fused_computation.31 | convolution fusion | flops 20185088 | bytes 113664 | tf_op jit(solution)/shard_map/dot_general | solution.py:87
  127.0 0.0 copy-start.4
  127.0 0.0 reduce-scatter.12.cloned.1.call-update
  127.0 0.0 reduce-scatter.14.cloned.1.call-start
  127.1 8.7 %reduce-scatter.12.cloned.1.call-done = f32[32,128]{1,0:T(8,128)} async-done(((f32[32,256]{1,0:T(8,128)}), f32[32,128]{1,0:T(8,128)}) %reduce-scatter.12.cloned.1.call-update) | async-done | bytes 16400 | tf_op jit(solution)/shard_map/reduce_scatter | solution.py:93
  135.8 0.0 copy-done.4
  135.8 1.3 multiply_convert_fusion
  137.1 12.9 %all_gather.27 = bf16[32,1024]{1,0:T(8,128)(2,1)S(1)} all-gather(bf16[32,128]{1,0:T(8,128)(2,1)S(1)} %get-tuple-element.27), channel_id=1, replica_groups=mesh['groups'=2,'tgt'=4,'src'=2,'sub'=2] {'tgt','sub'}, dimensions={1}, use_global_device_ids=true | all-gather | bytes 73728 | tf_op jit(solution)/shard_map/all_gather | solution.py:103
  150.0 4.4 %fusion = f32[32,256]{1,0:T(8,128)} fusion(bf16[32,1024]{1,0:T(8,128)(2,1)S(1)} %all_gather.27, f32[256]{0:T(256)S(1)} %get-tuple-element.54, f32[256]{0:T(256)S(1)} %get-tuple-element.53, f32[256]{0:T(256)S(1)} %get-tuple-element.25, f32[1024]{0:T(1024)S(1)} %bitcast.25, f32[1024]{0:T(1024)S(1)} %bitcast.30, f32[1024]{0:T(1024)S(1)} %bitcast.20), kind=kOutput, calls=%fused_computation.2 | convolution fusion | flops 18612224 | bytes 113664 | tf_op jit(solution)/shard_map/while/body/eval_jaxpr/dot_general | solution.py:53
  154.4 0.0 reduce-scatter.14.cloned.1.call-update
  154.5 8.7 %reduce-scatter.14.cloned.1.call-done = f32[32,128]{1,0:T(8,128)} async-done(((f32[32,256]{1,0:T(8,128)}), f32[32,128]{1,0:T(8,128)}) %reduce-scatter.14.cloned.1.call-update) | async-done | bytes 16400 | tf_op jit(solution)/shard_map/reduce_scatter | solution.py:108
  (5 shorter events, 0.1 us)
Async XLA Ops:
  7.2 64.8 %copy-start = (s32[2048]{0:T(1024)S(1)}, s32[2048]{0:T(1024)}, u32[]{:S(2)}) copy-start(s32[2048]{0:T(1024)} %param.9) | copy-start | bytes 24580
  7.2 14.6 %copy-start.6 = (f32[3,128]{1,0:T(4,128)S(1)}, f32[3,128]{1,0:T(4,128)}, u32[]{:S(2)}) copy-start(f32[3,128]{1,0:T(4,128)} %param.5) | copy-start | bytes 4612
  7.2 46.1 %reduce-scatter.6.cloned.1.call-start = ((), (), s32[]{:S(2)}) async-start(), calls=%async_computation.5 | async-start | bytes 49152 | tf_op jit(solution)/shard_map/reduce_scatter | solution.py:93
  26.1 0.7 copy-start.2
  44.7 8.6 %copy-start.1 = (f32[32,128]{1,0:T(8,128)S(1)}, f32[32,128]{1,0:T(8,128)}, u32[]{:S(2)}) copy-start(f32[32,128]{1,0:T(8,128)} %param.7) | copy-start | bytes 49156
  44.7 36.0 %reduce-scatter.8.cloned.1.call-start = ((), (), s32[]{:S(2)}) async-start(), calls=%async_computation.6 | async-start | bytes 49152 | tf_op jit(solution)/shard_map/reduce_scatter | solution.py:93
  44.8 8.5 %copy-start.5 = (f32[128]{0:T(128)S(1)}, f32[128]{0:T(128)}, u32[]{:S(2)}) copy-start(f32[128]{0:T(128)} %param.8) | copy-start | bytes 1540
  71.9 8.8 %copy-start.3 = (f32[32,128]{1,0:T(8,128)S(1)}, f32[32,128]{1,0:T(8,128)}, u32[]{:S(2)}) copy-start(f32[32,128]{1,0:T(8,128)} %reduce-scatter.6.cloned.1.call-done) | copy-start | bytes 49156
  72.0 36.4 %reduce-scatter.10.cloned.1.call-start = ((), (), s32[]{:S(2)}) async-start(), calls=%async_computation.7 | async-start | bytes 49152 | tf_op jit(solution)/shard_map/reduce_scatter | solution.py:93
  99.6 36.2 %reduce-scatter.12.cloned.1.call-start = ((), (), s32[]{:S(2)}) async-start(), calls=%async_computation.8 | async-start | bytes 49152 | tf_op jit(solution)/shard_map/reduce_scatter | solution.py:93
  127.0 8.8 %copy-start.4 = (f32[32,128]{1,0:T(8,128)S(1)}, f32[32,128]{1,0:T(8,128)}, u32[]{:S(2)}) copy-start(f32[32,128]{1,0:T(8,128)} %reduce-scatter.10.cloned.1.call-done) | copy-start | bytes 49156
  127.0 36.2 %reduce-scatter.14.cloned.1.call-start = ((), (), s32[]{:S(2)}) async-start(), calls=%async_computation.9 | async-start | bytes 49152 | tf_op jit(solution)/shard_map/reduce_scatter | solution.py:108
Sparse Core Ops, SparseCore 0:
  44.8 8.4 reduce-scatter.5
  72.1 8.5 reduce-scatter.7
  99.7 8.5 reduce-scatter.9
  127.1 8.5 reduce-scatter.11
  154.6 8.5 reduce-scatter.13
where the time goes:
time: 170 us
  blocking collectives  82.8 us (49%)
  waiting for transfers between devices  43.3 us (25%)
  matrix products  25.2 us (15%)
  between operations  13.9 us (8%)
  other arithmetic  3.62 us (2%)
    all_gather x5, blocking collectives, shards(): lax.all_gather(weighted, ('tgt', 'sub'), axis=1, tiled=True)  64 us
    reduce_scatter x4, waiting for transfers between devices, shards(): lax.psum_scatter(partial_sum, 'src', scatter_dimension=1, tiled=True)  34.5 us
    dot_general x4, matrix products, shards(): lax.dot_general(lax.all_gather(weighted, ('tgt', 'sub'), axis=1, tiled=Tr...  20.8 us
    all_gather x1, blocking collectives, shards(): column_points = lax.all_gather(points, ('tgt', 'sub'), axis=1, tiled=True)  14.5 us
    reduce_scatter x1, waiting for transfers between devices, shards(): lax.psum_scatter(far_partial, 'src', scatter_dimension=1, tiled=True)  8.74 us
    dot_general x1, matrix products, fold_one_block(): lax.dot_general(part_density, kernel_table, (((1,), (1,)), ((), ())), pre...  4.39 us
    all_gather x1, blocking collectives, shards(): row_points = lax.all_gather(points, 'src', axis=1, tiled=True)  4.33 us
    convert_element_type x5, other arithmetic, shards(): weighted = (density * cell_area).astype(jnp.bfloat16)  3.52 us
  transfers between devices with their start and end apart: 5, of which 5 were waited for; matrix products, arithmetic and copies ran while one was open for 0% of the time, Pallas kernels for 0%

commit v1 on v0

--- a/solution.py
+++ b/solution.py
@@ -3,6 +3,8 @@
 import jax
 import jax.numpy as jnp
 from jax import lax
+from jax.experimental import pallas as pl
+from jax.experimental.pallas import tpu as pltpu
 from jax.sharding import PartitionSpec as P
 
 ITERS = 4
@@ -12,6 +14,221 @@
 WAVENUMBER = 32.0
 SMOOTHING = 0.02
 FOUR_PI = 4.0 * math.pi
+
+TURNS = WAVENUMBER / (2.0 * math.pi)
+SMOOTH_TURNS = (SMOOTHING * TURNS) ** 2
+BLOCK = 256
+TABLE_LIMIT = 24 * 2**20
+VMEM_LIMIT = 56 * 2**20
+
+
+def sine_coefficients(count):
+    nodes = [0.03125 + 0.03125 * math.cos(math.pi * (k + 0.5) / count) for k in range(count)]
+    values = [math.sin(2.0 * math.pi * math.sqrt(u)) / math.sqrt(u) for u in nodes]
+    divided = list(values)
+    for level in range(1, count):
+        for k in range(count - 1, level - 1, -1):
+            divided[k] = (divided[k] - divided[k - 1]) / (nodes[k] - nodes[k - level])
+    poly = [0.0] * count
+    for k in range(count - 1, -1, -1):
+        shifted = [0.0] + poly[:-1]
+        poly = [s - nodes[k] * p for s, p in zip(shifted, poly)]
+        poly[0] += divided[k]
+    return poly
+
+
+SINE = sine_coefficients(4)
+
+
+def cos_turns(turns, scale):
+    folded = 0.25 - jnp.abs(turns - jnp.round(turns))
+    square = folded * folded
+    value = SINE[-1] * scale
+    for c in SINE[-2::-1]:
+        value = value * square + c * scale
+    return value * folded
+
+
+def green(squared):
+    kept = jnp.maximum(squared, 1e-12)
+    turns = kept * lax.rsqrt(kept)
+    return (cos_turns(turns, TURNS / FOUR_PI) * lax.rsqrt(squared + SMOOTH_TURNS)).astype(jnp.bfloat16)
+
+
+def split3(x):
+    high = x.astype(jnp.bfloat16).astype(jnp.float32)
+    rest = x - high
+    mid = rest.astype(jnp.bfloat16).astype(jnp.float32)
+    low = (rest - mid).astype(jnp.bfloat16).astype(jnp.float32)
+    return high, mid, low
+
+
+def replicated_kernel(counts, *refs):
+    blocks, points_row, columns = counts
+    data = refs[:blocks]
+    toward_ref = refs[blocks]
+    density_out, far_out = refs[blocks + 1 : blocks + 3]
+    lhs, rhs, table, half_table, plane, dens, inc = refs[blocks + 3 : blocks + 10]
+    stage = refs[blocks + 10 :]
+    total = blocks * BLOCK
+    shards_per_block = data[0].shape[0]
+    width = data[0].shape[2]
+    full = blocks // 2
+
+    def lanes(start, count):
+        return jnp.concatenate(
+            [data[b][s, start : start + count, :] for b in range(blocks) for s in range(shards_per_block)], axis=1
+        )
+
+    head = lanes(0, 8)
+    coords = head[0:3] * TURNS
+    inverse = 1.0 / head[3:4]
+    dens[...] = lanes(8, columns)
+    inc[...] = lanes(8 + columns, columns)
+
+    ones = jnp.ones((1, total), jnp.float32)
+    left, right = [], []
+    for k in range(3):
+        h, m, l = split3(coords[k : k + 1])
+        left += [-2.0 * h, -2.0 * h, -2.0 * m, -2.0 * m, -2.0 * h, -2.0 * l]
+        right += [h, m, h, m, l, h]
+    norm = coords[0:1] * coords[0:1] + coords[1:2] * coords[1:2] + coords[2:3] * coords[2:3]
+    h, m, l = split3(norm)
+    left += [h, m, l, ones, ones, ones]
+    right += [ones, ones, ones, h, m, l]
+    zeros = jnp.zeros((8, total), jnp.float32)
+    left = jnp.concatenate(left + [zeros], axis=0)
+    rhs[...] = jnp.concatenate(right + [zeros], axis=0).astype(jnp.bfloat16)
+    lhs[...] = left.T.astype(jnp.bfloat16)
+
+    def distances(row, count, column):
+        return lax.dot_general(
+            lhs[pl.ds(pl.multiple_of(row, 128), count), :],
+            rhs[:, pl.ds(pl.multiple_of(column, BLOCK), BLOCK)],
+            (((1,), (0,)), ((), ())),
+            preferred_element_type=jnp.float32,
+        )
+
+    def fill(block, d, source):
+        for r in range(0, BLOCK, 32):
+            table[block, d, r : r + 32, :] = green(source[r : r + 32, :])
+
+    stage[0][...] = distances(0, BLOCK, 0)
+
+    def one_row(block, carry):
+        for d in range(1, full):
+            stage[d][...] = distances(block * BLOCK, BLOCK, lax.rem(block + d, blocks) * BLOCK)
+            fill(block, d - 1, stage[d - 1])
+        low = lax.rem(block, full)
+        part = block // full
+        stage[full][...] = distances(low * BLOCK + part * 128, 128, (low + full) * BLOCK)
+        fill(block, full - 1, stage[full - 1])
+        following = lax.rem(block + 1, blocks) * BLOCK
+        stage[0][...] = distances(following, BLOCK, following)
+        base = pl.multiple_of(part * 128, 128)
+        for r in range(0, 128, 32):
+            half_table[low, pl.ds(base + r, 32), :] = green(stage[full][r : r + 32, :])
+        return carry
+
+    lax.fori_loop(0, blocks, one_row, 0)
+
+    toward = toward_ref[...].T
+    for b in range(blocks):
+        span = slice(b * BLOCK, (b + 1) * BLOCK)
+        phase = toward[:, 0:1] * coords[0:1, span] + toward[:, 1:2] * coords[1:2, span]
+        phase = phase + toward[:, 2:3] * coords[2:3, span]
+        plane[:, span] = cos_turns(phase, 1.0).astype(jnp.bfloat16)
+
+    cell_area = FOUR_PI / total
+
+    def rounded():
+        return (dens[...] * cell_area).astype(jnp.bfloat16)
+
+    def product(w, b, kernel_block, dim):
+        return lax.dot_general(
+            w[:, b * BLOCK : (b + 1) * BLOCK],
+            kernel_block,
+            (((1,), (dim,)), ((), ())),
+            preferred_element_type=jnp.float32,
+        )
+
+    def iterate(step, carry):
+        w = rounded()
+        for b in range(blocks):
+            field = product(w, b, table[b, 0], 1)
+            for d in range(1, full):
+                field += product(w, (b + d) % blocks, table[b, d], 1)
+                field += product(w, (b - d) % blocks, table[(b - d) % blocks, d], 0)
+            if b < full:
+                field += product(w, b + full, half_table[b], 1)
+            else:
+                field += product(w, b - full, half_table[b - full], 0)
+            span = slice(b * BLOCK, (b + 1) * BLOCK)
+            dens[:, span] = dens[:, span] - (field + inc[:, span]) * inverse[:, span]
+        return carry
+
+    lax.fori_loop(0, ITERS, iterate, 0)
+    density_out[...] = dens[:, 0:width]
+    w = rounded()
+    far_out[...] = lax.dot_general(
+        w, plane[...], (((1,), (1,)), ((), ())), preferred_element_type=jnp.float32
+    )
+
+
+def replicated_shards(points, density, incident, precond, receivers):
+    count_tgt = lax.axis_size("tgt")
+    count_src = lax.axis_size("src")
+    count_sub = lax.axis_size("sub")
+    chips = count_tgt * count_src
+    columns, width = density.shape
+    names = ("tgt", "src", "sub")
+    payload = jnp.concatenate(
+        [points, precond[None, :], jnp.zeros((4, width), jnp.float32), density, incident], axis=0
+    )
+    swap = [(0, 1), (1, 0)]
+    own = jnp.stack([payload, lax.ppermute(payload, "sub", swap)])
+
+    def fetch(offsets):
+        pairs = [(q * 2 + c, (q ^ offsets[c]) * 2 + c) for q in range(chips) for c in range(2)]
+        return lax.ppermute(own, names, pairs)
+
+    held = [own]
+    for k in range(1, chips - 1, 2):
+        near = fetch((k, k + 1))
+        held += [near, lax.ppermute(near, "sub", swap)]
+    held.append(fetch((chips - 1, chips - 1)))
+
+    place = (lax.axis_index("tgt") * count_src + lax.axis_index("src")) * count_sub + lax.axis_index("sub")
+    rows = receivers.shape[0] // (chips * count_sub)
+    toward = receiver_directions(lax.dynamic_slice_in_dim(receivers, place * rows, rows, 0))
+    toward = jnp.concatenate([toward, jnp.zeros((5, rows), jnp.float32)], axis=0)
+
+    blocks = len(held)
+    total = blocks * BLOCK
+    full = blocks // 2
+    vmem = pl.BlockSpec(memory_space=pltpu.VMEM)
+    return pl.pallas_call(
+        lambda *refs: replicated_kernel((blocks, 8, columns), *refs),
+        out_shape=(
+            jax.ShapeDtypeStruct((columns, width), jnp.float32),
+            jax.ShapeDtypeStruct((columns, rows), jnp.float32),
+        ),
+        in_specs=[vmem] * (blocks + 1),
+        out_specs=(vmem, vmem),
+        scratch_shapes=[
+            pltpu.VMEM((total, 32), jnp.bfloat16),
+            pltpu.VMEM((32, total), jnp.bfloat16),
+            pltpu.VMEM((blocks, full, BLOCK, BLOCK), jnp.bfloat16),
+            pltpu.VMEM((full, BLOCK, BLOCK), jnp.bfloat16),
+            pltpu.VMEM((rows, total), jnp.bfloat16),
+            pltpu.VMEM((columns, total), jnp.float32),
+            pltpu.VMEM((columns, total), jnp.float32),
+        ]
+        + [pltpu.VMEM((BLOCK, BLOCK), jnp.float32) for _ in range(full)]
+        + [pltpu.VMEM((128, BLOCK), jnp.float32)],
+        compiler_params=pltpu.CompilerParams(vmem_limit_bytes=VMEM_LIMIT),
+        name="iterate",
+    )(*held, toward)
 
 
 def single_layer(targets, sources):
@@ -72,7 +289,7 @@
     return lax.fori_loop(0, source_count // block_width, build_one_block, table)
 
 
-def shards(points, density, incident, precond, receivers):
+def shared_shards(points, density, incident, precond, receivers):
     count_tgt = lax.axis_size("tgt")
     count_src = lax.axis_size("src")
     count_sub = lax.axis_size("sub")
@@ -109,6 +326,20 @@
     return (density, far_field)
 
 
+def can_replicate(mesh, points):
+    sizes = mesh.shape
+    chips = sizes["tgt"] * sizes["src"]
+    per_group = chips * sizes["sub"]
+    total = points.shape[1] // sizes["groups"]
+    return (
+        sizes["sub"] == 2
+        and chips >= 2
+        and chips & (chips - 1) == 0
+        and total == per_group * (BLOCK // 2)
+        and total * total <= TABLE_LIMIT
+    )
+
+
 def solution(mesh):
     placed = (
         P(None, ("groups", "tgt", "src", "sub")),
@@ -117,13 +348,18 @@
         P(("groups", "tgt", "src", "sub")),
         P("groups"),
     )
-    return jax.shard_map(
-        shards,
-        mesh=mesh,
-        in_specs=placed,
-        out_specs=(
-            P(None, ("groups", "tgt", "src", "sub")),
-            P(None, ("groups", "tgt", "src", "sub")),
-        ),
-        check_vma=False,
-    )
+
+    def whole(points, density, incident, precond, receivers):
+        body = replicated_shards if can_replicate(mesh, points) else shared_shards
+        return jax.shard_map(
+            body,
+            mesh=mesh,
+            in_specs=placed,
+            out_specs=(
+                P(None, ("groups", "tgt", "src", "sub")),
+                P(None, ("groups", "tgt", "src", "sub")),
+            ),
+            check_vma=False,
+        )(points, density, incident, precond, receivers)
+
+    return whole

time: 170 us -> 39.9 us (0.23)
  blocking collectives: 82.8 us -> 0 us
  waiting for transfers between devices: 43.3 us -> 5.91 us
  matrix products: 25.2 us -> 0 us
  Pallas kernels: 0 us -> 18.9 us
  between operations: 13.9 us -> 0.75 us
  starting transfers between devices: 0.2 us -> 8.93 us
  local copies, waits for them, and re-layouts: 0.75 us -> 3.45 us
  other arithmetic: 3.62 us -> 1.52 us
    all_gather x7 -> x0, blocking collectives: 82.8 us -> none  [the longest x5 64 us: shards(): lax.all_gather(weighted, ('tgt', 'sub'), axis=1, tiled=True)]
    reduce_scatter x5 -> x0, waiting for transfers between devices: 43.2 us -> none  [the longest x4 34.5 us: shards(): lax.psum_scatter(partial_sum, 'src', scatter_dimension=1, tiled=True)]
    dot_general x5 -> x0, matrix products: 25.2 us -> none  [the longest x4 20.8 us: shards(): lax.dot_general(lax.all_gather(weighted, ('tgt', 'sub'), axis=1, tiled=Tr...]
    pallas_call x0 -> x1, Pallas kernels: none -> 18.9 us  [replicated_shards(): pl.pallas_call(lambda *refs: replicated_kernel((blocks, 8, columns), *ref...]
    ppermute x0 -> x8, starting transfers between devices: none -> 8.93 us  [the longest x4 7.97 us: fetch(): return lax.ppermute(own, names, pairs)]
    ppermute x0 -> x8, waiting for transfers between devices: none -> 5.91 us  [the longest x4 5.86 us: fetch(): return lax.ppermute(own, names, pairs)]
    convert_element_type x5 -> x0, other arithmetic: 3.52 us -> none  [shards(): weighted = (density * cell_area).astype(jnp.bfloat16)]
  transfers between devices with their start and end apart: 5 -> 8, of which waited for: 5 -> 3; matrix products, arithmetic and copies ran while one was open for 0% -> 4% of each run, Pallas kernels for 0% -> 0%
where the time goes in v1:
time: 39.9 us; the launch traced here: 39.5 us
  Pallas kernels  18.9 us (47%)
  starting transfers between devices  8.93 us (22%)
  waiting for transfers between devices  5.91 us (15%)
  local copies, waits for them, and re-layouts  3.45 us (9%)
  other arithmetic  1.52 us (4%)
  between operations  0.75 us (2%)
    pallas_call x1, Pallas kernels, replicated_shards(): pl.pallas_call(lambda *refs: replicated_kernel((blocks, 8, columns), *ref...  18.9 us
    ppermute x4, starting transfers between devices, fetch(): return lax.ppermute(own, names, pairs)  7.97 us
    ppermute x4, waiting for transfers between devices, fetch(): return lax.ppermute(own, names, pairs)  5.86 us
    unnamed x20, local copies, waits for them, and re-layouts  1.91 us
    concatenate x1, local copies, waits for them, and re-layouts, replicated_shards(): jnp.concatenate([points, precond[None, :], jnp.zeros((4, width), jnp.floa...  1.46 us
    another operation x2, other arithmetic, receiver_directions(): jnp.stack([radial * jnp.cos(azimuth), radial * jnp.sin(azimuth), height])  0.86 us
  transfers between devices with their start and end apart: 8, of which 3 were waited for; matrix products, arithmetic and copies ran while one was open for 4% of the time, Pallas kernels for 0%

profile of v1, /device:TPU:0, one launch (start us, length us, event | category | flops | bytes accessed | tf_op | source)
XLA Modules:
  0.0 39.5 jit_solution(11776044647439442968)
XLA Ops:
  0.6 0.0 copy-start.8
  0.6 0.0 copy-start.9
  0.7 0.7 %copy-done.8 = f32[3,128]{1,0:T(4,128)S(1)} copy-done((f32[3,128]{1,0:T(4,128)S(1)}, f32[3,128]{1,0:T(4,128)}, u32[]{:S(2)}) %copy-start.8) | copy-done | bytes 1560
  1.3 0.0 copy-done.9
  1.3 1.5 %concatenate.6 = f32[72,128]{1,0:T(8,128)S(1)} concatenate(f32[3,128]{1,0:T(4,128)S(1)} %copy-done.8, f32[1,128]{1,0:T(1,128)S(1)} %bitcast.11, f32[4,128]{1,0:T(4,128)S(1)} %broadcast_in_dim.10, f32[32,128]{1,0:T(8,128)} %param.6, f32[32,128]{1,0:T(8,128)} %param.7), dimensions={0} | concatenate | bytes 73728 | tf_op jit(solution)/shard_map/concatenate | solution.py:185
  2.8 0.5 %collective-permute-start = (f32[72,128]{1,0:T(8,128)S(1)}, f32[72,128]{1,0:T(8,128)S(1)}, u32[]{:S(2)}, u32[]{:S(2)}) collective-permute-start(f32[72,128]{1,0:T(8,128)S(1)} %concatenate.6), channel_id=1, source_target_pairs={{0,1},{1,0},{2,3},{3,2},{4,5},{5,4},{6,7},{7,6},{8,9},{9,8},{10,11... | collective-permute-start | bytes 110600 | tf_op jit(solution)/shard_map/ppermute | solution.py:189
  3.2 0.8 %multiply_bitcast_fusion.1 = (f32[1,128]{1,0:T(1,128)S(1)}, f32[128]{0:T(128)S(1)}, f32[128]{0:T(128)S(1)}) fusion(s32[2048]{0:T(1024)} %param.9, s32[]{:T(128)S(6)} %select_n.19), kind=kLoop, calls=%fused_computation.16 | loop fusion | flops 5632 | bytes 2052 | tf_op jit(solution)/shard_map/stack | solution.py:258
  4.0 0.0 collective-permute-done
  4.1 0.0 copy-start
  4.1 4.9 %collective-permute-start.5 = (f32[2,72,128]{2,1,0:T(8,128)S(1)}, f32[2,72,128]{2,1,0:T(8,128)S(1)}, u32[]{:S(2)}, u32[]{:S(2)}) collective-permute-start(f32[2,72,128]{2,1,0:T(8,128)S(1)} %pad_maximum_fusion.refs_0_), channel_id=1, source_target_pairs={{0,10},{1,13},{2,8},{3,15},{4,14},{5,9},{6,12},{7,11},{8,2},{9,5},... | collective-permute-start | bytes 221192 | tf_op jit(solution)/shard_map/ppermute | solution.py:193
  9.0 1.5 %collective-permute-start.3 = (f32[2,72,128]{2,1,0:T(8,128)S(1)}, f32[2,72,128]{2,1,0:T(8,128)S(1)}, u32[]{:S(2)}, u32[]{:S(2)}) collective-permute-start(f32[2,72,128]{2,1,0:T(8,128)S(1)} %pad_maximum_fusion.refs_0_), channel_id=1, source_target_pairs={{0,6},{1,9},{2,4},{3,11},{4,2},{5,13},{6,0},{7,15},{8,14},{9,1},{1... | collective-permute-start | bytes 221192 | tf_op jit(solution)/shard_map/ppermute | solution.py:193
  10.6 1.5 %collective-permute-start.1 = (f32[2,72,128]{2,1,0:T(8,128)S(1)}, f32[2,72,128]{2,1,0:T(8,128)S(1)}, u32[]{:S(2)}, u32[]{:S(2)}) collective-permute-start(f32[2,72,128]{2,1,0:T(8,128)S(1)} %pad_maximum_fusion.refs_0_), channel_id=1, source_target_pairs={{0,2},{1,5},{2,0},{3,7},{4,6},{5,1},{6,4},{7,3},{8,10},{9,13},{10,... | collective-permute-start | bytes 221192 | tf_op jit(solution)/shard_map/ppermute | solution.py:193
  12.1 0.1 pad.3.clone
  12.2 0.0 collective-permute-start.7
  12.2 2.3 %collective-permute-done.5.refs_5_ = f32[2,72,128]{2,1,0:T(8,128)S(1)} collective-permute-done((f32[2,72,128]{2,1,0:T(8,128)S(1)}, f32[2,72,128]{2,1,0:T(8,128)S(1)}, u32[]{:S(2)}, u32[]{:S(2)}) %collective-permute-start.5) | collective-permute-done | bytes 73760 | tf_op jit(solution)/shard_map/ppermute | solution.py:193
  14.5 0.0 copy-start.1
  14.5 0.0 collective-permute-start.6
  14.5 1.8 %collective-permute-done.3.refs_3_ = f32[2,72,128]{2,1,0:T(8,128)S(1)} collective-permute-done((f32[2,72,128]{2,1,0:T(8,128)S(1)}, f32[2,72,128]{2,1,0:T(8,128)S(1)}, u32[]{:S(2)}, u32[]{:S(2)}) %collective-permute-start.3) | collective-permute-done | bytes 73760 | tf_op jit(solution)/shard_map/ppermute | solution.py:193
  16.4 0.0 copy-start.2
  16.4 0.0 collective-permute-start.4
  16.4 0.0 collective-permute-done.1.refs_1_
  16.4 0.0 copy-start.3
  16.4 0.5 %collective-permute-start.2 = (f32[2,72,128]{2,1,0:T(8,128)S(1)}, f32[2,72,128]{2,1,0:T(8,128)S(1)}, u32[]{:S(2)}, u32[]{:S(2)}) collective-permute-start(f32[2,72,128]{2,1,0:T(8,128)S(1)} %collective-permute-done.1.refs_1_), channel_id=1, source_target_pairs={{0,1},{1,0},{2,3},{3,2},{4,5},{5,4},{6,7},{7,6},{8,9},{9,8},{10,11... | collective-permute-start | bytes 221192 | tf_op jit(solution)/shard_map/ppermute | solution.py:198
  16.9 0.7 %maximum_maximum_fusion.refs_8_ = f32[8,128]{1,0:T(8,128)} fusion(f32[1,128]{1,0:T(1,128)S(1)} %bitcast.10, f32[1,128]{1,0:T(1,128)S(1)} %multiply_bitcast_fusion, f32[1,128]{1,0:T(1,128)S(1)} %get-tuple-element.2, f32[8]{0:T(128)S(1)} %pad.3.clone), kind=kLoop, calls=%fused_computation.1 | loop fusion | flops 3072 | bytes 5664 | tf_op jit(solution)/shard_map/concatenate | solution.py:204
  17.5 1.7 %collective-permute-done.7.refs_7_ = f32[2,72,128]{2,1,0:T(8,128)S(1)} collective-permute-done((f32[2,72,128]{2,1,0:T(8,128)S(1)}, f32[2,72,128]{2,1,0:T(8,128)S(1)}, u32[]{:S(2)}, u32[]{:S(2)}) %collective-permute-start.7) | collective-permute-done | bytes 73760 | tf_op jit(solution)/shard_map/ppermute | solution.py:193
  19.2 0.0 copy-start.4
  19.3 0.0 collective-permute-done.6.refs_6_
  19.3 0.0 copy-start.5
  19.3 0.0 collective-permute-done.4.refs_4_
  19.3 0.0 copy-start.6
  19.3 0.0 collective-permute-done.2.refs_2_
  19.3 0.0 copy-done
  19.3 0.0 copy-done.1
  19.3 0.0 copy-done.2
  19.3 0.0 copy-done.3
  19.3 0.6 %copy-done.4 = f32[2,72,128]{2,1,0:T(8,128)} copy-done((f32[2,72,128]{2,1,0:T(8,128)}, f32[2,72,128]{2,1,0:T(8,128)S(1)}, u32[]{:S(2)}) %copy-start.4) | copy-done | bytes 73752
  19.9 0.0 copy-done.5
  19.9 0.0 copy-done.6
  19.9 0.0 copy-start.7
  19.9 0.6 %copy-done.7 = f32[2,72,128]{2,1,0:T(8,128)} copy-done((f32[2,72,128]{2,1,0:T(8,128)}, f32[2,72,128]{2,1,0:T(8,128)S(1)}, u32[]{:S(2)}) %copy-start.7) | copy-done | bytes 73752
  20.6 18.9 %iterate.1 = (f32[32,128]{1,0:T(8,128)}, f32[32,128]{1,0:T(8,128)}) custom-call(f32[2,72,128]{2,1,0:T(8,128)} %copy-done, f32[2,72,128]{2,1,0:T(8,128)} %copy-done.3, f32[2,72,128]{2,1,0:T(8,128)} %copy-done.7, f32[2,72,128]{2,1,0:T(8,128)} %copy-done.2, f32[2,72,128]{2,1,0:T(8,128)} %copy-done.6, f32[2,72,128]{2,1,0:T(8,128)} %copy-done.1, ...), custom_call_target="tpu_custom_call" | custom-call | tf_op jit(solution)/shard_map/iterate/pallas_call | solution.py:210
  (4 shorter events, 0.1 us)
Async XLA Ops:
  0.6 0.7 %copy-start.8 = (f32[3,128]{1,0:T(4,128)S(1)}, f32[3,128]{1,0:T(4,128)}, u32[]{:S(2)}) copy-start(f32[3,128]{1,0:T(4,128)} %param.5) | copy-start | bytes 4612
  0.6 0.7 %copy-start.9 = (f32[128]{0:T(128)S(1)}, f32[128]{0:T(128)}, u32[]{:S(2)}) copy-start(f32[128]{0:T(128)} %param.8) | copy-start | bytes 1540
  2.8 1.3 %collective-permute-start = (f32[72,128]{1,0:T(8,128)S(1)}, f32[72,128]{1,0:T(8,128)S(1)}, u32[]{:S(2)}, u32[]{:S(2)}) collective-permute-start(f32[72,128]{1,0:T(8,128)S(1)} %concatenate.6), channel_id=1, source_target_pairs={{0,1},{1,0},{2,3},{3,2},{4,5},{5,4},{6,7},{7,6},{8,9},{9,8},{10,11... | collective-permute-start | bytes 110600 | tf_op jit(solution)/shard_map/ppermute | solution.py:189
  4.1 15.2 %copy-start = (f32[2,72,128]{2,1,0:T(8,128)}, f32[2,72,128]{2,1,0:T(8,128)S(1)}, u32[]{:S(2)}) copy-start(f32[2,72,128]{2,1,0:T(8,128)S(1)} %pad_maximum_fusion.refs_0_) | copy-start | bytes 221188
  4.1 10.4 %collective-permute-start.5 = (f32[2,72,128]{2,1,0:T(8,128)S(1)}, f32[2,72,128]{2,1,0:T(8,128)S(1)}, u32[]{:S(2)}, u32[]{:S(2)}) collective-permute-start(f32[2,72,128]{2,1,0:T(8,128)S(1)} %pad_maximum_fusion.refs_0_), channel_id=1, source_target_pairs={{0,10},{1,13},{2,8},{3,15},{4,14},{5,9},{6,12},{7,11},{8,2},{9,5},... | collective-permute-start | bytes 221192 | tf_op jit(solution)/shard_map/ppermute | solution.py:193
  9.0 7.3 %collective-permute-start.3 = (f32[2,72,128]{2,1,0:T(8,128)S(1)}, f32[2,72,128]{2,1,0:T(8,128)S(1)}, u32[]{:S(2)}, u32[]{:S(2)}) collective-permute-start(f32[2,72,128]{2,1,0:T(8,128)S(1)} %pad_maximum_fusion.refs_0_), channel_id=1, source_target_pairs={{0,6},{1,9},{2,4},{3,11},{4,2},{5,13},{6,0},{7,15},{8,14},{9,1},{1... | collective-permute-start | bytes 221192 | tf_op jit(solution)/shard_map/ppermute | solution.py:193
  10.6 5.8 %collective-permute-start.1 = (f32[2,72,128]{2,1,0:T(8,128)S(1)}, f32[2,72,128]{2,1,0:T(8,128)S(1)}, u32[]{:S(2)}, u32[]{:S(2)}) collective-permute-start(f32[2,72,128]{2,1,0:T(8,128)S(1)} %pad_maximum_fusion.refs_0_), channel_id=1, source_target_pairs={{0,2},{1,5},{2,0},{3,7},{4,6},{5,1},{6,4},{7,3},{8,10},{9,13},{10,... | collective-permute-start | bytes 221192 | tf_op jit(solution)/shard_map/ppermute | solution.py:193
  12.2 7.1 %collective-permute-start.7 = (f32[2,72,128]{2,1,0:T(8,128)S(1)}, f32[2,72,128]{2,1,0:T(8,128)S(1)}, u32[]{:S(2)}, u32[]{:S(2)}) collective-permute-start(f32[2,72,128]{2,1,0:T(8,128)S(1)} %pad_maximum_fusion.refs_0_), channel_id=1, source_target_pairs={{0,14},{1,15},{2,12},{3,13},{4,10},{5,11},{6,8},{7,9},{8,6},{9,7},... | collective-permute-start | bytes 221192 | tf_op jit(solution)/shard_map/ppermute | solution.py:193
  14.5 4.8 %copy-start.1 = (f32[2,72,128]{2,1,0:T(8,128)}, f32[2,72,128]{2,1,0:T(8,128)S(1)}, u32[]{:S(2)}) copy-start(f32[2,72,128]{2,1,0:T(8,128)S(1)} %collective-permute-done.5.refs_5_) | copy-start | bytes 221188
  14.5 4.7 %collective-permute-start.6 = (f32[2,72,128]{2,1,0:T(8,128)S(1)}, f32[2,72,128]{2,1,0:T(8,128)S(1)}, u32[]{:S(2)}, u32[]{:S(2)}) collective-permute-start(f32[2,72,128]{2,1,0:T(8,128)S(1)} %collective-permute-done.5.refs_5_), channel_id=1, source_target_pairs={{0,1},{1,0},{2,3},{3,2},{4,5},{5,4},{6,7},{7,6},{8,9},{9,8},{10,11... | collective-permute-start | bytes 221192 | tf_op jit(solution)/shard_map/ppermute | solution.py:198
  16.4 2.9 %copy-start.2 = (f32[2,72,128]{2,1,0:T(8,128)}, f32[2,72,128]{2,1,0:T(8,128)S(1)}, u32[]{:S(2)}) copy-start(f32[2,72,128]{2,1,0:T(8,128)S(1)} %collective-permute-done.3.refs_3_) | copy-start | bytes 221188
  16.4 2.9 %collective-permute-start.4 = (f32[2,72,128]{2,1,0:T(8,128)S(1)}, f32[2,72,128]{2,1,0:T(8,128)S(1)}, u32[]{:S(2)}, u32[]{:S(2)}) collective-permute-start(f32[2,72,128]{2,1,0:T(8,128)S(1)} %collective-permute-done.3.refs_3_), channel_id=1, source_target_pairs={{0,1},{1,0},{2,3},{3,2},{4,5},{5,4},{6,7},{7,6},{8,9},{9,8},{10,11... | collective-permute-start | bytes 221192 | tf_op jit(solution)/shard_map/ppermute | solution.py:198
  16.4 2.9 %copy-start.3 = (f32[2,72,128]{2,1,0:T(8,128)}, f32[2,72,128]{2,1,0:T(8,128)S(1)}, u32[]{:S(2)}) copy-start(f32[2,72,128]{2,1,0:T(8,128)S(1)} %collective-permute-done.1.refs_1_) | copy-start | bytes 221188
  16.4 2.9 %collective-permute-start.2 = (f32[2,72,128]{2,1,0:T(8,128)S(1)}, f32[2,72,128]{2,1,0:T(8,128)S(1)}, u32[]{:S(2)}, u32[]{:S(2)}) collective-permute-start(f32[2,72,128]{2,1,0:T(8,128)S(1)} %collective-permute-done.1.refs_1_), channel_id=1, source_target_pairs={{0,1},{1,0},{2,3},{3,2},{4,5},{5,4},{6,7},{7,6},{8,9},{9,8},{10,11... | collective-permute-start | bytes 221192 | tf_op jit(solution)/shard_map/ppermute | solution.py:198
  19.2 0.6 %copy-start.4 = (f32[2,72,128]{2,1,0:T(8,128)}, f32[2,72,128]{2,1,0:T(8,128)S(1)}, u32[]{:S(2)}) copy-start(f32[2,72,128]{2,1,0:T(8,128)S(1)} %collective-permute-done.7.refs_7_) | copy-start | bytes 221188
  19.3 0.7 %copy-start.5 = (f32[2,72,128]{2,1,0:T(8,128)}, f32[2,72,128]{2,1,0:T(8,128)S(1)}, u32[]{:S(2)}) copy-start(f32[2,72,128]{2,1,0:T(8,128)S(1)} %collective-permute-done.6.refs_6_) | copy-start | bytes 221188
  19.3 0.7 %copy-start.6 = (f32[2,72,128]{2,1,0:T(8,128)}, f32[2,72,128]{2,1,0:T(8,128)S(1)}, u32[]{:S(2)}) copy-start(f32[2,72,128]{2,1,0:T(8,128)S(1)} %collective-permute-done.4.refs_4_) | copy-start | bytes 221188
  19.9 0.6 %copy-start.7 = (f32[2,72,128]{2,1,0:T(8,128)}, f32[2,72,128]{2,1,0:T(8,128)S(1)}, u32[]{:S(2)}) copy-start(f32[2,72,128]{2,1,0:T(8,128)S(1)} %collective-permute-done.2.refs_2_) | copy-start | bytes 221188

commit v2 on v1

--- a/solution.py
+++ b/solution.py
@@ -18,8 +18,8 @@
 TURNS = WAVENUMBER / (2.0 * math.pi)
 SMOOTH_TURNS = (SMOOTHING * TURNS) ** 2
 BLOCK = 256
-TABLE_LIMIT = 24 * 2**20
-VMEM_LIMIT = 56 * 2**20
+TABLE_LIMIT = 8 * 2**20
+VMEM_LIMIT = 24 * 2**20
 
 
 def sine_coefficients(count):
@@ -63,13 +63,32 @@
     return high, mid, low
 
 
-def replicated_kernel(counts, *refs):
-    blocks, points_row, columns = counts
+def pack_kernel(points, precond, density, incident, out, head, sems):
+    columns = density.shape[0]
+    moves = [
+        (points, head.at[0]),
+        (precond, head.at[1, pl.ds(0, 1)]),
+        (density, out.at[pl.ds(8, columns)]),
+        (incident, out.at[pl.ds(8 + columns, columns)]),
+    ]
+    copies = [pltpu.make_async_copy(src, dst, sems.at[k]) for k, (src, dst) in enumerate(moves)]
+    for copy in copies:
+        copy.start()
+    copies[0].wait()
+    copies[1].wait()
+    out[0:3, :] = head[0]
+    out[3:4, :] = head[1, 0:1]
+    out[4:8, :] = jnp.zeros((4, out.shape[1]), jnp.float32)
+    copies[2].wait()
+    copies[3].wait()
+
+
+def replicated_kernel(blocks, columns, *refs):
     data = refs[:blocks]
     toward_ref = refs[blocks]
     density_out, far_out = refs[blocks + 1 : blocks + 3]
-    lhs, rhs, table, half_table, plane, dens, inc = refs[blocks + 3 : blocks + 10]
-    stage = refs[blocks + 10 :]
+    lhs, rhs, coords, table, half_table, plane, dens, inc = refs[blocks + 3 : blocks + 11]
+    stage = refs[blocks + 11 :]
     total = blocks * BLOCK
     shards_per_block = data[0].shape[0]
     width = data[0].shape[2]
@@ -81,7 +100,8 @@
         )
 
     head = lanes(0, 8)
-    coords = head[0:3] * TURNS
+    scaled = head[0:3] * TURNS
+    coords[0:3, :] = scaled
     inverse = 1.0 / head[3:4]
     dens[...] = lanes(8, columns)
     inc[...] = lanes(8 + columns, columns)
@@ -89,10 +109,10 @@
     ones = jnp.ones((1, total), jnp.float32)
     left, right = [], []
     for k in range(3):
-        h, m, l = split3(coords[k : k + 1])
+        h, m, l = split3(scaled[k : k + 1])
         left += [-2.0 * h, -2.0 * h, -2.0 * m, -2.0 * m, -2.0 * h, -2.0 * l]
         right += [h, m, h, m, l, h]
-    norm = coords[0:1] * coords[0:1] + coords[1:2] * coords[1:2] + coords[2:3] * coords[2:3]
+    norm = scaled[0:1] * scaled[0:1] + scaled[1:2] * scaled[1:2] + scaled[2:3] * scaled[2:3]
     h, m, l = split3(norm)
     left += [h, m, l, ones, ones, ones]
     right += [ones, ones, ones, h, m, l]
@@ -133,46 +153,52 @@
     lax.fori_loop(0, blocks, one_row, 0)
 
     toward = toward_ref[...].T
-    for b in range(blocks):
-        span = slice(b * BLOCK, (b + 1) * BLOCK)
-        phase = toward[:, 0:1] * coords[0:1, span] + toward[:, 1:2] * coords[1:2, span]
-        phase = phase + toward[:, 2:3] * coords[2:3, span]
-        plane[:, span] = cos_turns(phase, 1.0).astype(jnp.bfloat16)
-
     cell_area = FOUR_PI / total
 
     def rounded():
         return (dens[...] * cell_area).astype(jnp.bfloat16)
 
-    def product(w, b, kernel_block, dim):
-        return lax.dot_general(
-            w[:, b * BLOCK : (b + 1) * BLOCK],
-            kernel_block,
-            (((1,), (dim,)), ((), ())),
-            preferred_element_type=jnp.float32,
-        )
+    def part_of(w, b):
+        b = b % blocks
+        return w[:, b * BLOCK : (b + 1) * BLOCK]
+
+    def entry(b, d):
+        b = b % blocks
+        return table[b, d] if d < full else half_table[b]
+
+    def down(w, kernel_block):
+        return lax.dot_general(w, kernel_block, (((1,), (0,)), ((), ())), preferred_element_type=jnp.float32)
+
+    def across(kernel_block, w):
+        return lax.dot_general(kernel_block, w, (((1,), (1,)), ((), ())), preferred_element_type=jnp.float32)
+
+    per_step = -(-blocks // ITERS)
 
     def iterate(step, carry):
         w = rounded()
+        for k in range(per_step):
+            b = jnp.minimum(step * per_step + k, blocks - 1)
+            span = pl.ds(pl.multiple_of(b * BLOCK, BLOCK), BLOCK)
+            phase = toward[:, 0:1] * coords[0:1, span] + toward[:, 1:2] * coords[1:2, span]
+            phase = phase + toward[:, 2:3] * coords[2:3, span]
+            plane[:, span] = cos_turns(phase, 1.0).astype(jnp.bfloat16)
         for b in range(blocks):
-            field = product(w, b, table[b, 0], 1)
-            for d in range(1, full):
-                field += product(w, (b + d) % blocks, table[b, d], 1)
-                field += product(w, (b - d) % blocks, table[(b - d) % blocks, d], 0)
-            if b < full:
-                field += product(w, b + full, half_table[b], 1)
-            else:
-                field += product(w, b - full, half_table[b - full], 0)
+            field = down(part_of(w, b), entry(b, 0))
+            turned = None
+            for d in range(1, full + 1):
+                if d < full or b >= full:
+                    field += down(part_of(w, b - d), entry(b - d, d))
+                if d < full or b < full:
+                    term = across(entry(b, d), part_of(w, b + d))
+                    turned = term if turned is None else turned + term
+            field += turned.T
             span = slice(b * BLOCK, (b + 1) * BLOCK)
             dens[:, span] = dens[:, span] - (field + inc[:, span]) * inverse[:, span]
         return carry
 
     lax.fori_loop(0, ITERS, iterate, 0)
     density_out[...] = dens[:, 0:width]
-    w = rounded()
-    far_out[...] = lax.dot_general(
-        w, plane[...], (((1,), (1,)), ((), ())), preferred_element_type=jnp.float32
-    )
+    far_out[...] = across(plane[...], rounded()).T
 
 
 def replicated_shards(points, density, incident, precond, receivers):
@@ -182,9 +208,16 @@
     chips = count_tgt * count_src
     columns, width = density.shape
     names = ("tgt", "src", "sub")
-    payload = jnp.concatenate(
-        [points, precond[None, :], jnp.zeros((4, width), jnp.float32), density, incident], axis=0
-    )
+    vmem = pl.BlockSpec(memory_space=pltpu.VMEM)
+    payload = pl.pallas_call(
+        pack_kernel,
+        out_shape=jax.ShapeDtypeStruct((8 + 2 * columns, width), jnp.float32),
+        in_specs=[pl.BlockSpec(memory_space=pltpu.HBM)] * 4,
+        out_specs=vmem,
+        scratch_shapes=[pltpu.VMEM((2, 3, width), jnp.float32), pltpu.SemaphoreType.DMA((4,))],
+        compiler_params=pltpu.CompilerParams(vmem_limit_bytes=4 * 2**20),
+        name="pack",
+    )(*(pltpu.with_memory_space_constraint(a, pltpu.HBM) for a in (points, precond[None, :], density, incident)))
     swap = [(0, 1), (1, 0)]
     own = jnp.stack([payload, lax.ppermute(payload, "sub", swap)])
 
@@ -206,9 +239,8 @@
     blocks = len(held)
     total = blocks * BLOCK
     full = blocks // 2
-    vmem = pl.BlockSpec(memory_space=pltpu.VMEM)
     return pl.pallas_call(
-        lambda *refs: replicated_kernel((blocks, 8, columns), *refs),
+        lambda *refs: replicated_kernel(blocks, columns, *refs),
         out_shape=(
             jax.ShapeDtypeStruct((columns, width), jnp.float32),
             jax.ShapeDtypeStruct((columns, rows), jnp.float32),
@@ -218,6 +250,7 @@
         scratch_shapes=[
             pltpu.VMEM((total, 32), jnp.bfloat16),
             pltpu.VMEM((32, total), jnp.bfloat16),
+            pltpu.VMEM((8, total), jnp.float32),
             pltpu.VMEM((blocks, full, BLOCK, BLOCK), jnp.bfloat16),
             pltpu.VMEM((full, BLOCK, BLOCK), jnp.bfloat16),
             pltpu.VMEM((rows, total), jnp.bfloat16),
@@ -333,7 +366,7 @@
     total = points.shape[1] // sizes["groups"]
     return (
         sizes["sub"] == 2
-        and chips >= 2
+        and chips >= 4
         and chips & (chips - 1) == 0
         and total == per_group * (BLOCK // 2)
         and total * total <= TABLE_LIMIT

time: 39.9 us -> 33.4 us (0.84)
  local copies, waits for them, and re-layouts: 3.45 us -> 0.08 us
  Pallas kernels: 18.9 us -> 16 us
  waiting for transfers between devices: 5.91 us -> 6.51 us
  other arithmetic: 1.52 us -> 0.94 us
    pallas_call x1 -> x2, Pallas kernels: 18.9 us -> 16 us  [the longest x1 15.1 us: replicated_shards(): pl.pallas_call(lambda *refs: replicated_kernel(blocks, columns, *refs), o...]
    unnamed x20 -> x0, local copies, waits for them, and re-layouts: 1.91 us -> none
    concatenate x1 -> x0, local copies, waits for them, and re-layouts: 1.46 us -> none  [replicated_shards(): jnp.concatenate([points, precond[None, :], jnp.zeros((4, width), jnp.floa...]
    ppermute x4, waiting for transfers between devices: 5.86 us -> 6.45 us  [fetch(): return lax.ppermute(own, names, pairs)]
    concatenate x1, other arithmetic: 0.66 us -> 0.07 us  [replicated_shards(): jnp.concatenate([toward, jnp.zeros((5, rows), jnp.float32)], axis=0)]
  transfers between devices with their start and end apart: 8 -> 8, of which waited for: 3 -> 3; matrix products, arithmetic and copies ran while one was open for 4% -> 3% of each run, Pallas kernels for 0% -> 0%
where the time goes in v2:
time: 33.4 us; the launch traced here: 33.1 us
  Pallas kernels  16 us (48%)
  starting transfers between devices  8.94 us (27%)
  waiting for transfers between devices  6.51 us (19%)
  other arithmetic  0.94 us (3%)
  between operations  0.67 us (2%)
    pallas_call x1, Pallas kernels, replicated_shards(): pl.pallas_call(lambda *refs: replicated_kernel(blocks, columns, *refs), o...  15.1 us
    ppermute x4, starting transfers between devices, fetch(): return lax.ppermute(own, names, pairs)  7.91 us
    ppermute x4, waiting for transfers between devices, fetch(): return lax.ppermute(own, names, pairs)  6.45 us
    another operation x2, other arithmetic, receiver_directions(): jnp.stack([radial * jnp.cos(azimuth), radial * jnp.sin(azimuth), height])  0.86 us
    pallas_call x1, Pallas kernels, replicated_shards(): pl.pallas_call(pack_kernel, out_shape=jax.ShapeDtypeStruct((8 + 2 * colum...  0.8 us
  transfers between devices with their start and end apart: 8, of which 3 were waited for; matrix products, arithmetic and copies ran while one was open for 3% of the time, Pallas kernels for 0%

profile of v2, /device:TPU:0, one launch (start us, length us, event | category | flops | bytes accessed | tf_op | source)
XLA Modules:
  0.0 33.1 jit_solution(16004122811013177539)
XLA Ops:
  0.6 0.8 %pack.1 = f32[72,128]{1,0:T(8,128)S(1)} custom-call(f32[3,128]{1,0:T(4,128)} %points.1, f32[1,128]{1,0:T(1,128)} %bitcast.11, f32[32,128]{1,0:T(8,128)} %density.1, f32[32,128]{1,0:T(8,128)} %incident.1), custom_call_target="tpu_custom_call" | custom-call | tf_op jit(solution)/shard_map/pack/pallas_call | solution.py:212
  1.4 0.5 %collective-permute-start = (f32[72,128]{1,0:T(8,128)S(1)}, f32[72,128]{1,0:T(8,128)S(1)}, u32[]{:S(2)}, u32[]{:S(2)}) collective-permute-start(f32[72,128]{1,0:T(8,128)S(1)} %pack.1), channel_id=1, source_target_pairs={{0,1},{1,0},{2,3},{3,2},{4,5},{5,4},{6,7},{7,6},{8,9},{9,8},{10,11... | collective-permute-start | bytes 110600 | tf_op jit(solution)/shard_map/ppermute | solution.py:222
  2.0 0.8 %multiply_bitcast_fusion.1 = (f32[1,128]{1,0:T(1,128)S(1)}, f32[128]{0:T(128)S(1)}, f32[128]{0:T(128)S(1)}) fusion(s32[2048]{0:T(1024)} %param.9, s32[]{:T(128)S(6)} %select_n.19), kind=kLoop, calls=%fused_computation.16 | loop fusion | flops 5632 | bytes 2052 | tf_op jit(solution)/shard_map/stack | solution.py:291
  2.8 0.0 collective-permute-done
  2.8 4.9 %collective-permute-start.5 = (f32[2,72,128]{2,1,0:T(8,128)S(1)}, f32[2,72,128]{2,1,0:T(8,128)S(1)}, u32[]{:S(2)}, u32[]{:S(2)}) collective-permute-start(f32[2,72,128]{2,1,0:T(8,128)S(1)} %pad_maximum_fusion.refs_0_), channel_id=1, source_target_pairs={{0,10},{1,13},{2,8},{3,15},{4,14},{5,9},{6,12},{7,11},{8,2},{9,5},... | collective-permute-start | bytes 221192 | tf_op jit(solution)/shard_map/ppermute | solution.py:226
  7.7 1.5 %collective-permute-start.3 = (f32[2,72,128]{2,1,0:T(8,128)S(1)}, f32[2,72,128]{2,1,0:T(8,128)S(1)}, u32[]{:S(2)}, u32[]{:S(2)}) collective-permute-start(f32[2,72,128]{2,1,0:T(8,128)S(1)} %pad_maximum_fusion.refs_0_), channel_id=1, source_target_pairs={{0,6},{1,9},{2,4},{3,11},{4,2},{5,13},{6,0},{7,15},{8,14},{9,1},{1... | collective-permute-start | bytes 221192 | tf_op jit(solution)/shard_map/ppermute | solution.py:226
  9.2 1.5 %collective-permute-start.1 = (f32[2,72,128]{2,1,0:T(8,128)S(1)}, f32[2,72,128]{2,1,0:T(8,128)S(1)}, u32[]{:S(2)}, u32[]{:S(2)}) collective-permute-start(f32[2,72,128]{2,1,0:T(8,128)S(1)} %pad_maximum_fusion.refs_0_), channel_id=1, source_target_pairs={{0,2},{1,5},{2,0},{3,7},{4,6},{5,1},{6,4},{7,3},{8,10},{9,13},{10,... | collective-permute-start | bytes 221192 | tf_op jit(solution)/shard_map/ppermute | solution.py:226
  10.8 0.1 pad.3.clone
  10.9 0.0 collective-permute-start.7
  10.9 2.4 %collective-permute-done.5.refs_5_ = f32[2,72,128]{2,1,0:T(8,128)S(1)} collective-permute-done((f32[2,72,128]{2,1,0:T(8,128)S(1)}, f32[2,72,128]{2,1,0:T(8,128)S(1)}, u32[]{:S(2)}, u32[]{:S(2)}) %collective-permute-start.5) | collective-permute-done | bytes 73760 | tf_op jit(solution)/shard_map/ppermute | solution.py:226
  13.3 0.0 collective-permute-start.6
  13.3 1.0 %collective-permute-done.3.refs_3_ = f32[2,72,128]{2,1,0:T(8,128)S(1)} collective-permute-done((f32[2,72,128]{2,1,0:T(8,128)S(1)}, f32[2,72,128]{2,1,0:T(8,128)S(1)}, u32[]{:S(2)}, u32[]{:S(2)}) %collective-permute-start.3) | collective-permute-done | bytes 73760 | tf_op jit(solution)/shard_map/ppermute | solution.py:226
  14.3 0.0 collective-permute-start.4
  14.3 0.0 collective-permute-done.1.refs_1_
  14.3 0.5 %collective-permute-start.2 = (f32[2,72,128]{2,1,0:T(8,128)S(1)}, f32[2,72,128]{2,1,0:T(8,128)S(1)}, u32[]{:S(2)}, u32[]{:S(2)}) collective-permute-start(f32[2,72,128]{2,1,0:T(8,128)S(1)} %collective-permute-done.1.refs_1_), channel_id=1, source_target_pairs={{0,1},{1,0},{2,3},{3,2},{4,5},{5,4},{6,7},{7,6},{8,9},{9,8},{10,11... | collective-permute-start | bytes 221192 | tf_op jit(solution)/shard_map/ppermute | solution.py:231
  14.8 0.1 maximum_maximum_fusion.refs_8_
  14.9 3.0 %collective-permute-done.7.refs_7_ = f32[2,72,128]{2,1,0:T(8,128)S(1)} collective-permute-done((f32[2,72,128]{2,1,0:T(8,128)S(1)}, f32[2,72,128]{2,1,0:T(8,128)S(1)}, u32[]{:S(2)}, u32[]{:S(2)}) %collective-permute-start.7) | collective-permute-done | bytes 73760 | tf_op jit(solution)/shard_map/ppermute | solution.py:226
  17.9 0.0 collective-permute-done.6.refs_6_
  17.9 0.0 collective-permute-done.4.refs_4_
  17.9 0.0 collective-permute-done.2.refs_2_
  17.9 15.1 %iterate.1 = (f32[32,128]{1,0:T(8,128)}, f32[32,128]{1,0:T(8,128)}) custom-call(f32[2,72,128]{2,1,0:T(8,128)S(1)} %pad_maximum_fusion.refs_0_, f32[2,72,128]{2,1,0:T(8,128)S(1)} %collective-permute-done.1.refs_1_, f32[2,72,128]{2,1,0:T(8,128)S(1)} %collective-permute-done.2.refs_2_, f32[2,72,128]{2,1,0:T(8,128)S(1)} %collective-permute-done.3.refs_3_, ...), custom_call_target="tpu_custom_call" | custom-call | tf_op jit(solution)/shard_map/iterate/pallas_call | solution.py:242
  (3 shorter events, 0.1 us)
Async XLA Ops:
  1.4 1.4 %collective-permute-start = (f32[72,128]{1,0:T(8,128)S(1)}, f32[72,128]{1,0:T(8,128)S(1)}, u32[]{:S(2)}, u32[]{:S(2)}) collective-permute-start(f32[72,128]{1,0:T(8,128)S(1)} %pack.1), channel_id=1, source_target_pairs={{0,1},{1,0},{2,3},{3,2},{4,5},{5,4},{6,7},{7,6},{8,9},{9,8},{10,11... | collective-permute-start | bytes 110600 | tf_op jit(solution)/shard_map/ppermute | solution.py:222
  2.8 10.5 %collective-permute-start.5 = (f32[2,72,128]{2,1,0:T(8,128)S(1)}, f32[2,72,128]{2,1,0:T(8,128)S(1)}, u32[]{:S(2)}, u32[]{:S(2)}) collective-permute-start(f32[2,72,128]{2,1,0:T(8,128)S(1)} %pad_maximum_fusion.refs_0_), channel_id=1, source_target_pairs={{0,10},{1,13},{2,8},{3,15},{4,14},{5,9},{6,12},{7,11},{8,2},{9,5},... | collective-permute-start | bytes 221192 | tf_op jit(solution)/shard_map/ppermute | solution.py:226
  7.7 6.6 %collective-permute-start.3 = (f32[2,72,128]{2,1,0:T(8,128)S(1)}, f32[2,72,128]{2,1,0:T(8,128)S(1)}, u32[]{:S(2)}, u32[]{:S(2)}) collective-permute-start(f32[2,72,128]{2,1,0:T(8,128)S(1)} %pad_maximum_fusion.refs_0_), channel_id=1, source_target_pairs={{0,6},{1,9},{2,4},{3,11},{4,2},{5,13},{6,0},{7,15},{8,14},{9,1},{1... | collective-permute-start | bytes 221192 | tf_op jit(solution)/shard_map/ppermute | solution.py:226
  9.2 5.0 %collective-permute-start.1 = (f32[2,72,128]{2,1,0:T(8,128)S(1)}, f32[2,72,128]{2,1,0:T(8,128)S(1)}, u32[]{:S(2)}, u32[]{:S(2)}) collective-permute-start(f32[2,72,128]{2,1,0:T(8,128)S(1)} %pad_maximum_fusion.refs_0_), channel_id=1, source_target_pairs={{0,2},{1,5},{2,0},{3,7},{4,6},{5,1},{6,4},{7,3},{8,10},{9,13},{10,... | collective-permute-start | bytes 221192 | tf_op jit(solution)/shard_map/ppermute | solution.py:226
  10.9 7.1 %collective-permute-start.7 = (f32[2,72,128]{2,1,0:T(8,128)S(1)}, f32[2,72,128]{2,1,0:T(8,128)S(1)}, u32[]{:S(2)}, u32[]{:S(2)}) collective-permute-start(f32[2,72,128]{2,1,0:T(8,128)S(1)} %pad_maximum_fusion.refs_0_), channel_id=1, source_target_pairs={{0,14},{1,15},{2,12},{3,13},{4,10},{5,11},{6,8},{7,9},{8,6},{9,7},... | collective-permute-start | bytes 221192 | tf_op jit(solution)/shard_map/ppermute | solution.py:226
  13.3 4.6 %collective-permute-start.6 = (f32[2,72,128]{2,1,0:T(8,128)S(1)}, f32[2,72,128]{2,1,0:T(8,128)S(1)}, u32[]{:S(2)}, u32[]{:S(2)}) collective-permute-start(f32[2,72,128]{2,1,0:T(8,128)S(1)} %collective-permute-done.5.refs_5_), channel_id=1, source_target_pairs={{0,1},{1,0},{2,3},{3,2},{4,5},{5,4},{6,7},{7,6},{8,9},{9,8},{10,11... | collective-permute-start | bytes 221192 | tf_op jit(solution)/shard_map/ppermute | solution.py:231
  14.3 3.6 %collective-permute-start.4 = (f32[2,72,128]{2,1,0:T(8,128)S(1)}, f32[2,72,128]{2,1,0:T(8,128)S(1)}, u32[]{:S(2)}, u32[]{:S(2)}) collective-permute-start(f32[2,72,128]{2,1,0:T(8,128)S(1)} %collective-permute-done.3.refs_3_), channel_id=1, source_target_pairs={{0,1},{1,0},{2,3},{3,2},{4,5},{5,4},{6,7},{7,6},{8,9},{9,8},{10,11... | collective-permute-start | bytes 221192 | tf_op jit(solution)/shard_map/ppermute | solution.py:231
  14.3 3.6 %collective-permute-start.2 = (f32[2,72,128]{2,1,0:T(8,128)S(1)}, f32[2,72,128]{2,1,0:T(8,128)S(1)}, u32[]{:S(2)}, u32[]{:S(2)}) collective-permute-start(f32[2,72,128]{2,1,0:T(8,128)S(1)} %collective-permute-done.1.refs_1_), channel_id=1, source_target_pairs={{0,1},{1,0},{2,3},{3,2},{4,5},{5,4},{6,7},{7,6},{8,9},{9,8},{10,11... | collective-permute-start | bytes 221192 | tf_op jit(solution)/shard_map/ppermute | solution.py:231

commit v3 on v2

--- a/solution.py
+++ b/solution.py
@@ -1,3 +1,4 @@
+import functools
 import math
 
 import jax
@@ -83,30 +84,14 @@
     copies[3].wait()
 
 
-def replicated_kernel(blocks, columns, *refs):
-    data = refs[:blocks]
-    toward_ref = refs[blocks]
-    density_out, far_out = refs[blocks + 1 : blocks + 3]
-    lhs, rhs, coords, table, half_table, plane, dens, inc = refs[blocks + 3 : blocks + 11]
-    stage = refs[blocks + 11 :]
-    total = blocks * BLOCK
-    shards_per_block = data[0].shape[0]
-    width = data[0].shape[2]
-    full = blocks // 2
-
-    def lanes(start, count):
-        return jnp.concatenate(
-            [data[b][s, start : start + count, :] for b in range(blocks) for s in range(shards_per_block)], axis=1
-        )
-
-    head = lanes(0, 8)
-    scaled = head[0:3] * TURNS
-    coords[0:3, :] = scaled
-    inverse = 1.0 / head[3:4]
-    dens[...] = lanes(8, columns)
-    inc[...] = lanes(8 + columns, columns)
-
-    ones = jnp.ones((1, total), jnp.float32)
+def lanes(data, start, count):
+    return jnp.concatenate(
+        [piece[s, start : start + count, :] for piece in data for s in range(piece.shape[0])], axis=1
+    )
+
+
+def distance_operands(scaled):
+    ones = jnp.ones((1, scaled.shape[1]), jnp.float32)
     left, right = [], []
     for k in range(3):
         h, m, l = split3(scaled[k : k + 1])
@@ -116,41 +101,135 @@
     h, m, l = split3(norm)
     left += [h, m, l, ones, ones, ones]
     right += [ones, ones, ones, h, m, l]
-    zeros = jnp.zeros((8, total), jnp.float32)
+    zeros = jnp.zeros((8, scaled.shape[1]), jnp.float32)
     left = jnp.concatenate(left + [zeros], axis=0)
-    rhs[...] = jnp.concatenate(right + [zeros], axis=0).astype(jnp.bfloat16)
-    lhs[...] = left.T.astype(jnp.bfloat16)
-
-    def distances(row, count, column):
+    right = jnp.concatenate(right + [zeros], axis=0).astype(jnp.bfloat16)
+    return left.T.astype(jnp.bfloat16), right
+
+
+def down(w, kernel_block):
+    return lax.dot_general(w, kernel_block, (((1,), (0,)), ((), ())), preferred_element_type=jnp.float32)
+
+
+def across(kernel_block, w):
+    return lax.dot_general(kernel_block, w, (((1,), (1,)), ((), ())), preferred_element_type=jnp.float32)
+
+
+def block_span(index):
+    return pl.ds(pl.multiple_of(index * BLOCK, BLOCK), BLOCK)
+
+
+def strip_size(old, new):
+    return sum(j + 1 for j in range(old, old + new))
+
+
+def build_strips(old, new, lhs, rhs, weighted, table, field, turned, even, odd):
+    count = strip_size(old, new)
+    starts = [strip_size(old, k) for k in range(new)]
+
+    def place(k):
+        j, i = 0, k
+        for step in range(1, new):
+            past = k >= starts[step]
+            j = jnp.where(past, step, j)
+            i = jnp.where(past, k - starts[step], i)
+        return j, i
+
+    def distances(k):
+        j, i = place(k)
         return lax.dot_general(
-            lhs[pl.ds(pl.multiple_of(row, 128), count), :],
-            rhs[:, pl.ds(pl.multiple_of(column, BLOCK), BLOCK)],
-            (((1,), (0,)), ((), ())),
-            preferred_element_type=jnp.float32,
+            lhs[block_span(j), :], rhs[:, block_span(i)], (((1,), (0,)), ((), ())), preferred_element_type=jnp.float32
         )
 
-    def fill(block, d, source):
+    def fill(k, source):
         for r in range(0, BLOCK, 32):
-            table[block, d, r : r + 32, :] = green(source[r : r + 32, :])
-
-    stage[0][...] = distances(0, BLOCK, 0)
-
-    def one_row(block, carry):
-        for d in range(1, full):
-            stage[d][...] = distances(block * BLOCK, BLOCK, lax.rem(block + d, blocks) * BLOCK)
-            fill(block, d - 1, stage[d - 1])
-        low = lax.rem(block, full)
-        part = block // full
-        stage[full][...] = distances(low * BLOCK + part * 128, 128, (low + full) * BLOCK)
-        fill(block, full - 1, stage[full - 1])
-        following = lax.rem(block + 1, blocks) * BLOCK
-        stage[0][...] = distances(following, BLOCK, following)
-        base = pl.multiple_of(part * 128, 128)
-        for r in range(0, 128, 32):
-            half_table[low, pl.ds(base + r, 32), :] = green(stage[full][r : r + 32, :])
+            table[k, r : r + 32, :] = green(source[r : r + 32, :])
+
+    def products(k, valid):
+        j, i = place(k)
+        valid = jnp.where(valid, 1.0, 0.0)
+        beside = jnp.where(old + j == i, 0.0, valid).astype(jnp.bfloat16)
+        row = block_span(j)
+        turned[row, :] += across(table[k], weighted[:, block_span(i)] * valid.astype(jnp.bfloat16))
+        field[:, block_span(i)] += down(weighted[:, block_span(old + j)] * beside, table[k])
+
+    field[...] = jnp.zeros_like(field)
+    turned[...] = jnp.zeros_like(turned)
+    table[0] = jnp.zeros((BLOCK, BLOCK), jnp.bfloat16)
+    even[...] = distances(0)
+
+    def pair(t, carry):
+        k = 2 * t
+        odd[...] = distances(k + 1)
+        products(jnp.maximum(k - 1, 0), k > 0)
+        fill(k, even)
+        even[...] = distances(jnp.minimum(k + 2, count - 1))
+        products(k, True)
+        fill(k + 1, odd)
         return carry
 
-    lax.fori_loop(0, blocks, one_row, 0)
+    lax.fori_loop(0, count // 2, pair, 0)
+    if count >= 2:
+        products(2 * (count // 2) - 1, True)
+    if count % 2:
+        fill(count - 1, even)
+        products(count - 1, True)
+    field[:, old * BLOCK :] += turned[...].T
+
+
+def prepare(old, data, columns, total, lhs, rhs, weighted, before):
+    scaled = lanes(data, 0, 3) * TURNS
+    left, right = distance_operands(scaled)
+    lhs[...] = left
+    rhs[:, old * BLOCK :] = right
+    weighted[:, old * BLOCK :] = (lanes(data, 8, columns) * (FOUR_PI / total)).astype(jnp.bfloat16)
+    if old:
+        rhs[:, : old * BLOCK] = before[0][...]
+        weighted[:, : old * BLOCK] = before[1][...]
+    return scaled
+
+
+def strips_kernel(pieces, old, new, columns, total, *refs):
+    data, refs = refs[:pieces], refs[pieces:]
+    before = refs[: 2 if old else 0]
+    table, field, rhs, weighted, lhs, turned, even, odd = refs[len(before) :]
+    prepare(old, data, columns, total, lhs, rhs, weighted, before)
+    build_strips(old, new, lhs, rhs, weighted, table, field, turned, even, odd)
+
+
+def iterate_kernel(pieces, blocks, columns, groups, *refs):
+    data, refs = refs[:pieces], refs[pieces:]
+    last, toward_ref, before, refs = refs[0], refs[1], refs[2:4], refs[4:]
+    tables, refs = refs[: len(groups)], refs[len(groups) :]
+    fields, refs = refs[: len(groups)], refs[len(groups) :]
+    density_out, far_out = refs[:2]
+    lhs, rhs, weighted, table, field, turned, even, odd, coords, plane, dens, inc = refs[2:]
+    total = blocks * BLOCK
+    width = data[0].shape[2]
+    old = blocks - 1
+    prepare(old, [last], columns, total, lhs, rhs, weighted, before)
+    build_strips(old, 1, lhs, rhs, weighted, table, field, turned, even, odd)
+
+    everything = list(data) + [last]
+    coords[0:3, :] = lanes(everything, 0, 3) * TURNS
+    inverse = 1.0 / lanes(everything, 3, 1)
+    dens[...] = lanes(everything, 8, columns)
+    inc[...] = lanes(everything, 8 + columns, columns)
+    for part in fields:
+        field[:, : part.shape[1]] += part[...]
+    dens[...] = dens[...] - (field[...] + inc[...]) * inverse
+
+    entries = {}
+    for (first, count), part in zip(list(groups) + [(old, 1)], list(tables) + [table]):
+        k = 0
+        for j in range(first, first + count):
+            for i in range(j + 1):
+                entries[j, i] = (part, k)
+                k += 1
+
+    def entry(j, i):
+        part, k = entries[j, i]
+        return part[k]
 
     toward = toward_ref[...].T
     cell_area = FOUR_PI / total
@@ -159,44 +238,34 @@
         return (dens[...] * cell_area).astype(jnp.bfloat16)
 
     def part_of(w, b):
-        b = b % blocks
         return w[:, b * BLOCK : (b + 1) * BLOCK]
 
-    def entry(b, d):
-        b = b % blocks
-        return table[b, d] if d < full else half_table[b]
-
-    def down(w, kernel_block):
-        return lax.dot_general(w, kernel_block, (((1,), (0,)), ((), ())), preferred_element_type=jnp.float32)
-
-    def across(kernel_block, w):
-        return lax.dot_general(kernel_block, w, (((1,), (1,)), ((), ())), preferred_element_type=jnp.float32)
-
-    per_step = -(-blocks // ITERS)
+    steps = ITERS - 1
+    per_step = -(-blocks // steps)
 
     def iterate(step, carry):
         w = rounded()
         for k in range(per_step):
-            b = jnp.minimum(step * per_step + k, blocks - 1)
-            span = pl.ds(pl.multiple_of(b * BLOCK, BLOCK), BLOCK)
+            span = block_span(jnp.minimum(step * per_step + k, blocks - 1))
             phase = toward[:, 0:1] * coords[0:1, span] + toward[:, 1:2] * coords[1:2, span]
             phase = phase + toward[:, 2:3] * coords[2:3, span]
             plane[:, span] = cos_turns(phase, 1.0).astype(jnp.bfloat16)
         for b in range(blocks):
-            field = down(part_of(w, b), entry(b, 0))
-            turned = None
-            for d in range(1, full + 1):
-                if d < full or b >= full:
-                    field += down(part_of(w, b - d), entry(b - d, d))
-                if d < full or b < full:
-                    term = across(entry(b, d), part_of(w, b + d))
-                    turned = term if turned is None else turned + term
-            field += turned.T
+            total_field = None
+            for j in range(b, blocks):
+                term = down(part_of(w, j), entry(j, b))
+                total_field = term if total_field is None else total_field + term
+            side = None
+            for i in range(b):
+                term = across(entry(b, i), part_of(w, i))
+                side = term if side is None else side + term
+            if side is not None:
+                total_field += side.T
             span = slice(b * BLOCK, (b + 1) * BLOCK)
-            dens[:, span] = dens[:, span] - (field + inc[:, span]) * inverse[:, span]
+            dens[:, span] = dens[:, span] - (total_field + inc[:, span]) * inverse[:, span]
         return carry
 
-    lax.fori_loop(0, ITERS, iterate, 0)
+    lax.fori_loop(0, steps, iterate, 0)
     density_out[...] = dens[:, 0:width]
     far_out[...] = across(plane[...], rounded()).T
 
@@ -219,49 +288,91 @@
         name="pack",
     )(*(pltpu.with_memory_space_constraint(a, pltpu.HBM) for a in (points, precond[None, :], density, incident)))
     swap = [(0, 1), (1, 0)]
-    own = jnp.stack([payload, lax.ppermute(payload, "sub", swap)])
-
-    def fetch(offsets):
+    payload = payload[None]
+
+    def fetch(array, offsets):
         pairs = [(q * 2 + c, (q ^ offsets[c]) * 2 + c) for q in range(chips) for c in range(2)]
-        return lax.ppermute(own, names, pairs)
-
-    held = [own]
-    for k in range(1, chips - 1, 2):
-        near = fetch((k, k + 1))
-        held += [near, lax.ppermute(near, "sub", swap)]
-    held.append(fetch((chips - 1, chips - 1)))
+        return lax.ppermute(array, names, pairs)
+
+    own = jnp.concatenate([payload, lax.ppermute(payload, "sub", swap)], axis=0)
+    near = [fetch(own, (k, k + 1)) for k in range(1, chips - 1, 2)]
+    last = fetch(own, (chips - 1, chips - 1))
 
     place = (lax.axis_index("tgt") * count_src + lax.axis_index("src")) * count_sub + lax.axis_index("sub")
     rows = receivers.shape[0] // (chips * count_sub)
     toward = receiver_directions(lax.dynamic_slice_in_dim(receivers, place * rows, rows, 0))
     toward = jnp.concatenate([toward, jnp.zeros((5, rows), jnp.float32)], axis=0)
 
-    blocks = len(held)
+    blocks = chips
     total = blocks * BLOCK
-    full = blocks // 2
+    f32, bf16 = jnp.float32, jnp.bfloat16
+
+    def strip_shapes(old, new):
+        return [
+            ((strip_size(old, new), BLOCK, BLOCK), bf16),
+            ((columns, (old + new) * BLOCK), f32),
+            ((32, (old + new) * BLOCK), bf16),
+            ((columns, (old + new) * BLOCK), bf16),
+            ((new * BLOCK, 32), bf16),
+            ((new * BLOCK, columns), f32),
+            ((BLOCK, BLOCK), f32),
+            ((BLOCK, BLOCK), f32),
+        ]
+
+    groups, tables, fields, held, before = [], [], [], [], []
+
+    def strips(data):
+        old, new = len(held), len(data)
+        shapes = strip_shapes(old, new)
+        work = strip_size(old, new) * BLOCK * BLOCK
+        table, field, *state = pl.pallas_call(
+            functools.partial(strips_kernel, new, old, new, columns, total),
+            out_shape=[jax.ShapeDtypeStruct(*shape) for shape in shapes[:4]],
+            in_specs=[vmem] * (new + len(before)),
+            out_specs=[vmem] * 4,
+            scratch_shapes=[pltpu.VMEM(*shape) for shape in shapes[4:]],
+            compiler_params=pltpu.CompilerParams(vmem_limit_bytes=VMEM_LIMIT),
+            cost_estimate=pl.CostEstimate(flops=30 * work, bytes_accessed=2 * work, transcendentals=2 * work),
+            name=f"strips{old}",
+        )(*data, *before)
+        groups.append((old, new))
+        tables.append(table)
+        fields.append(field)
+        held.extend(data)
+        before[:] = state
+
+    early, late = near[:2], near[2:]
+    swapped = [lax.ppermute(array, "sub", swap) for array in early]
+    strips([own, early[0], swapped[0]])
+    for array, other in zip(early[1:], swapped[1:]):
+        strips([array, other])
+    for array in late:
+        array, fields[-1] = lax.optimization_barrier((array, fields[-1]))
+        other = lax.ppermute(array, "sub", swap)
+        strips([array])
+        strips([other])
+
+    old = len(held)
+    pieces = len(held)
+    shapes = strip_shapes(old, 1)
     return pl.pallas_call(
-        lambda *refs: replicated_kernel(blocks, columns, *refs),
+        functools.partial(iterate_kernel, pieces, blocks, columns, tuple(groups)),
         out_shape=(
-            jax.ShapeDtypeStruct((columns, width), jnp.float32),
-            jax.ShapeDtypeStruct((columns, rows), jnp.float32),
+            jax.ShapeDtypeStruct((columns, width), f32),
+            jax.ShapeDtypeStruct((columns, rows), f32),
         ),
-        in_specs=[vmem] * (blocks + 1),
+        in_specs=[vmem] * (pieces + 4 + 2 * len(groups)),
         out_specs=(vmem, vmem),
-        scratch_shapes=[
-            pltpu.VMEM((total, 32), jnp.bfloat16),
-            pltpu.VMEM((32, total), jnp.bfloat16),
-            pltpu.VMEM((8, total), jnp.float32),
-            pltpu.VMEM((blocks, full, BLOCK, BLOCK), jnp.bfloat16),
-            pltpu.VMEM((full, BLOCK, BLOCK), jnp.bfloat16),
-            pltpu.VMEM((rows, total), jnp.bfloat16),
-            pltpu.VMEM((columns, total), jnp.float32),
-            pltpu.VMEM((columns, total), jnp.float32),
-        ]
-        + [pltpu.VMEM((BLOCK, BLOCK), jnp.float32) for _ in range(full)]
-        + [pltpu.VMEM((128, BLOCK), jnp.float32)],
+        scratch_shapes=[pltpu.VMEM(*shapes[k]) for k in (4, 2, 3, 0, 1, 5, 6, 7)]
+        + [
+            pltpu.VMEM((8, total), f32),
+            pltpu.VMEM((rows, total), bf16),
+            pltpu.VMEM((columns, total), f32),
+            pltpu.VMEM((columns, total), f32),
+        ],
         compiler_params=pltpu.CompilerParams(vmem_limit_bytes=VMEM_LIMIT),
         name="iterate",
-    )(*held, toward)
+    )(*held, last, toward, *before, *tables, *fields)
 
 
 def single_layer(targets, sources):

time: 33.4 us -> 31.8 us (0.952)
  waiting for transfers between devices: 6.51 us -> 0.88 us
  starting transfers between devices: 8.94 us -> 11.6 us
  Pallas kernels: 16 us -> 17.3 us
    ppermute x8, waiting for transfers between devices: 6.51 us -> 0.88 us  [the longest x1 0.87 us: replicated_shards(): own = jnp.concatenate([payload, lax.ppermute(payload, 'sub', swap)], axis=0)]
    ppermute x8, starting transfers between devices: 8.94 us -> 11.6 us  [the longest x4 10.3 us: fetch(): return lax.ppermute(array, names, pairs)]
    pallas_call x1 -> x5, Pallas kernels: 15.1 us -> 16.5 us  [the longest x1 8.94 us: replicated_shards(): pl.pallas_call(functools.partial(iterate_kernel, pieces, blocks, columns,...]
  transfers between devices with their start and end apart: 8 -> 8, of which waited for: 3 -> 1; matrix products, arithmetic and copies ran while one was open for 3% -> 3% of each run, Pallas kernels for 0% -> 24%
where the time goes in v3:
time: 31.8 us; the launch traced here: 31.5 us
  Pallas kernels  17.3 us (54%)
  starting transfers between devices  11.6 us (36%)
  other arithmetic  0.94 us (3%)
  waiting for transfers between devices  0.88 us (3%)
  between operations  0.67 us (2%)
    ppermute x4, starting transfers between devices, fetch(): return lax.ppermute(array, names, pairs)  10.3 us
    pallas_call x1, Pallas kernels, replicated_shards(): pl.pallas_call(functools.partial(iterate_kernel, pieces, blocks, columns,...  8.94 us
    pallas_call x4, Pallas kernels, strips(): pl.pallas_call(functools.partial(strips_kernel, new, old, new, columns, t...  7.55 us
    ppermute x1, waiting for transfers between devices, replicated_shards(): own = jnp.concatenate([payload, lax.ppermute(payload, 'sub', swap)], axis=0)  0.87 us
    another operation x2, other arithmetic, receiver_directions(): jnp.stack([radial * jnp.cos(azimuth), radial * jnp.sin(azimuth), height])  0.86 us
    pallas_call x1, Pallas kernels, replicated_shards(): pl.pallas_call(pack_kernel, out_shape=jax.ShapeDtypeStruct((8 + 2 * colum...  0.8 us
  transfers between devices with their start and end apart: 8, of which 1 were waited for; matrix products, arithmetic and copies ran while one was open for 3% of the time, Pallas kernels for 24%

profile of v3, /device:TPU:0, one launch (start us, length us, event | category | flops | bytes accessed | tf_op | source)
XLA Modules:
  0.0 31.5 jit_solution(5335442040275740908)
XLA Ops:
  0.6 0.8 %pack.1 = f32[72,128]{1,0:T(8,128)S(1)} custom-call(f32[3,128]{1,0:T(4,128)} %points.1, f32[1,128]{1,0:T(1,128)} %bitcast.10, f32[32,128]{1,0:T(8,128)} %density.1, f32[32,128]{1,0:T(8,128)} %incident.1), custom_call_target="tpu_custom_call" | custom-call | tf_op jit(solution)/shard_map/pack/pallas_call | solution.py:281
  1.4 0.5 %collective-permute-start = (f32[1,72,128]{2,1,0:T(8,128)S(1)}, f32[1,72,128]{2,1,0:T(8,128)S(1)}, u32[]{:S(2)}, u32[]{:S(2)}) collective-permute-start(f32[1,72,128]{2,1,0:T(8,128)S(1)} %bitcast.7), channel_id=1, source_target_pairs={{0,1},{1,0},{2,3},{3,2},{4,5},{5,4},{6,7},{7,6},{8,9},{9,8},{10,11... | collective-permute-start | bytes 110600 | tf_op jit(solution)/shard_map/ppermute | solution.py:297
  2.0 0.9 %collective-permute-done = f32[1,72,128]{2,1,0:T(8,128)S(1)} collective-permute-done((f32[1,72,128]{2,1,0:T(8,128)S(1)}, f32[1,72,128]{2,1,0:T(8,128)S(1)}, u32[]{:S(2)}, u32[]{:S(2)}) %collective-permute-start) | collective-permute-done | bytes 36896 | tf_op jit(solution)/shard_map/ppermute | solution.py:297
  2.8 2.8 %collective-permute-start.1 = (f32[2,72,128]{2,1,0:T(8,128)S(1)}, f32[2,72,128]{2,1,0:T(8,128)S(1)}, u32[]{:S(2)}, u32[]{:S(2)}) collective-permute-start(f32[2,72,128]{2,1,0:T(8,128)S(1)} %pad_maximum_fusion.refs_0_), channel_id=1, source_target_pairs={{0,2},{1,5},{2,0},{3,7},{4,6},{5,1},{6,4},{7,3},{8,10},{9,13},{10,... | collective-permute-start | bytes 221192 | tf_op jit(solution)/shard_map/ppermute | solution.py:295
  5.7 1.5 %collective-permute-start.3 = (f32[2,72,128]{2,1,0:T(8,128)S(1)}, f32[2,72,128]{2,1,0:T(8,128)S(1)}, u32[]{:S(2)}, u32[]{:S(2)}) collective-permute-start(f32[2,72,128]{2,1,0:T(8,128)S(1)} %pad_maximum_fusion.refs_0_), channel_id=1, source_target_pairs={{0,6},{1,9},{2,4},{3,11},{4,2},{5,13},{6,0},{7,15},{8,14},{9,1},{1... | collective-permute-start | bytes 221192 | tf_op jit(solution)/shard_map/ppermute | solution.py:295
  7.2 0.8 %multiply_bitcast_fusion.1 = (f32[1,128]{1,0:T(1,128)S(1)}, f32[128]{0:T(128)S(1)}, f32[128]{0:T(128)S(1)}) fusion(s32[2048]{0:T(1024)} %param.9, s32[]{:T(128)S(6)} %select_n.19), kind=kLoop, calls=%fused_computation.16 | loop fusion | flops 5632 | bytes 2052 | tf_op jit(solution)/shard_map/stack | solution.py:402
  8.0 3.6 %collective-permute-start.5 = (f32[2,72,128]{2,1,0:T(8,128)S(1)}, f32[2,72,128]{2,1,0:T(8,128)S(1)}, u32[]{:S(2)}, u32[]{:S(2)}) collective-permute-start(f32[2,72,128]{2,1,0:T(8,128)S(1)} %pad_maximum_fusion.refs_0_), channel_id=1, source_target_pairs={{0,10},{1,13},{2,8},{3,15},{4,14},{5,9},{6,12},{7,11},{8,2},{9,5},... | collective-permute-start | bytes 221192 | tf_op jit(solution)/shard_map/ppermute | solution.py:295
  11.6 0.0 collective-permute-done.1.refs_1_
  11.6 0.0 collective-permute-start.2
  11.6 0.0 collective-permute-done.3.refs_0_.refs_3_
  11.6 0.5 %collective-permute-start.4 = (f32[2,72,128]{2,1,0:T(8,128)S(1)}, f32[2,72,128]{2,1,0:T(8,128)S(1)}, u32[]{:S(2)}, u32[]{:S(2)}) collective-permute-start(f32[2,72,128]{2,1,0:T(8,128)S(1)} %collective-permute-done.3.refs_0_.refs_3_), channel_id=1, source_target_pairs={{0,1},{1,0},{2,3},{3,2},{4,5},{5,4},{6,7},{7,6},{8,9},{9,8},{10,11... | collective-permute-start | bytes 221192 | tf_op jit(solution)/shard_map/ppermute | solution.py:345
  12.2 0.1 pad.3.clone
  12.3 2.4 %collective-permute-start.7 = (f32[2,72,128]{2,1,0:T(8,128)S(1)}, f32[2,72,128]{2,1,0:T(8,128)S(1)}, u32[]{:S(2)}, u32[]{:S(2)}) collective-permute-start(f32[2,72,128]{2,1,0:T(8,128)S(1)} %pad_maximum_fusion.refs_0_), channel_id=1, source_target_pairs={{0,14},{1,15},{2,12},{3,13},{4,10},{5,11},{6,8},{7,9},{8,6},{9,7},... | collective-permute-start | bytes 221192 | tf_op jit(solution)/shard_map/ppermute | solution.py:295
  14.6 0.0 collective-permute-done.2.refs_2_
  14.6 1.7 %strips0.1 = (bf16[6,256,256]{2,1,0:T(8,128)(2,1)S(1)}, f32[32,768]{1,0:T(8,128)S(1)}, bf16[32,768]{1,0:T(8,128)(2,1)S(1)}, bf16[32,768]{1,0:T(8,128)(2,1)S(1)}) custom-call(f32[2,72,128]{2,1,0:T(8,128)S(1)} %pad_maximum_fusion.refs_0_, f32[2,72,128]{2,1,0:T(8,128)S(1)} %collective-permute-done.1.refs_1_, f32[2,72,128]{2,1,0:T(8,128)S(1)} %collective-permute-done.2.refs_2_), custom_call_target="tpu_custom_call" | custom-call | flops 11796480 | bytes 786432 | tf_op jit(solution)/shard_map/strips0/pallas_call | solution.py:328
  16.4 0.0 collective-permute-done.4.refs_1_.refs_4_
  16.4 2.2 %strips3.1 = (bf16[9,256,256]{2,1,0:T(8,128)(2,1)S(1)}, f32[32,1280]{1,0:T(8,128)S(1)}, bf16[32,1280]{1,0:T(8,128)(2,1)S(1)}, bf16[32,1280]{1,0:T(8,128)(2,1)S(1)}) custom-call(f32[2,72,128]{2,1,0:T(8,128)S(1)} %collective-permute-done.3.refs_0_.refs_3_, f32[2,72,128]{2,1,0:T(8,128)S(1)} %collective-permute-done.4.refs_1_.refs_4_, ...), custom_call_target="tpu_custom_call" | custom-call | flops 17694720 | bytes 1179648 | tf_op jit(solution)/shard_map/strips3/pallas_call | solution.py:328
  18.6 0.0 collective-permute-done.5.refs_0_.refs_5_
  18.6 0.3 collective-permute-start.6
  18.9 0.1 maximum_maximum_fusion.refs_8_
  19.0 1.7 %strips5.1 = (bf16[6,256,256]{2,1,0:T(8,128)(2,1)S(1)}, f32[32,1536]{1,0:T(8,128)S(1)}, bf16[32,1536]{1,0:T(8,128)(2,1)S(1)}, bf16[32,1536]{1,0:T(8,128)(2,1)S(1)}) custom-call(f32[2,72,128]{2,1,0:T(8,128)S(1)} %collective-permute-done.5.refs_0_.refs_5_, bf16[32,1280]{1,0:T(8,128)(2,1)S(1)} %get-tuple-element.24.refs_1_, ...), custom_call_target="tpu_custom_call" | custom-call | flops 11796480 | bytes 786432 | tf_op jit(solution)/shard_map/strips5/pallas_call | solution.py:328
  20.7 0.0 collective-permute-done.6.refs_0_.refs_6_
  20.7 1.9 %strips6.1 = (bf16[7,256,256]{2,1,0:T(8,128)(2,1)S(1)}, f32[32,1792]{1,0:T(8,128)S(1)}, bf16[32,1792]{1,0:T(8,128)(2,1)S(1)}, bf16[32,1792]{1,0:T(8,128)(2,1)S(1)}) custom-call(f32[2,72,128]{2,1,0:T(8,128)S(1)} %collective-permute-done.6.refs_0_.refs_6_, bf16[32,1536]{1,0:T(8,128)(2,1)S(1)} %get-tuple-element.26.refs_1_, ...), custom_call_target="tpu_custom_call" | custom-call | flops 13762560 | bytes 917504 | tf_op jit(solution)/shard_map/strips6/pallas_call | solution.py:328
  22.6 0.0 collective-permute-done.7.refs_7_
  22.6 8.9 %iterate.1 = (f32[32,128]{1,0:T(8,128)}, f32[32,128]{1,0:T(8,128)}) custom-call(f32[2,72,128]{2,1,0:T(8,128)S(1)} %pad_maximum_fusion.refs_0_, f32[2,72,128]{2,1,0:T(8,128)S(1)} %collective-permute-done.1.refs_1_, f32[2,72,128]{2,1,0:T(8,128)S(1)} %collective-permute-done.2.refs_2_, f32[2,72,128]{2,1,0:T(8,128)S(1)} %collective-permute-done.3.refs_0_.refs_3_, ...), custom_call_target="tpu_custom_call" | custom-call | tf_op jit(solution)/shard_map/iterate/pallas_call | solution.py:358
  (3 shorter events, 0.1 us)
Async XLA Ops:
  1.4 1.4 %collective-permute-start = (f32[1,72,128]{2,1,0:T(8,128)S(1)}, f32[1,72,128]{2,1,0:T(8,128)S(1)}, u32[]{:S(2)}, u32[]{:S(2)}) collective-permute-start(f32[1,72,128]{2,1,0:T(8,128)S(1)} %bitcast.7), channel_id=1, source_target_pairs={{0,1},{1,0},{2,3},{3,2},{4,5},{5,4},{6,7},{7,6},{8,9},{9,8},{10,11... | collective-permute-start | bytes 110600 | tf_op jit(solution)/shard_map/ppermute | solution.py:297
  2.8 8.8 %collective-permute-start.1 = (f32[2,72,128]{2,1,0:T(8,128)S(1)}, f32[2,72,128]{2,1,0:T(8,128)S(1)}, u32[]{:S(2)}, u32[]{:S(2)}) collective-permute-start(f32[2,72,128]{2,1,0:T(8,128)S(1)} %pad_maximum_fusion.refs_0_), channel_id=1, source_target_pairs={{0,2},{1,5},{2,0},{3,7},{4,6},{5,1},{6,4},{7,3},{8,10},{9,13},{10,... | collective-permute-start | bytes 221192 | tf_op jit(solution)/shard_map/ppermute | solution.py:295
  5.7 6.0 %collective-permute-start.3 = (f32[2,72,128]{2,1,0:T(8,128)S(1)}, f32[2,72,128]{2,1,0:T(8,128)S(1)}, u32[]{:S(2)}, u32[]{:S(2)}) collective-permute-start(f32[2,72,128]{2,1,0:T(8,128)S(1)} %pad_maximum_fusion.refs_0_), channel_id=1, source_target_pairs={{0,6},{1,9},{2,4},{3,11},{4,2},{5,13},{6,0},{7,15},{8,14},{9,1},{1... | collective-permute-start | bytes 221192 | tf_op jit(solution)/shard_map/ppermute | solution.py:295
  8.0 10.6 %collective-permute-start.5 = (f32[2,72,128]{2,1,0:T(8,128)S(1)}, f32[2,72,128]{2,1,0:T(8,128)S(1)}, u32[]{:S(2)}, u32[]{:S(2)}) collective-permute-start(f32[2,72,128]{2,1,0:T(8,128)S(1)} %pad_maximum_fusion.refs_0_), channel_id=1, source_target_pairs={{0,10},{1,13},{2,8},{3,15},{4,14},{5,9},{6,12},{7,11},{8,2},{9,5},... | collective-permute-start | bytes 221192 | tf_op jit(solution)/shard_map/ppermute | solution.py:295
  11.6 3.0 %collective-permute-start.2 = (f32[2,72,128]{2,1,0:T(8,128)S(1)}, f32[2,72,128]{2,1,0:T(8,128)S(1)}, u32[]{:S(2)}, u32[]{:S(2)}) collective-permute-start(f32[2,72,128]{2,1,0:T(8,128)S(1)} %collective-permute-done.1.refs_1_), channel_id=1, source_target_pairs={{0,1},{1,0},{2,3},{3,2},{4,5},{5,4},{6,7},{7,6},{8,9},{9,8},{10,11... | collective-permute-start | bytes 221192 | tf_op jit(solution)/shard_map/ppermute | solution.py:345
  11.6 4.7 %collective-permute-start.4 = (f32[2,72,128]{2,1,0:T(8,128)S(1)}, f32[2,72,128]{2,1,0:T(8,128)S(1)}, u32[]{:S(2)}, u32[]{:S(2)}) collective-permute-start(f32[2,72,128]{2,1,0:T(8,128)S(1)} %collective-permute-done.3.refs_0_.refs_3_), channel_id=1, source_target_pairs={{0,1},{1,0},{2,3},{3,2},{4,5},{5,4},{6,7},{7,6},{8,9},{9,8},{10,11... | collective-permute-start | bytes 221192 | tf_op jit(solution)/shard_map/ppermute | solution.py:345
  12.3 10.3 %collective-permute-start.7 = (f32[2,72,128]{2,1,0:T(8,128)S(1)}, f32[2,72,128]{2,1,0:T(8,128)S(1)}, u32[]{:S(2)}, u32[]{:S(2)}) collective-permute-start(f32[2,72,128]{2,1,0:T(8,128)S(1)} %pad_maximum_fusion.refs_0_), channel_id=1, source_target_pairs={{0,14},{1,15},{2,12},{3,13},{4,10},{5,11},{6,8},{7,9},{8,6},{9,7},... | collective-permute-start | bytes 221192 | tf_op jit(solution)/shard_map/ppermute | solution.py:295
  18.6 2.1 %collective-permute-start.6 = (f32[2,72,128]{2,1,0:T(8,128)S(1)}, f32[2,72,128]{2,1,0:T(8,128)S(1)}, u32[]{:S(2)}, u32[]{:S(2)}) collective-permute-start(f32[2,72,128]{2,1,0:T(8,128)S(1)} %collective-permute-done.5.refs_0_.refs_5_), channel_id=1, source_target_pairs={{0,1},{1,0},{2,3},{3,2},{4,5},{5,4},{6,7},{7,6},{8,9},{9,8},{10,11... | collective-permute-start | bytes 221192 | tf_op jit(solution)/shard_map/ppermute | solution.py:351

commit v4 on v3

--- a/solution.py
+++ b/solution.py
@@ -197,20 +197,21 @@
     build_strips(old, new, lhs, rhs, weighted, table, field, turned, even, odd)
 
 
-def iterate_kernel(pieces, blocks, columns, groups, *refs):
+def iterate_kernel(pieces, new, blocks, columns, groups, *refs):
     data, refs = refs[:pieces], refs[pieces:]
-    last, toward_ref, before, refs = refs[0], refs[1], refs[2:4], refs[4:]
+    rest, refs = refs[:new], refs[new:]
+    toward_ref, before, refs = refs[0], refs[1:3], refs[3:]
     tables, refs = refs[: len(groups)], refs[len(groups) :]
     fields, refs = refs[: len(groups)], refs[len(groups) :]
     density_out, far_out = refs[:2]
     lhs, rhs, weighted, table, field, turned, even, odd, coords, plane, dens, inc = refs[2:]
     total = blocks * BLOCK
     width = data[0].shape[2]
-    old = blocks - 1
-    prepare(old, [last], columns, total, lhs, rhs, weighted, before)
-    build_strips(old, 1, lhs, rhs, weighted, table, field, turned, even, odd)
-
-    everything = list(data) + [last]
+    old = blocks - new
+    prepare(old, rest, columns, total, lhs, rhs, weighted, before)
+    build_strips(old, new, lhs, rhs, weighted, table, field, turned, even, odd)
+
+    everything = list(data) + list(rest)
     coords[0:3, :] = lanes(everything, 0, 3) * TURNS
     inverse = 1.0 / lanes(everything, 3, 1)
     dens[...] = lanes(everything, 8, columns)
@@ -220,7 +221,7 @@
     dens[...] = dens[...] - (field[...] + inc[...]) * inverse
 
     entries = {}
-    for (first, count), part in zip(list(groups) + [(old, 1)], list(tables) + [table]):
+    for (first, count), part in zip(list(groups) + [(old, new)], list(tables) + [table]):
         k = 0
         for j in range(first, first + count):
             for i in range(j + 1):
@@ -250,17 +251,18 @@
             phase = toward[:, 0:1] * coords[0:1, span] + toward[:, 1:2] * coords[1:2, span]
             phase = phase + toward[:, 2:3] * coords[2:3, span]
             plane[:, span] = cos_turns(phase, 1.0).astype(jnp.bfloat16)
+        downs, sides = [None] * blocks, [None] * blocks
         for b in range(blocks):
-            total_field = None
-            for j in range(b, blocks):
-                term = down(part_of(w, j), entry(j, b))
-                total_field = term if total_field is None else total_field + term
-            side = None
-            for i in range(b):
-                term = across(entry(b, i), part_of(w, i))
-                side = term if side is None else side + term
-            if side is not None:
-                total_field += side.T
+            top = blocks - 1 - b
+            for n in range(max(blocks - b, top)):
+                if b + n < blocks:
+                    term = down(part_of(w, b + n), entry(b + n, b))
+                    downs[b] = term if n == 0 else downs[b] + term
+                if n < top:
+                    term = across(entry(top, n), part_of(w, n))
+                    sides[top] = term if n == 0 else sides[top] + term
+        for b in range(blocks):
+            total_field = downs[b] if sides[b] is None else downs[b] + sides[b].T
             span = slice(b * BLOCK, (b + 1) * BLOCK)
             dens[:, span] = dens[:, span] - (total_field + inc[:, span]) * inverse[:, span]
         return carry
@@ -343,25 +345,24 @@
 
     early, late = near[:2], near[2:]
     swapped = [lax.ppermute(array, "sub", swap) for array in early]
-    strips([own, early[0], swapped[0]])
-    for array, other in zip(early[1:], swapped[1:]):
-        strips([array, other])
+    strips([own] + [array for pair in zip(early, swapped) for array in pair])
+    rest = []
     for array in late:
         array, fields[-1] = lax.optimization_barrier((array, fields[-1]))
         other = lax.ppermute(array, "sub", swap)
-        strips([array])
-        strips([other])
-
-    old = len(held)
-    pieces = len(held)
-    shapes = strip_shapes(old, 1)
+        strips(rest + [array])
+        rest = [other]
+    rest.append(last)
+
+    pieces, new = len(held), len(rest)
+    shapes = strip_shapes(pieces, new)
     return pl.pallas_call(
-        functools.partial(iterate_kernel, pieces, blocks, columns, tuple(groups)),
+        functools.partial(iterate_kernel, pieces, new, blocks, columns, tuple(groups)),
         out_shape=(
             jax.ShapeDtypeStruct((columns, width), f32),
             jax.ShapeDtypeStruct((columns, rows), f32),
         ),
-        in_specs=[vmem] * (pieces + 4 + 2 * len(groups)),
+        in_specs=[vmem] * (pieces + new + 3 + 2 * len(groups)),
         out_specs=(vmem, vmem),
         scratch_shapes=[pltpu.VMEM(*shapes[k]) for k in (4, 2, 3, 0, 1, 5, 6, 7)]
         + [
@@ -372,7 +373,7 @@
         ],
         compiler_params=pltpu.CompilerParams(vmem_limit_bytes=VMEM_LIMIT),
         name="iterate",
-    )(*held, last, toward, *before, *tables, *fields)
+    )(*held, *rest, toward, *before, *tables, *fields)
 
 
 def single_layer(targets, sources):

time: 31.8 us -> 29.5 us (0.928)
  Pallas kernels: 17.3 us -> 15 us
    pallas_call x4 -> x2, Pallas kernels: 7.55 us -> 5.27 us  [strips(): pl.pallas_call(functools.partial(strips_kernel, new, old, new, columns, t...]
  transfers between devices with their start and end apart: 8 -> 8, of which waited for: 1 -> 1; matrix products, arithmetic and copies ran while one was open for 3% -> 3% of each run, Pallas kernels for 24% -> 18%
where the time goes in v4:
time: 29.5 us; the launch traced here: 29.2 us
  Pallas kernels  15 us (51%)
  starting transfers between devices  11.7 us (40%)
  other arithmetic  0.94 us (3%)
  waiting for transfers between devices  0.88 us (3%)
  between operations  0.68 us (2%)
    ppermute x4, starting transfers between devices, fetch(): return lax.ppermute(array, names, pairs)  10.3 us
    pallas_call x1, Pallas kernels, replicated_shards(): pl.pallas_call(functools.partial(iterate_kernel, pieces, new, blocks, col...  8.92 us
    pallas_call x2, Pallas kernels, strips(): pl.pallas_call(functools.partial(strips_kernel, new, old, new, columns, t...  5.27 us
    ppermute x1, waiting for transfers between devices, replicated_shards(): own = jnp.concatenate([payload, lax.ppermute(payload, 'sub', swap)], axis=0)  0.87 us
    another operation x2, other arithmetic, receiver_directions(): jnp.stack([radial * jnp.cos(azimuth), radial * jnp.sin(azimuth), height])  0.86 us
    pallas_call x1, Pallas kernels, replicated_shards(): pl.pallas_call(pack_kernel, out_shape=jax.ShapeDtypeStruct((8 + 2 * colum...  0.8 us
  transfers between devices with their start and end apart: 8, of which 1 were waited for; matrix products, arithmetic and copies ran while one was open for 3% of the time, Pallas kernels for 18%

profile of v4, /device:TPU:0, one launch (start us, length us, event | category | flops | bytes accessed | tf_op | source)
XLA Modules:
  0.0 29.2 jit_solution(7556497770701098556)
XLA Ops:
  0.6 0.8 %pack.1 = f32[72,128]{1,0:T(8,128)S(1)} custom-call(f32[3,128]{1,0:T(4,128)} %points.1, f32[1,128]{1,0:T(1,128)} %bitcast.10, f32[32,128]{1,0:T(8,128)} %density.1, f32[32,128]{1,0:T(8,128)} %incident.1), custom_call_target="tpu_custom_call" | custom-call | tf_op jit(solution)/shard_map/pack/pallas_call | solution.py:283
  1.4 0.5 %collective-permute-start = (f32[1,72,128]{2,1,0:T(8,128)S(1)}, f32[1,72,128]{2,1,0:T(8,128)S(1)}, u32[]{:S(2)}, u32[]{:S(2)}) collective-permute-start(f32[1,72,128]{2,1,0:T(8,128)S(1)} %bitcast.7), channel_id=1, source_target_pairs={{0,1},{1,0},{2,3},{3,2},{4,5},{5,4},{6,7},{7,6},{8,9},{9,8},{10,11... | collective-permute-start | bytes 110600 | tf_op jit(solution)/shard_map/ppermute | solution.py:299
  2.0 0.9 %collective-permute-done = f32[1,72,128]{2,1,0:T(8,128)S(1)} collective-permute-done((f32[1,72,128]{2,1,0:T(8,128)S(1)}, f32[1,72,128]{2,1,0:T(8,128)S(1)}, u32[]{:S(2)}, u32[]{:S(2)}) %collective-permute-start) | collective-permute-done | bytes 36896 | tf_op jit(solution)/shard_map/ppermute | solution.py:299
  2.8 2.8 %collective-permute-start.1 = (f32[2,72,128]{2,1,0:T(8,128)S(1)}, f32[2,72,128]{2,1,0:T(8,128)S(1)}, u32[]{:S(2)}, u32[]{:S(2)}) collective-permute-start(f32[2,72,128]{2,1,0:T(8,128)S(1)} %pad_maximum_fusion.refs_0_), channel_id=1, source_target_pairs={{0,2},{1,5},{2,0},{3,7},{4,6},{5,1},{6,4},{7,3},{8,10},{9,13},{10,... | collective-permute-start | bytes 221192 | tf_op jit(solution)/shard_map/ppermute | solution.py:297
  5.7 1.5 %collective-permute-start.3 = (f32[2,72,128]{2,1,0:T(8,128)S(1)}, f32[2,72,128]{2,1,0:T(8,128)S(1)}, u32[]{:S(2)}, u32[]{:S(2)}) collective-permute-start(f32[2,72,128]{2,1,0:T(8,128)S(1)} %pad_maximum_fusion.refs_0_), channel_id=1, source_target_pairs={{0,6},{1,9},{2,4},{3,11},{4,2},{5,13},{6,0},{7,15},{8,14},{9,1},{1... | collective-permute-start | bytes 221192 | tf_op jit(solution)/shard_map/ppermute | solution.py:297
  7.2 0.8 %multiply_bitcast_fusion.1 = (f32[1,128]{1,0:T(1,128)S(1)}, f32[128]{0:T(128)S(1)}, f32[128]{0:T(128)S(1)}) fusion(s32[2048]{0:T(1024)} %param.9, s32[]{:T(128)S(6)} %select_n.19), kind=kLoop, calls=%fused_computation.16 | loop fusion | flops 5632 | bytes 2052 | tf_op jit(solution)/shard_map/stack | solution.py:403
  8.0 3.6 %collective-permute-start.5 = (f32[2,72,128]{2,1,0:T(8,128)S(1)}, f32[2,72,128]{2,1,0:T(8,128)S(1)}, u32[]{:S(2)}, u32[]{:S(2)}) collective-permute-start(f32[2,72,128]{2,1,0:T(8,128)S(1)} %pad_maximum_fusion.refs_0_), channel_id=1, source_target_pairs={{0,10},{1,13},{2,8},{3,15},{4,14},{5,9},{6,12},{7,11},{8,2},{9,5},... | collective-permute-start | bytes 221192 | tf_op jit(solution)/shard_map/ppermute | solution.py:297
  11.6 0.0 collective-permute-done.1.refs_1_
  11.6 0.0 collective-permute-start.2
  11.6 0.0 collective-permute-done.3.refs_3_
  11.6 0.5 %collective-permute-start.4 = (f32[2,72,128]{2,1,0:T(8,128)S(1)}, f32[2,72,128]{2,1,0:T(8,128)S(1)}, u32[]{:S(2)}, u32[]{:S(2)}) collective-permute-start(f32[2,72,128]{2,1,0:T(8,128)S(1)} %collective-permute-done.3.refs_3_), channel_id=1, source_target_pairs={{0,1},{1,0},{2,3},{3,2},{4,5},{5,4},{6,7},{7,6},{8,9},{9,8},{10,11... | collective-permute-start | bytes 221192 | tf_op jit(solution)/shard_map/ppermute | solution.py:347
  12.2 0.1 pad.3.clone
  12.3 2.4 %collective-permute-start.7 = (f32[2,72,128]{2,1,0:T(8,128)S(1)}, f32[2,72,128]{2,1,0:T(8,128)S(1)}, u32[]{:S(2)}, u32[]{:S(2)}) collective-permute-start(f32[2,72,128]{2,1,0:T(8,128)S(1)} %pad_maximum_fusion.refs_0_), channel_id=1, source_target_pairs={{0,14},{1,15},{2,12},{3,13},{4,10},{5,11},{6,8},{7,9},{8,6},{9,7},... | collective-permute-start | bytes 221192 | tf_op jit(solution)/shard_map/ppermute | solution.py:297
  14.6 0.0 collective-permute-done.2.refs_2_
  14.6 0.0 collective-permute-done.4.refs_4_
  14.6 3.5 %strips0.1 = (bf16[15,256,256]{2,1,0:T(8,128)(2,1)S(1)}, f32[32,1280]{1,0:T(8,128)S(1)}, bf16[32,1280]{1,0:T(8,128)(2,1)S(1)}, bf16[32,1280]{1,0:T(8,128)(2,1)S(1)}) custom-call(f32[2,72,128]{2,1,0:T(8,128)S(1)} %pad_maximum_fusion.refs_0_, f32[2,72,128]{2,1,0:T(8,128)S(1)} %collective-permute-done.1.refs_1_, ...), custom_call_target="tpu_custom_call" | custom-call | flops 29491200 | bytes 1966080 | tf_op jit(solution)/shard_map/strips0/pallas_call | solution.py:330
  18.2 0.0 collective-permute-done.5.refs_0_.refs_5_
  18.2 0.3 %collective-permute-start.6 = (f32[2,72,128]{2,1,0:T(8,128)S(1)}, f32[2,72,128]{2,1,0:T(8,128)S(1)}, u32[]{:S(2)}, u32[]{:S(2)}) collective-permute-start(f32[2,72,128]{2,1,0:T(8,128)S(1)} %collective-permute-done.5.refs_0_.refs_5_), channel_id=1, source_target_pairs={{0,1},{1,0},{2,3},{3,2},{4,5},{5,4},{6,7},{7,6},{8,9},{9,8},{10,11... | collective-permute-start | bytes 221192 | tf_op jit(solution)/shard_map/ppermute | solution.py:352
  18.5 0.1 maximum_maximum_fusion.refs_8_
  18.6 1.7 %strips5.1 = (bf16[6,256,256]{2,1,0:T(8,128)(2,1)S(1)}, f32[32,1536]{1,0:T(8,128)S(1)}, bf16[32,1536]{1,0:T(8,128)(2,1)S(1)}, bf16[32,1536]{1,0:T(8,128)(2,1)S(1)}) custom-call(f32[2,72,128]{2,1,0:T(8,128)S(1)} %collective-permute-done.5.refs_0_.refs_5_, bf16[32,1280]{1,0:T(8,128)(2,1)S(1)} %get-tuple-element.14.refs_1_, ...), custom_call_target="tpu_custom_call" | custom-call | flops 11796480 | bytes 786432 | tf_op jit(solution)/shard_map/strips5/pallas_call | solution.py:330
  20.3 0.0 collective-permute-done.7.refs_7_
  20.3 0.0 collective-permute-done.6.refs_6_
  20.3 8.9 %iterate.1 = (f32[32,128]{1,0:T(8,128)}, f32[32,128]{1,0:T(8,128)}) custom-call(f32[2,72,128]{2,1,0:T(8,128)S(1)} %pad_maximum_fusion.refs_0_, f32[2,72,128]{2,1,0:T(8,128)S(1)} %collective-permute-done.1.refs_1_, f32[2,72,128]{2,1,0:T(8,128)S(1)} %collective-permute-done.2.refs_2_, f32[2,72,128]{2,1,0:T(8,128)S(1)} %collective-permute-done.3.refs_3_, ...), custom_call_target="tpu_custom_call" | custom-call | tf_op jit(solution)/shard_map/iterate/pallas_call | solution.py:359
  (3 shorter events, 0.1 us)
Async XLA Ops:
  1.4 1.4 %collective-permute-start = (f32[1,72,128]{2,1,0:T(8,128)S(1)}, f32[1,72,128]{2,1,0:T(8,128)S(1)}, u32[]{:S(2)}, u32[]{:S(2)}) collective-permute-start(f32[1,72,128]{2,1,0:T(8,128)S(1)} %bitcast.7), channel_id=1, source_target_pairs={{0,1},{1,0},{2,3},{3,2},{4,5},{5,4},{6,7},{7,6},{8,9},{9,8},{10,11... | collective-permute-start | bytes 110600 | tf_op jit(solution)/shard_map/ppermute | solution.py:299
  2.8 8.8 %collective-permute-start.1 = (f32[2,72,128]{2,1,0:T(8,128)S(1)}, f32[2,72,128]{2,1,0:T(8,128)S(1)}, u32[]{:S(2)}, u32[]{:S(2)}) collective-permute-start(f32[2,72,128]{2,1,0:T(8,128)S(1)} %pad_maximum_fusion.refs_0_), channel_id=1, source_target_pairs={{0,2},{1,5},{2,0},{3,7},{4,6},{5,1},{6,4},{7,3},{8,10},{9,13},{10,... | collective-permute-start | bytes 221192 | tf_op jit(solution)/shard_map/ppermute | solution.py:297
  5.7 6.0 %collective-permute-start.3 = (f32[2,72,128]{2,1,0:T(8,128)S(1)}, f32[2,72,128]{2,1,0:T(8,128)S(1)}, u32[]{:S(2)}, u32[]{:S(2)}) collective-permute-start(f32[2,72,128]{2,1,0:T(8,128)S(1)} %pad_maximum_fusion.refs_0_), channel_id=1, source_target_pairs={{0,6},{1,9},{2,4},{3,11},{4,2},{5,13},{6,0},{7,15},{8,14},{9,1},{1... | collective-permute-start | bytes 221192 | tf_op jit(solution)/shard_map/ppermute | solution.py:297
  8.0 10.1 %collective-permute-start.5 = (f32[2,72,128]{2,1,0:T(8,128)S(1)}, f32[2,72,128]{2,1,0:T(8,128)S(1)}, u32[]{:S(2)}, u32[]{:S(2)}) collective-permute-start(f32[2,72,128]{2,1,0:T(8,128)S(1)} %pad_maximum_fusion.refs_0_), channel_id=1, source_target_pairs={{0,10},{1,13},{2,8},{3,15},{4,14},{5,9},{6,12},{7,11},{8,2},{9,5},... | collective-permute-start | bytes 221192 | tf_op jit(solution)/shard_map/ppermute | solution.py:297
  11.6 3.0 %collective-permute-start.2 = (f32[2,72,128]{2,1,0:T(8,128)S(1)}, f32[2,72,128]{2,1,0:T(8,128)S(1)}, u32[]{:S(2)}, u32[]{:S(2)}) collective-permute-start(f32[2,72,128]{2,1,0:T(8,128)S(1)} %collective-permute-done.1.refs_1_), channel_id=1, source_target_pairs={{0,1},{1,0},{2,3},{3,2},{4,5},{5,4},{6,7},{7,6},{8,9},{9,8},{10,11... | collective-permute-start | bytes 221192 | tf_op jit(solution)/shard_map/ppermute | solution.py:347
  11.6 3.0 %collective-permute-start.4 = (f32[2,72,128]{2,1,0:T(8,128)S(1)}, f32[2,72,128]{2,1,0:T(8,128)S(1)}, u32[]{:S(2)}, u32[]{:S(2)}) collective-permute-start(f32[2,72,128]{2,1,0:T(8,128)S(1)} %collective-permute-done.3.refs_3_), channel_id=1, source_target_pairs={{0,1},{1,0},{2,3},{3,2},{4,5},{5,4},{6,7},{7,6},{8,9},{9,8},{10,11... | collective-permute-start | bytes 221192 | tf_op jit(solution)/shard_map/ppermute | solution.py:347
  12.3 8.0 %collective-permute-start.7 = (f32[2,72,128]{2,1,0:T(8,128)S(1)}, f32[2,72,128]{2,1,0:T(8,128)S(1)}, u32[]{:S(2)}, u32[]{:S(2)}) collective-permute-start(f32[2,72,128]{2,1,0:T(8,128)S(1)} %pad_maximum_fusion.refs_0_), channel_id=1, source_target_pairs={{0,14},{1,15},{2,12},{3,13},{4,10},{5,11},{6,8},{7,9},{8,6},{9,7},... | collective-permute-start | bytes 221192 | tf_op jit(solution)/shard_map/ppermute | solution.py:297
  18.2 2.1 %collective-permute-start.6 = (f32[2,72,128]{2,1,0:T(8,128)S(1)}, f32[2,72,128]{2,1,0:T(8,128)S(1)}, u32[]{:S(2)}, u32[]{:S(2)}) collective-permute-start(f32[2,72,128]{2,1,0:T(8,128)S(1)} %collective-permute-done.5.refs_0_.refs_5_), channel_id=1, source_target_pairs={{0,1},{1,0},{2,3},{3,2},{4,5},{5,4},{6,7},{7,6},{8,9},{9,8},{10,11... | collective-permute-start | bytes 221192 | tf_op jit(solution)/shard_map/ppermute | solution.py:352

commit v5 on v4

--- a/solution.py
+++ b/solution.py
@@ -19,6 +19,7 @@
 TURNS = WAVENUMBER / (2.0 * math.pi)
 SMOOTH_TURNS = (SMOOTHING * TURNS) ** 2
 BLOCK = 256
+UNROLL = 4
 TABLE_LIMIT = 8 * 2**20
 VMEM_LIMIT = 24 * 2**20
 
@@ -156,24 +157,28 @@
     field[...] = jnp.zeros_like(field)
     turned[...] = jnp.zeros_like(turned)
     table[0] = jnp.zeros((BLOCK, BLOCK), jnp.bfloat16)
+    stage = (even, odd)
     even[...] = distances(0)
 
-    def pair(t, carry):
-        k = 2 * t
-        odd[...] = distances(k + 1)
-        products(jnp.maximum(k - 1, 0), k > 0)
-        fill(k, even)
-        even[...] = distances(jnp.minimum(k + 2, count - 1))
-        products(k, True)
-        fill(k + 1, odd)
+    def several(t, carry):
+        k = UNROLL * t
+        for n in range(UNROLL):
+            stage[(n + 1) % 2][...] = distances(jnp.minimum(k + n + 1, count - 1))
+            if n == 0:
+                products(jnp.maximum(k - 1, 0), k > 0)
+            else:
+                products(k + n - 1, True)
+            fill(k + n, stage[n % 2])
         return carry
 
-    lax.fori_loop(0, count // 2, pair, 0)
-    if count >= 2:
-        products(2 * (count // 2) - 1, True)
-    if count % 2:
-        fill(count - 1, even)
-        products(count - 1, True)
+    lax.fori_loop(0, count // UNROLL, several, 0)
+    for n, k in enumerate(range(count // UNROLL * UNROLL, count)):
+        if k + 1 < count:
+            stage[(n + 1) % 2][...] = distances(k + 1)
+        if k:
+            products(k - 1, True)
+        fill(k, stage[n % 2])
+    products(count - 1, True)
     field[:, old * BLOCK :] += turned[...].T
 
 
@@ -296,9 +301,9 @@
         pairs = [(q * 2 + c, (q ^ offsets[c]) * 2 + c) for q in range(chips) for c in range(2)]
         return lax.ppermute(array, names, pairs)
 
+    far = fetch(payload, (chips - 1, chips - 1))
     own = jnp.concatenate([payload, lax.ppermute(payload, "sub", swap)], axis=0)
     near = [fetch(own, (k, k + 1)) for k in range(1, chips - 1, 2)]
-    last = fetch(own, (chips - 1, chips - 1))
 
     place = (lax.axis_index("tgt") * count_src + lax.axis_index("src")) * count_sub + lax.axis_index("sub")
     rows = receivers.shape[0] // (chips * count_sub)
@@ -324,13 +329,13 @@
     groups, tables, fields, held, before = [], [], [], [], []
 
     def strips(data):
-        old, new = len(held), len(data)
+        old, new = (sum(array.shape[0] for array in arrays) // 2 for arrays in (held, data))
         shapes = strip_shapes(old, new)
         work = strip_size(old, new) * BLOCK * BLOCK
         table, field, *state = pl.pallas_call(
-            functools.partial(strips_kernel, new, old, new, columns, total),
+            functools.partial(strips_kernel, len(data), old, new, columns, total),
             out_shape=[jax.ShapeDtypeStruct(*shape) for shape in shapes[:4]],
-            in_specs=[vmem] * (new + len(before)),
+            in_specs=[vmem] * (len(data) + len(before)),
             out_specs=[vmem] * 4,
             scratch_shapes=[pltpu.VMEM(*shape) for shape in shapes[4:]],
             compiler_params=pltpu.CompilerParams(vmem_limit_bytes=VMEM_LIMIT),
@@ -343,19 +348,22 @@
         held.extend(data)
         before[:] = state
 
-    early, late = near[:2], near[2:]
-    swapped = [lax.ppermute(array, "sub", swap) for array in early]
-    strips([own] + [array for pair in zip(early, swapped) for array in pair])
-    rest = []
-    for array in late:
-        array, fields[-1] = lax.optimization_barrier((array, fields[-1]))
-        other = lax.ppermute(array, "sub", swap)
-        strips(rest + [array])
-        rest = [other]
-    rest.append(last)
-
+    def both(array):
+        return [array, lax.ppermute(array, "sub", swap)]
+
+    def swapped(array):
+        return lax.ppermute(array, "sub", swap)
+
+    first, late = [own, far, swapped(far)], near
+    if len(near) > 1:
+        first[1:1] = [near[0], swapped(near[0])]
+        late = near[1:]
+    strips(first)
+    *late, fields[0] = lax.optimization_barrier((*late, fields[0]))
+    rest = [swapped(array) for array in late]
+    strips(late)
     pieces, new = len(held), len(rest)
-    shapes = strip_shapes(pieces, new)
+    shapes = strip_shapes(blocks - new, new)
     return pl.pallas_call(
         functools.partial(iterate_kernel, pieces, new, blocks, columns, tuple(groups)),
         out_shape=(

time: 29.5 us -> 28.6 us (0.969)
  starting transfers between devices: 11.7 us -> 10.5 us
  waiting for transfers between devices: 0.88 us -> 1.3 us
    ppermute x4, starting transfers between devices: 10.3 us -> 8.82 us  [fetch(): return lax.ppermute(array, names, pairs)]
    ppermute x3 -> x4, waiting for transfers between devices: 0.01 us -> 1.08 us  [swapped(): return lax.ppermute(array, 'sub', swap)]
    ppermute x1, waiting for transfers between devices: 0.87 us -> 0.01 us  [replicated_shards(): own = jnp.concatenate([payload, lax.ppermute(payload, 'sub', swap)], axis=0)]
    ppermute x3 -> x4, starting transfers between devices: 0.81 us -> 1.2 us  [swapped(): return lax.ppermute(array, 'sub', swap)]
  transfers between devices with their start and end apart: 8 -> 9, of which waited for: 1 -> 3; matrix products, arithmetic and copies ran while one was open for 3% -> 4% of each run, Pallas kernels for 18% -> 18%
where the time goes in v5:
time: 28.6 us; the launch traced here: 28.3 us
  Pallas kernels  14.8 us (52%)
  starting transfers between devices  10.5 us (37%)
  waiting for transfers between devices  1.3 us (5%)
  other arithmetic  0.93 us (3%)
  between operations  0.67 us (2%)
    pallas_call x1, Pallas kernels, replicated_shards(): pl.pallas_call(functools.partial(iterate_kernel, pieces, new, blocks, col...  8.87 us
    ppermute x4, starting transfers between devices, fetch(): return lax.ppermute(array, names, pairs)  8.82 us
    pallas_call x2, Pallas kernels, strips(): pl.pallas_call(functools.partial(strips_kernel, len(data), old, new, colu...  5.08 us
    ppermute x4, starting transfers between devices, swapped(): return lax.ppermute(array, 'sub', swap)  1.2 us
    ppermute x4, waiting for transfers between devices, swapped(): return lax.ppermute(array, 'sub', swap)  1.08 us
    another operation x2, other arithmetic, receiver_directions(): jnp.stack([radial * jnp.cos(azimuth), radial * jnp.sin(azimuth), height])  0.86 us
    pallas_call x1, Pallas kernels, replicated_shards(): pl.pallas_call(pack_kernel, out_shape=jax.ShapeDtypeStruct((8 + 2 * colum...  0.8 us
  transfers between devices with their start and end apart: 9, of which 3 were waited for; matrix products, arithmetic and copies ran while one was open for 4% of the time, Pallas kernels for 18%

profile of v5, /device:TPU:0, one launch (start us, length us, event | category | flops | bytes accessed | tf_op | source)
XLA Modules:
  0.0 28.3 jit_solution(2822120633833548645)
XLA Ops:
  0.6 0.8 %pack.1 = f32[72,128]{1,0:T(8,128)S(1)} custom-call(f32[3,128]{1,0:T(4,128)} %points.1, f32[1,128]{1,0:T(1,128)} %bitcast.11, f32[32,128]{1,0:T(8,128)} %density.1, f32[32,128]{1,0:T(8,128)} %incident.1), custom_call_target="tpu_custom_call" | custom-call | tf_op jit(solution)/shard_map/pack/pallas_call | solution.py:288
  1.4 0.5 %collective-permute-start = (f32[1,72,128]{2,1,0:T(8,128)S(1)}, f32[1,72,128]{2,1,0:T(8,128)S(1)}, u32[]{:S(2)}, u32[]{:S(2)}) collective-permute-start(f32[1,72,128]{2,1,0:T(8,128)S(1)} %bitcast.7), channel_id=1, source_target_pairs={{0,1},{1,0},{2,3},{3,2},{4,5},{5,4},{6,7},{7,6},{8,9},{9,8},{10,11... | collective-permute-start | bytes 110600 | tf_op jit(solution)/shard_map/ppermute | solution.py:305
  2.0 5.6 %collective-permute-start.3 = (f32[1,72,128]{2,1,0:T(8,128)S(1)}, f32[1,72,128]{2,1,0:T(8,128)S(1)}, u32[]{:S(2)}, u32[]{:S(2)}) collective-permute-start(f32[1,72,128]{2,1,0:T(8,128)S(1)} %bitcast.8), channel_id=1, source_target_pairs={{0,14},{1,15},{2,12},{3,13},{4,10},{5,11},{6,8},{7,9},{8,6},{9,7},... | collective-permute-start | bytes 110600 | tf_op jit(solution)/shard_map/ppermute | solution.py:302
  7.6 0.0 collective-permute-done
  7.6 0.6 %collective-permute-start.1 = (f32[2,72,128]{2,1,0:T(8,128)S(1)}, f32[2,72,128]{2,1,0:T(8,128)S(1)}, u32[]{:S(2)}, u32[]{:S(2)}) collective-permute-start(f32[2,72,128]{2,1,0:T(8,128)S(1)} %pad_maximum_fusion.refs_0_), channel_id=1, source_target_pairs={{0,2},{1,5},{2,0},{3,7},{4,6},{5,1},{6,4},{7,3},{8,10},{9,13},{10,... | collective-permute-start | bytes 221192 | tf_op jit(solution)/shard_map/ppermute | solution.py:302
  8.2 0.8 %multiply_bitcast_fusion.1 = (f32[1,128]{1,0:T(1,128)S(1)}, f32[128]{0:T(128)S(1)}, f32[128]{0:T(128)S(1)}) fusion(s32[2048]{0:T(1024)} %param.9, s32[]{:T(128)S(6)} %select_n.19), kind=kLoop, calls=%fused_computation.16 | loop fusion | flops 5632 | bytes 2052 | tf_op jit(solution)/shard_map/stack | solution.py:411
  9.0 0.5 %collective-permute-start.5 = (f32[2,72,128]{2,1,0:T(8,128)S(1)}, f32[2,72,128]{2,1,0:T(8,128)S(1)}, u32[]{:S(2)}, u32[]{:S(2)}) collective-permute-start(f32[2,72,128]{2,1,0:T(8,128)S(1)} %pad_maximum_fusion.refs_0_), channel_id=1, source_target_pairs={{0,6},{1,9},{2,4},{3,11},{4,2},{5,13},{6,0},{7,15},{8,14},{9,1},{1... | collective-permute-start | bytes 221192 | tf_op jit(solution)/shard_map/ppermute | solution.py:302
  9.5 2.1 %collective-permute-start.6 = (f32[2,72,128]{2,1,0:T(8,128)S(1)}, f32[2,72,128]{2,1,0:T(8,128)S(1)}, u32[]{:S(2)}, u32[]{:S(2)}) collective-permute-start(f32[2,72,128]{2,1,0:T(8,128)S(1)} %pad_maximum_fusion.refs_0_), channel_id=1, source_target_pairs={{0,10},{1,13},{2,8},{3,15},{4,14},{5,9},{6,12},{7,11},{8,2},{9,5},... | collective-permute-start | bytes 221192 | tf_op jit(solution)/shard_map/ppermute | solution.py:302
  11.6 0.0 collective-permute-done.3.refs_3_
  11.6 0.6 %collective-permute-start.4 = (f32[1,72,128]{2,1,0:T(8,128)S(1)}, f32[1,72,128]{2,1,0:T(8,128)S(1)}, u32[]{:S(2)}, u32[]{:S(2)}) collective-permute-start(f32[1,72,128]{2,1,0:T(8,128)S(1)} %collective-permute-done.3.refs_3_), channel_id=1, source_target_pairs={{0,1},{1,0},{2,3},{3,2},{4,5},{5,4},{6,7},{7,6},{8,9},{9,8},{10,11... | collective-permute-start | bytes 110600 | tf_op jit(solution)/shard_map/ppermute | solution.py:355
  12.2 0.0 collective-permute-done.1.refs_1_
  12.2 0.1 collective-permute-start.2
  12.4 0.1 pad.3.clone
  12.4 0.7 %collective-permute-done.4.refs_4_ = f32[1,72,128]{2,1,0:T(8,128)S(1)} collective-permute-done((f32[1,72,128]{2,1,0:T(8,128)S(1)}, f32[1,72,128]{2,1,0:T(8,128)S(1)}, u32[]{:S(2)}, u32[]{:S(2)}) %collective-permute-start.4) | collective-permute-done | bytes 36896 | tf_op jit(solution)/shard_map/ppermute | solution.py:355
  13.1 0.4 %collective-permute-done.2.refs_2_ = f32[2,72,128]{2,1,0:T(8,128)S(1)} collective-permute-done((f32[2,72,128]{2,1,0:T(8,128)S(1)}, f32[2,72,128]{2,1,0:T(8,128)S(1)}, u32[]{:S(2)}, u32[]{:S(2)}) %collective-permute-start.2) | collective-permute-done | bytes 73760 | tf_op jit(solution)/shard_map/ppermute | solution.py:355
  13.5 2.5 %strips0.1 = (bf16[10,256,256]{2,1,0:T(8,128)(2,1)S(1)}, f32[32,1024]{1,0:T(8,128)S(1)}, bf16[32,1024]{1,0:T(8,128)(2,1)S(1)}, bf16[32,1024]{1,0:T(8,128)(2,1)S(1)}) custom-call(f32[2,72,128]{2,1,0:T(8,128)S(1)} %pad_maximum_fusion.refs_0_, f32[2,72,128]{2,1,0:T(8,128)S(1)} %collective-permute-done.1.refs_1_, ...), custom_call_target="tpu_custom_call" | custom-call | flops 19660800 | bytes 1310720 | tf_op jit(solution)/shard_map/strips0/pallas_call | solution.py:335
  16.0 0.0 collective-permute-done.5.refs_0_.refs_5_
  16.0 0.2 collective-permute-done.6.refs_1_.refs_6_
  16.2 0.0 collective-permute-start.7
  16.2 0.5 %collective-permute-start.8 = (f32[2,72,128]{2,1,0:T(8,128)S(1)}, f32[2,72,128]{2,1,0:T(8,128)S(1)}, u32[]{:S(2)}, u32[]{:S(2)}) collective-permute-start(f32[2,72,128]{2,1,0:T(8,128)S(1)} %collective-permute-done.6.refs_1_.refs_6_), channel_id=1, source_target_pairs={{0,1},{1,0},{2,3},{3,2},{4,5},{5,4},{6,7},{7,6},{8,9},{9,8},{10,11... | collective-permute-start | bytes 221192 | tf_op jit(solution)/shard_map/ppermute | solution.py:355
  16.7 0.1 maximum_maximum_fusion.refs_9_
  16.8 2.6 %strips4.1 = (bf16[11,256,256]{2,1,0:T(8,128)(2,1)S(1)}, f32[32,1536]{1,0:T(8,128)S(1)}, bf16[32,1536]{1,0:T(8,128)(2,1)S(1)}, bf16[32,1536]{1,0:T(8,128)(2,1)S(1)}) custom-call(f32[2,72,128]{2,1,0:T(8,128)S(1)} %collective-permute-done.5.refs_0_.refs_5_, f32[2,72,128]{2,1,0:T(8,128)S(1)} %collective-permute-done.6.refs_1_.refs_6_, ...), custom_call_target="tpu_custom_call" | custom-call | flops 21626880 | bytes 1441792 | tf_op jit(solution)/shard_map/strips4/pallas_call | solution.py:335
  19.4 0.0 collective-permute-done.7.refs_7_
  19.4 0.0 collective-permute-done.8.refs_8_
  19.4 8.9 %iterate.1 = (f32[32,128]{1,0:T(8,128)}, f32[32,128]{1,0:T(8,128)}) custom-call(f32[2,72,128]{2,1,0:T(8,128)S(1)} %pad_maximum_fusion.refs_0_, f32[2,72,128]{2,1,0:T(8,128)S(1)} %collective-permute-done.1.refs_1_, f32[2,72,128]{2,1,0:T(8,128)S(1)} %collective-permute-done.2.refs_2_, f32[1,72,128]{2,1,0:T(8,128)S(1)} %collective-permute-done.3.refs_3_, ...), custom_call_target="tpu_custom_call" | custom-call | tf_op jit(solution)/shard_map/iterate/pallas_call | solution.py:367
  (3 shorter events, 0.0 us)
Async XLA Ops:
  1.4 6.1 %collective-permute-start = (f32[1,72,128]{2,1,0:T(8,128)S(1)}, f32[1,72,128]{2,1,0:T(8,128)S(1)}, u32[]{:S(2)}, u32[]{:S(2)}) collective-permute-start(f32[1,72,128]{2,1,0:T(8,128)S(1)} %bitcast.7), channel_id=1, source_target_pairs={{0,1},{1,0},{2,3},{3,2},{4,5},{5,4},{6,7},{7,6},{8,9},{9,8},{10,11... | collective-permute-start | bytes 110600 | tf_op jit(solution)/shard_map/ppermute | solution.py:305
  2.0 9.7 %collective-permute-start.3 = (f32[1,72,128]{2,1,0:T(8,128)S(1)}, f32[1,72,128]{2,1,0:T(8,128)S(1)}, u32[]{:S(2)}, u32[]{:S(2)}) collective-permute-start(f32[1,72,128]{2,1,0:T(8,128)S(1)} %bitcast.8), channel_id=1, source_target_pairs={{0,14},{1,15},{2,12},{3,13},{4,10},{5,11},{6,8},{7,9},{8,6},{9,7},... | collective-permute-start | bytes 110600 | tf_op jit(solution)/shard_map/ppermute | solution.py:302
  7.6 4.7 %collective-permute-start.1 = (f32[2,72,128]{2,1,0:T(8,128)S(1)}, f32[2,72,128]{2,1,0:T(8,128)S(1)}, u32[]{:S(2)}, u32[]{:S(2)}) collective-permute-start(f32[2,72,128]{2,1,0:T(8,128)S(1)} %pad_maximum_fusion.refs_0_), channel_id=1, source_target_pairs={{0,2},{1,5},{2,0},{3,7},{4,6},{5,1},{6,4},{7,3},{8,10},{9,13},{10,... | collective-permute-start | bytes 221192 | tf_op jit(solution)/shard_map/ppermute | solution.py:302
  9.0 7.0 %collective-permute-start.5 = (f32[2,72,128]{2,1,0:T(8,128)S(1)}, f32[2,72,128]{2,1,0:T(8,128)S(1)}, u32[]{:S(2)}, u32[]{:S(2)}) collective-permute-start(f32[2,72,128]{2,1,0:T(8,128)S(1)} %pad_maximum_fusion.refs_0_), channel_id=1, source_target_pairs={{0,6},{1,9},{2,4},{3,11},{4,2},{5,13},{6,0},{7,15},{8,14},{9,1},{1... | collective-permute-start | bytes 221192 | tf_op jit(solution)/shard_map/ppermute | solution.py:302
  9.5 6.7 %collective-permute-start.6 = (f32[2,72,128]{2,1,0:T(8,128)S(1)}, f32[2,72,128]{2,1,0:T(8,128)S(1)}, u32[]{:S(2)}, u32[]{:S(2)}) collective-permute-start(f32[2,72,128]{2,1,0:T(8,128)S(1)} %pad_maximum_fusion.refs_0_), channel_id=1, source_target_pairs={{0,10},{1,13},{2,8},{3,15},{4,14},{5,9},{6,12},{7,11},{8,2},{9,5},... | collective-permute-start | bytes 221192 | tf_op jit(solution)/shard_map/ppermute | solution.py:302
  11.6 1.5 %collective-permute-start.4 = (f32[1,72,128]{2,1,0:T(8,128)S(1)}, f32[1,72,128]{2,1,0:T(8,128)S(1)}, u32[]{:S(2)}, u32[]{:S(2)}) collective-permute-start(f32[1,72,128]{2,1,0:T(8,128)S(1)} %collective-permute-done.3.refs_3_), channel_id=1, source_target_pairs={{0,1},{1,0},{2,3},{3,2},{4,5},{5,4},{6,7},{7,6},{8,9},{9,8},{10,11... | collective-permute-start | bytes 110600 | tf_op jit(solution)/shard_map/ppermute | solution.py:355
  12.2 1.3 %collective-permute-start.2 = (f32[2,72,128]{2,1,0:T(8,128)S(1)}, f32[2,72,128]{2,1,0:T(8,128)S(1)}, u32[]{:S(2)}, u32[]{:S(2)}) collective-permute-start(f32[2,72,128]{2,1,0:T(8,128)S(1)} %collective-permute-done.1.refs_1_), channel_id=1, source_target_pairs={{0,1},{1,0},{2,3},{3,2},{4,5},{5,4},{6,7},{7,6},{8,9},{9,8},{10,11... | collective-permute-start | bytes 221192 | tf_op jit(solution)/shard_map/ppermute | solution.py:355
  16.2 3.2 %collective-permute-start.7 = (f32[2,72,128]{2,1,0:T(8,128)S(1)}, f32[2,72,128]{2,1,0:T(8,128)S(1)}, u32[]{:S(2)}, u32[]{:S(2)}) collective-permute-start(f32[2,72,128]{2,1,0:T(8,128)S(1)} %collective-permute-done.5.refs_0_.refs_5_), channel_id=1, source_target_pairs={{0,1},{1,0},{2,3},{3,2},{4,5},{5,4},{6,7},{7,6},{8,9},{9,8},{10,11... | collective-permute-start | bytes 221192 | tf_op jit(solution)/shard_map/ppermute | solution.py:355
  16.2 3.2 %collective-permute-start.8 = (f32[2,72,128]{2,1,0:T(8,128)S(1)}, f32[2,72,128]{2,1,0:T(8,128)S(1)}, u32[]{:S(2)}, u32[]{:S(2)}) collective-permute-start(f32[2,72,128]{2,1,0:T(8,128)S(1)} %collective-permute-done.6.refs_1_.refs_6_), channel_id=1, source_target_pairs={{0,1},{1,0},{2,3},{3,2},{4,5},{5,4},{6,7},{7,6},{8,9},{9,8},{10,11... | collective-permute-start | bytes 221192 | tf_op jit(solution)/shard_map/ppermute | solution.py:355

commit v6 on v5

--- a/solution.py
+++ b/solution.py
@@ -65,13 +65,16 @@
     return high, mid, low
 
 
-def pack_kernel(points, precond, density, incident, out, head, sems):
+def pack_kernel(points, precond, density, incident, receivers, out, picked, head, sems):
     columns = density.shape[0]
+    chip = lax.axis_index("tgt") * lax.axis_size("src") + lax.axis_index("src")
+    place = chip * lax.axis_size("sub") + lax.axis_index("sub")
     moves = [
         (points, head.at[0]),
         (precond, head.at[1, pl.ds(0, 1)]),
         (density, out.at[pl.ds(8, columns)]),
         (incident, out.at[pl.ds(8 + columns, columns)]),
+        (receivers.at[pl.ds(place, 1)], picked),
     ]
     copies = [pltpu.make_async_copy(src, dst, sems.at[k]) for k, (src, dst) in enumerate(moves)]
     for copy in copies:
@@ -81,8 +84,8 @@
     out[0:3, :] = head[0]
     out[3:4, :] = head[1, 0:1]
     out[4:8, :] = jnp.zeros((4, out.shape[1]), jnp.float32)
-    copies[2].wait()
-    copies[3].wait()
+    for copy in copies[2:]:
+        copy.wait()
 
 
 def lanes(data, start, count):
@@ -285,15 +288,20 @@
     columns, width = density.shape
     names = ("tgt", "src", "sub")
     vmem = pl.BlockSpec(memory_space=pltpu.VMEM)
-    payload = pl.pallas_call(
+    rows = receivers.shape[0] // (chips * count_sub)
+    inputs = (points, precond[None, :], density, incident, receivers.reshape(-1, rows))
+    payload, picked = pl.pallas_call(
         pack_kernel,
-        out_shape=jax.ShapeDtypeStruct((8 + 2 * columns, width), jnp.float32),
-        in_specs=[pl.BlockSpec(memory_space=pltpu.HBM)] * 4,
-        out_specs=vmem,
-        scratch_shapes=[pltpu.VMEM((2, 3, width), jnp.float32), pltpu.SemaphoreType.DMA((4,))],
+        out_shape=(
+            jax.ShapeDtypeStruct((8 + 2 * columns, width), jnp.float32),
+            jax.ShapeDtypeStruct((1, rows), jnp.int32),
+        ),
+        in_specs=[pl.BlockSpec(memory_space=pltpu.HBM)] * len(inputs),
+        out_specs=(vmem, vmem),
+        scratch_shapes=[pltpu.VMEM((2, 3, width), jnp.float32), pltpu.SemaphoreType.DMA((len(inputs),))],
         compiler_params=pltpu.CompilerParams(vmem_limit_bytes=4 * 2**20),
         name="pack",
-    )(*(pltpu.with_memory_space_constraint(a, pltpu.HBM) for a in (points, precond[None, :], density, incident)))
+    )(*(pltpu.with_memory_space_constraint(array, pltpu.HBM) for array in inputs))
     swap = [(0, 1), (1, 0)]
     payload = payload[None]
 
@@ -305,9 +313,7 @@
     own = jnp.concatenate([payload, lax.ppermute(payload, "sub", swap)], axis=0)
     near = [fetch(own, (k, k + 1)) for k in range(1, chips - 1, 2)]
 
-    place = (lax.axis_index("tgt") * count_src + lax.axis_index("src")) * count_sub + lax.axis_index("sub")
-    rows = receivers.shape[0] // (chips * count_sub)
-    toward = receiver_directions(lax.dynamic_slice_in_dim(receivers, place * rows, rows, 0))
+    toward = receiver_directions(picked[0])
     toward = jnp.concatenate([toward, jnp.zeros((5, rows), jnp.float32)], axis=0)
 
     blocks = chips

time: 28.6 us -> 28.1 us (0.983)
  other arithmetic: 0.93 us -> 0.18 us
  waiting for transfers between devices: 1.3 us -> 1.66 us
    another operation x2 -> x0, other arithmetic: 0.86 us -> none  [receiver_directions(): jnp.stack([radial * jnp.cos(azimuth), radial * jnp.sin(azimuth), height])]
    ppermute x4, waiting for transfers between devices: 0.22 us -> 0.52 us  [fetch(): return lax.ppermute(array, names, pairs)]
  transfers between devices with their start and end apart: 9 -> 9, of which waited for: 3 -> 3; matrix products, arithmetic and copies ran while one was open for 4% -> 1% of each run, Pallas kernels for 18% -> 18%
where the time goes in v6:
time: 28.1 us; the launch traced here: 27.9 us
  Pallas kernels  14.8 us (53%)
  starting transfers between devices  10.5 us (37%)
  waiting for transfers between devices  1.66 us (6%)
  between operations  0.68 us (2%)
    pallas_call x1, Pallas kernels, replicated_shards(): pl.pallas_call(functools.partial(iterate_kernel, pieces, new, blocks, col...  8.87 us
    ppermute x4, starting transfers between devices, fetch(): return lax.ppermute(array, names, pairs)  8.82 us
    pallas_call x2, Pallas kernels, strips(): pl.pallas_call(functools.partial(strips_kernel, len(data), old, new, colu...  5.08 us
    ppermute x4, starting transfers between devices, swapped(): return lax.ppermute(array, 'sub', swap)  1.2 us
    ppermute x4, waiting for transfers between devices, swapped(): return lax.ppermute(array, 'sub', swap)  1.14 us
    pallas_call x1, Pallas kernels, replicated_shards(): pl.pallas_call(pack_kernel, out_shape=(jax.ShapeDtypeStruct((8 + 2 * colu...  0.81 us
  transfers between devices with their start and end apart: 9, of which 3 were waited for; matrix products, arithmetic and copies ran while one was open for 1% of the time, Pallas kernels for 18%

profile of v6, /device:TPU:0, one launch (start us, length us, event | category | flops | bytes accessed | tf_op | source)
XLA Modules:
  0.0 27.9 jit_solution(16387522836510769094)
XLA Ops:
  0.6 0.8 %pack.1 = (f32[72,128]{1,0:T(8,128)S(1)}, s32[1,128]{1,0:T(1,128)S(1)}) custom-call(f32[3,128]{1,0:T(4,128)} %points.1, f32[1,128]{1,0:T(1,128)} %bitcast.7, f32[32,128]{1,0:T(8,128)} %density.1, f32[32,128]{1,0:T(8,128)} %incident.1, s32[16,128]{1,0:T(8,128)} %bitcast.6), custom_call_target="tpu_custom_call" | custom-call | tf_op jit(solution)/shard_map/pack/pallas_call | solution.py:293
  1.5 0.5 %collective-permute-start = (f32[1,72,128]{2,1,0:T(8,128)S(1)}, f32[1,72,128]{2,1,0:T(8,128)S(1)}, u32[]{:S(2)}, u32[]{:S(2)}) collective-permute-start(f32[1,72,128]{2,1,0:T(8,128)S(1)} %bitcast.3), channel_id=1, source_target_pairs={{0,1},{1,0},{2,3},{3,2},{4,5},{5,4},{6,7},{7,6},{8,9},{9,8},{10,11... | collective-permute-start | bytes 110600 | tf_op jit(solution)/shard_map/ppermute | solution.py:313
  2.0 5.6 %collective-permute-start.3 = (f32[1,72,128]{2,1,0:T(8,128)S(1)}, f32[1,72,128]{2,1,0:T(8,128)S(1)}, u32[]{:S(2)}, u32[]{:S(2)}) collective-permute-start(f32[1,72,128]{2,1,0:T(8,128)S(1)} %bitcast.4), channel_id=1, source_target_pairs={{0,14},{1,15},{2,12},{3,13},{4,10},{5,11},{6,8},{7,9},{8,6},{9,7},... | collective-permute-start | bytes 110600 | tf_op jit(solution)/shard_map/ppermute | solution.py:310
  7.6 0.0 collective-permute-done
  7.6 0.6 %collective-permute-start.1 = (f32[2,72,128]{2,1,0:T(8,128)S(1)}, f32[2,72,128]{2,1,0:T(8,128)S(1)}, u32[]{:S(2)}, u32[]{:S(2)}) collective-permute-start(f32[2,72,128]{2,1,0:T(8,128)S(1)} %pad_maximum_fusion.refs_0_), channel_id=1, source_target_pairs={{0,2},{1,5},{2,0},{3,7},{4,6},{5,1},{6,4},{7,3},{8,10},{9,13},{10,... | collective-permute-start | bytes 221192 | tf_op jit(solution)/shard_map/ppermute | solution.py:310
  8.2 0.1 cosine_multiply_fusion
  8.2 0.5 %collective-permute-start.5 = (f32[2,72,128]{2,1,0:T(8,128)S(1)}, f32[2,72,128]{2,1,0:T(8,128)S(1)}, u32[]{:S(2)}, u32[]{:S(2)}) collective-permute-start(f32[2,72,128]{2,1,0:T(8,128)S(1)} %pad_maximum_fusion.refs_0_), channel_id=1, source_target_pairs={{0,6},{1,9},{2,4},{3,11},{4,2},{5,13},{6,0},{7,15},{8,14},{9,1},{1... | collective-permute-start | bytes 221192 | tf_op jit(solution)/shard_map/ppermute | solution.py:310
  8.8 2.1 %collective-permute-start.6 = (f32[2,72,128]{2,1,0:T(8,128)S(1)}, f32[2,72,128]{2,1,0:T(8,128)S(1)}, u32[]{:S(2)}, u32[]{:S(2)}) collective-permute-start(f32[2,72,128]{2,1,0:T(8,128)S(1)} %pad_maximum_fusion.refs_0_), channel_id=1, source_target_pairs={{0,10},{1,13},{2,8},{3,15},{4,14},{5,9},{6,12},{7,11},{8,2},{9,5},... | collective-permute-start | bytes 221192 | tf_op jit(solution)/shard_map/ppermute | solution.py:310
  10.9 0.0 collective-permute-done.3.refs_3_
  10.9 0.6 %collective-permute-start.4 = (f32[1,72,128]{2,1,0:T(8,128)S(1)}, f32[1,72,128]{2,1,0:T(8,128)S(1)}, u32[]{:S(2)}, u32[]{:S(2)}) collective-permute-start(f32[1,72,128]{2,1,0:T(8,128)S(1)} %collective-permute-done.3.refs_3_), channel_id=1, source_target_pairs={{0,1},{1,0},{2,3},{3,2},{4,5},{5,4},{6,7},{7,6},{8,9},{9,8},{10,11... | collective-permute-start | bytes 110600 | tf_op jit(solution)/shard_map/ppermute | solution.py:361
  11.5 0.5 %collective-permute-done.1.refs_1_ = f32[2,72,128]{2,1,0:T(8,128)S(1)} collective-permute-done((f32[2,72,128]{2,1,0:T(8,128)S(1)}, f32[2,72,128]{2,1,0:T(8,128)S(1)}, u32[]{:S(2)}, u32[]{:S(2)}) %collective-permute-start.1) | collective-permute-done | bytes 73760 | tf_op jit(solution)/shard_map/ppermute | solution.py:310
  12.0 0.0 collective-permute-start.2
  12.1 0.1 pad.3.clone
  12.1 0.2 collective-permute-done.4.refs_4_
  12.4 0.9 %collective-permute-done.2.refs_2_ = f32[2,72,128]{2,1,0:T(8,128)S(1)} collective-permute-done((f32[2,72,128]{2,1,0:T(8,128)S(1)}, f32[2,72,128]{2,1,0:T(8,128)S(1)}, u32[]{:S(2)}, u32[]{:S(2)}) %collective-permute-start.2) | collective-permute-done | bytes 73760 | tf_op jit(solution)/shard_map/ppermute | solution.py:361
  13.3 2.5 %strips0.1 = (bf16[10,256,256]{2,1,0:T(8,128)(2,1)S(1)}, f32[32,1024]{1,0:T(8,128)S(1)}, bf16[32,1024]{1,0:T(8,128)(2,1)S(1)}, bf16[32,1024]{1,0:T(8,128)(2,1)S(1)}) custom-call(f32[2,72,128]{2,1,0:T(8,128)S(1)} %pad_maximum_fusion.refs_0_, f32[2,72,128]{2,1,0:T(8,128)S(1)} %collective-permute-done.1.refs_1_, ...), custom_call_target="tpu_custom_call" | custom-call | flops 19660800 | bytes 1310720 | tf_op jit(solution)/shard_map/strips0/pallas_call | solution.py:341
  15.7 0.0 collective-permute-done.5.refs_0_.refs_5_
  15.7 0.0 collective-permute-done.6.refs_1_.refs_6_
  15.8 0.2 collective-permute-start.7
  16.0 0.4 %collective-permute-start.8 = (f32[2,72,128]{2,1,0:T(8,128)S(1)}, f32[2,72,128]{2,1,0:T(8,128)S(1)}, u32[]{:S(2)}, u32[]{:S(2)}) collective-permute-start(f32[2,72,128]{2,1,0:T(8,128)S(1)} %collective-permute-done.6.refs_1_.refs_6_), channel_id=1, source_target_pairs={{0,1},{1,0},{2,3},{3,2},{4,5},{5,4},{6,7},{7,6},{8,9},{9,8},{10,11... | collective-permute-start | bytes 221192 | tf_op jit(solution)/shard_map/ppermute | solution.py:361
  16.3 0.1 maximum_maximum_fusion.refs_9_
  16.4 2.6 %strips4.1 = (bf16[11,256,256]{2,1,0:T(8,128)(2,1)S(1)}, f32[32,1536]{1,0:T(8,128)S(1)}, bf16[32,1536]{1,0:T(8,128)(2,1)S(1)}, bf16[32,1536]{1,0:T(8,128)(2,1)S(1)}) custom-call(f32[2,72,128]{2,1,0:T(8,128)S(1)} %collective-permute-done.5.refs_0_.refs_5_, f32[2,72,128]{2,1,0:T(8,128)S(1)} %collective-permute-done.6.refs_1_.refs_6_, ...), custom_call_target="tpu_custom_call" | custom-call | flops 21626880 | bytes 1441792 | tf_op jit(solution)/shard_map/strips4/pallas_call | solution.py:341
  19.0 0.0 collective-permute-done.7.refs_7_
  19.0 0.0 collective-permute-done.8.refs_8_
  19.0 8.9 %iterate.1 = (f32[32,128]{1,0:T(8,128)}, f32[32,128]{1,0:T(8,128)}) custom-call(f32[2,72,128]{2,1,0:T(8,128)S(1)} %pad_maximum_fusion.refs_0_, f32[2,72,128]{2,1,0:T(8,128)S(1)} %collective-permute-done.1.refs_1_, f32[2,72,128]{2,1,0:T(8,128)S(1)} %collective-permute-done.2.refs_2_, f32[1,72,128]{2,1,0:T(8,128)S(1)} %collective-permute-done.3.refs_3_, ...), custom_call_target="tpu_custom_call" | custom-call | tf_op jit(solution)/shard_map/iterate/pallas_call | solution.py:373
  (3 shorter events, 0.0 us)
Async XLA Ops:
  1.5 6.1 %collective-permute-start = (f32[1,72,128]{2,1,0:T(8,128)S(1)}, f32[1,72,128]{2,1,0:T(8,128)S(1)}, u32[]{:S(2)}, u32[]{:S(2)}) collective-permute-start(f32[1,72,128]{2,1,0:T(8,128)S(1)} %bitcast.3), channel_id=1, source_target_pairs={{0,1},{1,0},{2,3},{3,2},{4,5},{5,4},{6,7},{7,6},{8,9},{9,8},{10,11... | collective-permute-start | bytes 110600 | tf_op jit(solution)/shard_map/ppermute | solution.py:313
  2.0 8.9 %collective-permute-start.3 = (f32[1,72,128]{2,1,0:T(8,128)S(1)}, f32[1,72,128]{2,1,0:T(8,128)S(1)}, u32[]{:S(2)}, u32[]{:S(2)}) collective-permute-start(f32[1,72,128]{2,1,0:T(8,128)S(1)} %bitcast.4), channel_id=1, source_target_pairs={{0,14},{1,15},{2,12},{3,13},{4,10},{5,11},{6,8},{7,9},{8,6},{9,7},... | collective-permute-start | bytes 110600 | tf_op jit(solution)/shard_map/ppermute | solution.py:310
  7.6 4.4 %collective-permute-start.1 = (f32[2,72,128]{2,1,0:T(8,128)S(1)}, f32[2,72,128]{2,1,0:T(8,128)S(1)}, u32[]{:S(2)}, u32[]{:S(2)}) collective-permute-start(f32[2,72,128]{2,1,0:T(8,128)S(1)} %pad_maximum_fusion.refs_0_), channel_id=1, source_target_pairs={{0,2},{1,5},{2,0},{3,7},{4,6},{5,1},{6,4},{7,3},{8,10},{9,13},{10,... | collective-permute-start | bytes 221192 | tf_op jit(solution)/shard_map/ppermute | solution.py:310
  8.2 7.5 %collective-permute-start.5 = (f32[2,72,128]{2,1,0:T(8,128)S(1)}, f32[2,72,128]{2,1,0:T(8,128)S(1)}, u32[]{:S(2)}, u32[]{:S(2)}) collective-permute-start(f32[2,72,128]{2,1,0:T(8,128)S(1)} %pad_maximum_fusion.refs_0_), channel_id=1, source_target_pairs={{0,6},{1,9},{2,4},{3,11},{4,2},{5,13},{6,0},{7,15},{8,14},{9,1},{1... | collective-permute-start | bytes 221192 | tf_op jit(solution)/shard_map/ppermute | solution.py:310
  8.8 7.0 %collective-permute-start.6 = (f32[2,72,128]{2,1,0:T(8,128)S(1)}, f32[2,72,128]{2,1,0:T(8,128)S(1)}, u32[]{:S(2)}, u32[]{:S(2)}) collective-permute-start(f32[2,72,128]{2,1,0:T(8,128)S(1)} %pad_maximum_fusion.refs_0_), channel_id=1, source_target_pairs={{0,10},{1,13},{2,8},{3,15},{4,14},{5,9},{6,12},{7,11},{8,2},{9,5},... | collective-permute-start | bytes 221192 | tf_op jit(solution)/shard_map/ppermute | solution.py:310
  10.9 1.5 %collective-permute-start.4 = (f32[1,72,128]{2,1,0:T(8,128)S(1)}, f32[1,72,128]{2,1,0:T(8,128)S(1)}, u32[]{:S(2)}, u32[]{:S(2)}) collective-permute-start(f32[1,72,128]{2,1,0:T(8,128)S(1)} %collective-permute-done.3.refs_3_), channel_id=1, source_target_pairs={{0,1},{1,0},{2,3},{3,2},{4,5},{5,4},{6,7},{7,6},{8,9},{9,8},{10,11... | collective-permute-start | bytes 110600 | tf_op jit(solution)/shard_map/ppermute | solution.py:361
  12.0 1.3 %collective-permute-start.2 = (f32[2,72,128]{2,1,0:T(8,128)S(1)}, f32[2,72,128]{2,1,0:T(8,128)S(1)}, u32[]{:S(2)}, u32[]{:S(2)}) collective-permute-start(f32[2,72,128]{2,1,0:T(8,128)S(1)} %collective-permute-done.1.refs_1_), channel_id=1, source_target_pairs={{0,1},{1,0},{2,3},{3,2},{4,5},{5,4},{6,7},{7,6},{8,9},{9,8},{10,11... | collective-permute-start | bytes 221192 | tf_op jit(solution)/shard_map/ppermute | solution.py:361
  15.8 3.3 %collective-permute-start.7 = (f32[2,72,128]{2,1,0:T(8,128)S(1)}, f32[2,72,128]{2,1,0:T(8,128)S(1)}, u32[]{:S(2)}, u32[]{:S(2)}) collective-permute-start(f32[2,72,128]{2,1,0:T(8,128)S(1)} %collective-permute-done.5.refs_0_.refs_5_), channel_id=1, source_target_pairs={{0,1},{1,0},{2,3},{3,2},{4,5},{5,4},{6,7},{7,6},{8,9},{9,8},{10,11... | collective-permute-start | bytes 221192 | tf_op jit(solution)/shard_map/ppermute | solution.py:361
  16.0 3.0 %collective-permute-start.8 = (f32[2,72,128]{2,1,0:T(8,128)S(1)}, f32[2,72,128]{2,1,0:T(8,128)S(1)}, u32[]{:S(2)}, u32[]{:S(2)}) collective-permute-start(f32[2,72,128]{2,1,0:T(8,128)S(1)} %collective-permute-done.6.refs_1_.refs_6_), channel_id=1, source_target_pairs={{0,1},{1,0},{2,3},{3,2},{4,5},{5,4},{6,7},{7,6},{8,9},{9,8},{10,11... | collective-permute-start | bytes 221192 | tf_op jit(solution)/shard_map/ppermute | solution.py:361

commit v7 on v6

--- a/solution.py
+++ b/solution.py
@@ -127,7 +127,7 @@
     return sum(j + 1 for j in range(old, old + new))
 
 
-def build_strips(old, new, lhs, rhs, weighted, table, field, turned, even, odd):
+def build_strips(old, new, lhs, rhs, weighted, table, field, even, odd):
     count = strip_size(old, new)
     starts = [strip_size(old, k) for k in range(new)]
 
@@ -149,16 +149,20 @@
         for r in range(0, BLOCK, 32):
             table[k, r : r + 32, :] = green(source[r : r + 32, :])
 
-    def products(k, valid):
+    def products(k, valid=None):
         j, i = place(k)
-        valid = jnp.where(valid, 1.0, 0.0)
-        beside = jnp.where(old + j == i, 0.0, valid).astype(jnp.bfloat16)
-        row = block_span(j)
-        turned[row, :] += across(table[k], weighted[:, block_span(i)] * valid.astype(jnp.bfloat16))
-        field[:, block_span(i)] += down(weighted[:, block_span(old + j)] * beside, table[k])
+        beside = jnp.where(old + j == i, 0.0, 1.0)
+        above, below = weighted[:, block_span(i)], weighted[:, block_span(old + j)]
+        if valid is not None:
+            valid = jnp.where(valid, 1.0, 0.0)
+            beside = beside * valid
+            above = above * valid.astype(jnp.bfloat16)
+        field[:, block_span(old + j)] += lax.dot_general(
+            above, table[k], (((1,), (1,)), ((), ())), preferred_element_type=jnp.float32
+        )
+        field[:, block_span(i)] += down(below * beside.astype(jnp.bfloat16), table[k])
 
     field[...] = jnp.zeros_like(field)
-    turned[...] = jnp.zeros_like(turned)
     table[0] = jnp.zeros((BLOCK, BLOCK), jnp.bfloat16)
     stage = (even, odd)
     even[...] = distances(0)
@@ -170,7 +174,7 @@
             if n == 0:
                 products(jnp.maximum(k - 1, 0), k > 0)
             else:
-                products(k + n - 1, True)
+                products(k + n - 1)
             fill(k + n, stage[n % 2])
         return carry
 
@@ -179,10 +183,9 @@
         if k + 1 < count:
             stage[(n + 1) % 2][...] = distances(k + 1)
         if k:
-            products(k - 1, True)
+            products(k - 1)
         fill(k, stage[n % 2])
-    products(count - 1, True)
-    field[:, old * BLOCK :] += turned[...].T
+    products(count - 1)
 
 
 def prepare(old, data, columns, total, lhs, rhs, weighted, before):
@@ -200,9 +203,9 @@
 def strips_kernel(pieces, old, new, columns, total, *refs):
     data, refs = refs[:pieces], refs[pieces:]
     before = refs[: 2 if old else 0]
-    table, field, rhs, weighted, lhs, turned, even, odd = refs[len(before) :]
+    table, field, rhs, weighted, lhs, even, odd = refs[len(before) :]
     prepare(old, data, columns, total, lhs, rhs, weighted, before)
-    build_strips(old, new, lhs, rhs, weighted, table, field, turned, even, odd)
+    build_strips(old, new, lhs, rhs, weighted, table, field, even, odd)
 
 
 def iterate_kernel(pieces, new, blocks, columns, groups, *refs):
@@ -212,12 +215,12 @@
     tables, refs = refs[: len(groups)], refs[len(groups) :]
     fields, refs = refs[: len(groups)], refs[len(groups) :]
     density_out, far_out = refs[:2]
-    lhs, rhs, weighted, table, field, turned, even, odd, coords, plane, dens, inc = refs[2:]
+    lhs, rhs, weighted, table, field, even, odd, coords, plane, dens, inc = refs[2:]
     total = blocks * BLOCK
     width = data[0].shape[2]
     old = blocks - new
     prepare(old, rest, columns, total, lhs, rhs, weighted, before)
-    build_strips(old, new, lhs, rhs, weighted, table, field, turned, even, odd)
+    build_strips(old, new, lhs, rhs, weighted, table, field, even, odd)
 
     everything = list(data) + list(rest)
     coords[0:3, :] = lanes(everything, 0, 3) * TURNS
@@ -327,7 +330,6 @@
             ((32, (old + new) * BLOCK), bf16),
             ((columns, (old + new) * BLOCK), bf16),
             ((new * BLOCK, 32), bf16),
-            ((new * BLOCK, columns), f32),
             ((BLOCK, BLOCK), f32),
             ((BLOCK, BLOCK), f32),
         ]
@@ -378,7 +380,7 @@
         ),
         in_specs=[vmem] * (pieces + new + 3 + 2 * len(groups)),
         out_specs=(vmem, vmem),
-        scratch_shapes=[pltpu.VMEM(*shapes[k]) for k in (4, 2, 3, 0, 1, 5, 6, 7)]
+        scratch_shapes=[pltpu.VMEM(*shapes[k]) for k in (4, 2, 3, 0, 1, 5, 6)]
         + [
             pltpu.VMEM((8, total), f32),
             pltpu.VMEM((rows, total), bf16),

time: 28.1 us -> 27.6 us (0.982)
  Pallas kernels: 14.8 us -> 14.3 us
    pallas_call x2, Pallas kernels: 5.08 us -> 4.79 us  [strips(): pl.pallas_call(functools.partial(strips_kernel, len(data), old, new, colu...]
  transfers between devices with their start and end apart: 9 -> 9, of which waited for: 3 -> 3; matrix products, arithmetic and copies ran while one was open for 1% -> 1% of each run, Pallas kernels for 18% -> 17%
where the time goes in v7:
time: 27.6 us; the launch traced here: 27.4 us
  Pallas kernels  14.3 us (52%)
  starting transfers between devices  10.5 us (38%)
  waiting for transfers between devices  1.66 us (6%)
  between operations  0.71 us (3%)
    ppermute x4, starting transfers between devices, fetch(): return lax.ppermute(array, names, pairs)  8.82 us
    pallas_call x1, Pallas kernels, replicated_shards(): pl.pallas_call(functools.partial(iterate_kernel, pieces, new, blocks, col...  8.67 us
    pallas_call x2, Pallas kernels, strips(): pl.pallas_call(functools.partial(strips_kernel, len(data), old, new, colu...  4.79 us
    ppermute x4, starting transfers between devices, swapped(): return lax.ppermute(array, 'sub', swap)  1.2 us
    ppermute x4, waiting for transfers between devices, swapped(): return lax.ppermute(array, 'sub', swap)  1.14 us
    pallas_call x1, Pallas kernels, replicated_shards(): pl.pallas_call(pack_kernel, out_shape=(jax.ShapeDtypeStruct((8 + 2 * colu...  0.81 us
  transfers between devices with their start and end apart: 9, of which 3 were waited for; matrix products, arithmetic and copies ran while one was open for 1% of the time, Pallas kernels for 17%

profile of v7, /device:TPU:0, one launch (start us, length us, event | category | flops | bytes accessed | tf_op | source)
XLA Modules:
  0.0 27.4 jit_solution(16044372703426362971)
XLA Ops:
  0.6 0.8 %pack.1 = (f32[72,128]{1,0:T(8,128)S(1)}, s32[1,128]{1,0:T(1,128)S(1)}) custom-call(f32[3,128]{1,0:T(4,128)} %points.1, f32[1,128]{1,0:T(1,128)} %bitcast.7, f32[32,128]{1,0:T(8,128)} %density.1, f32[32,128]{1,0:T(8,128)} %incident.1, s32[16,128]{1,0:T(8,128)} %bitcast.6), custom_call_target="tpu_custom_call" | custom-call | tf_op jit(solution)/shard_map/pack/pallas_call | solution.py:296
  1.5 0.5 %collective-permute-start = (f32[1,72,128]{2,1,0:T(8,128)S(1)}, f32[1,72,128]{2,1,0:T(8,128)S(1)}, u32[]{:S(2)}, u32[]{:S(2)}) collective-permute-start(f32[1,72,128]{2,1,0:T(8,128)S(1)} %bitcast.3), channel_id=1, source_target_pairs={{0,1},{1,0},{2,3},{3,2},{4,5},{5,4},{6,7},{7,6},{8,9},{9,8},{10,11... | collective-permute-start | bytes 110600 | tf_op jit(solution)/shard_map/ppermute | solution.py:316
  2.0 5.6 %collective-permute-start.3 = (f32[1,72,128]{2,1,0:T(8,128)S(1)}, f32[1,72,128]{2,1,0:T(8,128)S(1)}, u32[]{:S(2)}, u32[]{:S(2)}) collective-permute-start(f32[1,72,128]{2,1,0:T(8,128)S(1)} %bitcast.4), channel_id=1, source_target_pairs={{0,14},{1,15},{2,12},{3,13},{4,10},{5,11},{6,8},{7,9},{8,6},{9,7},... | collective-permute-start | bytes 110600 | tf_op jit(solution)/shard_map/ppermute | solution.py:313
  7.6 0.0 collective-permute-done
  7.6 0.6 %collective-permute-start.1 = (f32[2,72,128]{2,1,0:T(8,128)S(1)}, f32[2,72,128]{2,1,0:T(8,128)S(1)}, u32[]{:S(2)}, u32[]{:S(2)}) collective-permute-start(f32[2,72,128]{2,1,0:T(8,128)S(1)} %pad_maximum_fusion.refs_0_), channel_id=1, source_target_pairs={{0,2},{1,5},{2,0},{3,7},{4,6},{5,1},{6,4},{7,3},{8,10},{9,13},{10,... | collective-permute-start | bytes 221192 | tf_op jit(solution)/shard_map/ppermute | solution.py:313
  8.2 0.1 cosine_multiply_fusion
  8.2 0.5 %collective-permute-start.5 = (f32[2,72,128]{2,1,0:T(8,128)S(1)}, f32[2,72,128]{2,1,0:T(8,128)S(1)}, u32[]{:S(2)}, u32[]{:S(2)}) collective-permute-start(f32[2,72,128]{2,1,0:T(8,128)S(1)} %pad_maximum_fusion.refs_0_), channel_id=1, source_target_pairs={{0,6},{1,9},{2,4},{3,11},{4,2},{5,13},{6,0},{7,15},{8,14},{9,1},{1... | collective-permute-start | bytes 221192 | tf_op jit(solution)/shard_map/ppermute | solution.py:313
  8.8 2.1 %collective-permute-start.6 = (f32[2,72,128]{2,1,0:T(8,128)S(1)}, f32[2,72,128]{2,1,0:T(8,128)S(1)}, u32[]{:S(2)}, u32[]{:S(2)}) collective-permute-start(f32[2,72,128]{2,1,0:T(8,128)S(1)} %pad_maximum_fusion.refs_0_), channel_id=1, source_target_pairs={{0,10},{1,13},{2,8},{3,15},{4,14},{5,9},{6,12},{7,11},{8,2},{9,5},... | collective-permute-start | bytes 221192 | tf_op jit(solution)/shard_map/ppermute | solution.py:313
  10.9 0.0 collective-permute-done.3.refs_3_
  10.9 0.6 %collective-permute-start.4 = (f32[1,72,128]{2,1,0:T(8,128)S(1)}, f32[1,72,128]{2,1,0:T(8,128)S(1)}, u32[]{:S(2)}, u32[]{:S(2)}) collective-permute-start(f32[1,72,128]{2,1,0:T(8,128)S(1)} %collective-permute-done.3.refs_3_), channel_id=1, source_target_pairs={{0,1},{1,0},{2,3},{3,2},{4,5},{5,4},{6,7},{7,6},{8,9},{9,8},{10,11... | collective-permute-start | bytes 110600 | tf_op jit(solution)/shard_map/ppermute | solution.py:363
  11.5 0.5 %collective-permute-done.1.refs_1_ = f32[2,72,128]{2,1,0:T(8,128)S(1)} collective-permute-done((f32[2,72,128]{2,1,0:T(8,128)S(1)}, f32[2,72,128]{2,1,0:T(8,128)S(1)}, u32[]{:S(2)}, u32[]{:S(2)}) %collective-permute-start.1) | collective-permute-done | bytes 73760 | tf_op jit(solution)/shard_map/ppermute | solution.py:313
  12.0 0.0 collective-permute-start.2
  12.1 0.1 pad.3.clone
  12.1 0.2 collective-permute-done.4.refs_4_
  12.4 0.9 %collective-permute-done.2.refs_2_ = f32[2,72,128]{2,1,0:T(8,128)S(1)} collective-permute-done((f32[2,72,128]{2,1,0:T(8,128)S(1)}, f32[2,72,128]{2,1,0:T(8,128)S(1)}, u32[]{:S(2)}, u32[]{:S(2)}) %collective-permute-start.2) | collective-permute-done | bytes 73760 | tf_op jit(solution)/shard_map/ppermute | solution.py:363
  13.3 2.3 %strips0.1 = (bf16[10,256,256]{2,1,0:T(8,128)(2,1)S(1)}, f32[32,1024]{1,0:T(8,128)S(1)}, bf16[32,1024]{1,0:T(8,128)(2,1)S(1)}, bf16[32,1024]{1,0:T(8,128)(2,1)S(1)}) custom-call(f32[2,72,128]{2,1,0:T(8,128)S(1)} %pad_maximum_fusion.refs_0_, f32[2,72,128]{2,1,0:T(8,128)S(1)} %collective-permute-done.1.refs_1_, ...), custom_call_target="tpu_custom_call" | custom-call | flops 19660800 | bytes 1310720 | tf_op jit(solution)/shard_map/strips0/pallas_call | solution.py:343
  15.6 0.0 collective-permute-done.5.refs_0_.refs_5_
  15.6 0.0 collective-permute-done.6.refs_1_.refs_6_
  15.6 0.2 collective-permute-start.7
  15.8 0.4 %collective-permute-start.8 = (f32[2,72,128]{2,1,0:T(8,128)S(1)}, f32[2,72,128]{2,1,0:T(8,128)S(1)}, u32[]{:S(2)}, u32[]{:S(2)}) collective-permute-start(f32[2,72,128]{2,1,0:T(8,128)S(1)} %collective-permute-done.6.refs_1_.refs_6_), channel_id=1, source_target_pairs={{0,1},{1,0},{2,3},{3,2},{4,5},{5,4},{6,7},{7,6},{8,9},{9,8},{10,11... | collective-permute-start | bytes 221192 | tf_op jit(solution)/shard_map/ppermute | solution.py:363
  16.2 0.1 maximum_maximum_fusion.refs_9_
  16.3 2.5 %strips4.1 = (bf16[11,256,256]{2,1,0:T(8,128)(2,1)S(1)}, f32[32,1536]{1,0:T(8,128)S(1)}, bf16[32,1536]{1,0:T(8,128)(2,1)S(1)}, bf16[32,1536]{1,0:T(8,128)(2,1)S(1)}) custom-call(f32[2,72,128]{2,1,0:T(8,128)S(1)} %collective-permute-done.5.refs_0_.refs_5_, f32[2,72,128]{2,1,0:T(8,128)S(1)} %collective-permute-done.6.refs_1_.refs_6_, ...), custom_call_target="tpu_custom_call" | custom-call | flops 21626880 | bytes 1441792 | tf_op jit(solution)/shard_map/strips4/pallas_call | solution.py:343
  18.8 0.0 collective-permute-done.7.refs_7_
  18.8 0.0 collective-permute-done.8.refs_8_
  18.8 8.7 %iterate.1 = (f32[32,128]{1,0:T(8,128)}, f32[32,128]{1,0:T(8,128)}) custom-call(f32[2,72,128]{2,1,0:T(8,128)S(1)} %pad_maximum_fusion.refs_0_, f32[2,72,128]{2,1,0:T(8,128)S(1)} %collective-permute-done.1.refs_1_, f32[2,72,128]{2,1,0:T(8,128)S(1)} %collective-permute-done.2.refs_2_, f32[1,72,128]{2,1,0:T(8,128)S(1)} %collective-permute-done.3.refs_3_, ...), custom_call_target="tpu_custom_call" | custom-call | tf_op jit(solution)/shard_map/iterate/pallas_call | solution.py:375
  (3 shorter events, 0.0 us)
Async XLA Ops:
  1.5 6.1 %collective-permute-start = (f32[1,72,128]{2,1,0:T(8,128)S(1)}, f32[1,72,128]{2,1,0:T(8,128)S(1)}, u32[]{:S(2)}, u32[]{:S(2)}) collective-permute-start(f32[1,72,128]{2,1,0:T(8,128)S(1)} %bitcast.3), channel_id=1, source_target_pairs={{0,1},{1,0},{2,3},{3,2},{4,5},{5,4},{6,7},{7,6},{8,9},{9,8},{10,11... | collective-permute-start | bytes 110600 | tf_op jit(solution)/shard_map/ppermute | solution.py:316
  2.0 8.9 %collective-permute-start.3 = (f32[1,72,128]{2,1,0:T(8,128)S(1)}, f32[1,72,128]{2,1,0:T(8,128)S(1)}, u32[]{:S(2)}, u32[]{:S(2)}) collective-permute-start(f32[1,72,128]{2,1,0:T(8,128)S(1)} %bitcast.4), channel_id=1, source_target_pairs={{0,14},{1,15},{2,12},{3,13},{4,10},{5,11},{6,8},{7,9},{8,6},{9,7},... | collective-permute-start | bytes 110600 | tf_op jit(solution)/shard_map/ppermute | solution.py:313
  7.6 4.4 %collective-permute-start.1 = (f32[2,72,128]{2,1,0:T(8,128)S(1)}, f32[2,72,128]{2,1,0:T(8,128)S(1)}, u32[]{:S(2)}, u32[]{:S(2)}) collective-permute-start(f32[2,72,128]{2,1,0:T(8,128)S(1)} %pad_maximum_fusion.refs_0_), channel_id=1, source_target_pairs={{0,2},{1,5},{2,0},{3,7},{4,6},{5,1},{6,4},{7,3},{8,10},{9,13},{10,... | collective-permute-start | bytes 221192 | tf_op jit(solution)/shard_map/ppermute | solution.py:313
  8.2 7.4 %collective-permute-start.5 = (f32[2,72,128]{2,1,0:T(8,128)S(1)}, f32[2,72,128]{2,1,0:T(8,128)S(1)}, u32[]{:S(2)}, u32[]{:S(2)}) collective-permute-start(f32[2,72,128]{2,1,0:T(8,128)S(1)} %pad_maximum_fusion.refs_0_), channel_id=1, source_target_pairs={{0,6},{1,9},{2,4},{3,11},{4,2},{5,13},{6,0},{7,15},{8,14},{9,1},{1... | collective-permute-start | bytes 221192 | tf_op jit(solution)/shard_map/ppermute | solution.py:313
  8.8 6.8 %collective-permute-start.6 = (f32[2,72,128]{2,1,0:T(8,128)S(1)}, f32[2,72,128]{2,1,0:T(8,128)S(1)}, u32[]{:S(2)}, u32[]{:S(2)}) collective-permute-start(f32[2,72,128]{2,1,0:T(8,128)S(1)} %pad_maximum_fusion.refs_0_), channel_id=1, source_target_pairs={{0,10},{1,13},{2,8},{3,15},{4,14},{5,9},{6,12},{7,11},{8,2},{9,5},... | collective-permute-start | bytes 221192 | tf_op jit(solution)/shard_map/ppermute | solution.py:313
  10.9 1.5 %collective-permute-start.4 = (f32[1,72,128]{2,1,0:T(8,128)S(1)}, f32[1,72,128]{2,1,0:T(8,128)S(1)}, u32[]{:S(2)}, u32[]{:S(2)}) collective-permute-start(f32[1,72,128]{2,1,0:T(8,128)S(1)} %collective-permute-done.3.refs_3_), channel_id=1, source_target_pairs={{0,1},{1,0},{2,3},{3,2},{4,5},{5,4},{6,7},{7,6},{8,9},{9,8},{10,11... | collective-permute-start | bytes 110600 | tf_op jit(solution)/shard_map/ppermute | solution.py:363
  12.0 1.3 %collective-permute-start.2 = (f32[2,72,128]{2,1,0:T(8,128)S(1)}, f32[2,72,128]{2,1,0:T(8,128)S(1)}, u32[]{:S(2)}, u32[]{:S(2)}) collective-permute-start(f32[2,72,128]{2,1,0:T(8,128)S(1)} %collective-permute-done.1.refs_1_), channel_id=1, source_target_pairs={{0,1},{1,0},{2,3},{3,2},{4,5},{5,4},{6,7},{7,6},{8,9},{9,8},{10,11... | collective-permute-start | bytes 221192 | tf_op jit(solution)/shard_map/ppermute | solution.py:363
  15.6 3.1 %collective-permute-start.7 = (f32[2,72,128]{2,1,0:T(8,128)S(1)}, f32[2,72,128]{2,1,0:T(8,128)S(1)}, u32[]{:S(2)}, u32[]{:S(2)}) collective-permute-start(f32[2,72,128]{2,1,0:T(8,128)S(1)} %collective-permute-done.5.refs_0_.refs_5_), channel_id=1, source_target_pairs={{0,1},{1,0},{2,3},{3,2},{4,5},{5,4},{6,7},{7,6},{8,9},{9,8},{10,11... | collective-permute-start | bytes 221192 | tf_op jit(solution)/shard_map/ppermute | solution.py:363
  15.8 2.9 %collective-permute-start.8 = (f32[2,72,128]{2,1,0:T(8,128)S(1)}, f32[2,72,128]{2,1,0:T(8,128)S(1)}, u32[]{:S(2)}, u32[]{:S(2)}) collective-permute-start(f32[2,72,128]{2,1,0:T(8,128)S(1)} %collective-permute-done.6.refs_1_.refs_6_), channel_id=1, source_target_pairs={{0,1},{1,0},{2,3},{3,2},{4,5},{5,4},{6,7},{7,6},{8,9},{9,8},{10,11... | collective-permute-start | bytes 221192 | tf_op jit(solution)/shard_map/ppermute | solution.py:363

commit v8 on v7

--- a/solution.py
+++ b/solution.py
@@ -19,7 +19,7 @@
 TURNS = WAVENUMBER / (2.0 * math.pi)
 SMOOTH_TURNS = (SMOOTHING * TURNS) ** 2
 BLOCK = 256
-UNROLL = 4
+UNROLL = 8
 TABLE_LIMIT = 8 * 2**20
 VMEM_LIMIT = 24 * 2**20
 
@@ -280,7 +280,7 @@
 
     lax.fori_loop(0, steps, iterate, 0)
     density_out[...] = dens[:, 0:width]
-    far_out[...] = across(plane[...], rounded()).T
+    far_out[...] = across(rounded(), plane[...])
 
 
 def replicated_shards(points, density, incident, precond, receivers):

time: 27.6 us -> 27.4 us (level)
  no operation moved by 1% of the time
where the time goes in v8:
time: 27.4 us; the launch traced here: 27.2 us
  Pallas kernels  14.1 us (51%)
  starting transfers between devices  10.5 us (38%)
  waiting for transfers between devices  1.68 us (6%)
  between operations  0.68 us (2%)
    ppermute x4, starting transfers between devices, fetch(): return lax.ppermute(array, names, pairs)  8.82 us
    pallas_call x1, Pallas kernels, replicated_shards(): pl.pallas_call(functools.partial(iterate_kernel, pieces, new, blocks, col...  8.54 us
    pallas_call x2, Pallas kernels, strips(): pl.pallas_call(functools.partial(strips_kernel, len(data), old, new, colu...  4.71 us
    ppermute x4, starting transfers between devices, swapped(): return lax.ppermute(array, 'sub', swap)  1.2 us
    ppermute x4, waiting for transfers between devices, swapped(): return lax.ppermute(array, 'sub', swap)  1.15 us
    pallas_call x1, Pallas kernels, replicated_shards(): pl.pallas_call(pack_kernel, out_shape=(jax.ShapeDtypeStruct((8 + 2 * colu...  0.81 us
  transfers between devices with their start and end apart: 9, of which 3 were waited for; matrix products, arithmetic and copies ran while one was open for 1% of the time, Pallas kernels for 17%

profile of v8, /device:TPU:0, one launch (start us, length us, event | category | flops | bytes accessed | tf_op | source)
XLA Modules:
  0.0 27.2 jit_solution(6399366165657831980)
XLA Ops:
  0.6 0.8 %pack.1 = (f32[72,128]{1,0:T(8,128)S(1)}, s32[1,128]{1,0:T(1,128)S(1)}) custom-call(f32[3,128]{1,0:T(4,128)} %points.1, f32[1,128]{1,0:T(1,128)} %bitcast.7, f32[32,128]{1,0:T(8,128)} %density.1, f32[32,128]{1,0:T(8,128)} %incident.1, s32[16,128]{1,0:T(8,128)} %bitcast.6), custom_call_target="tpu_custom_call" | custom-call | tf_op jit(solution)/shard_map/pack/pallas_call | solution.py:296
  1.5 0.5 %collective-permute-start = (f32[1,72,128]{2,1,0:T(8,128)S(1)}, f32[1,72,128]{2,1,0:T(8,128)S(1)}, u32[]{:S(2)}, u32[]{:S(2)}) collective-permute-start(f32[1,72,128]{2,1,0:T(8,128)S(1)} %bitcast.3), channel_id=1, source_target_pairs={{0,1},{1,0},{2,3},{3,2},{4,5},{5,4},{6,7},{7,6},{8,9},{9,8},{10,11... | collective-permute-start | bytes 110600 | tf_op jit(solution)/shard_map/ppermute | solution.py:316
  2.0 5.6 %collective-permute-start.3 = (f32[1,72,128]{2,1,0:T(8,128)S(1)}, f32[1,72,128]{2,1,0:T(8,128)S(1)}, u32[]{:S(2)}, u32[]{:S(2)}) collective-permute-start(f32[1,72,128]{2,1,0:T(8,128)S(1)} %bitcast.4), channel_id=1, source_target_pairs={{0,14},{1,15},{2,12},{3,13},{4,10},{5,11},{6,8},{7,9},{8,6},{9,7},... | collective-permute-start | bytes 110600 | tf_op jit(solution)/shard_map/ppermute | solution.py:313
  7.6 0.0 collective-permute-done
  7.6 0.6 %collective-permute-start.1 = (f32[2,72,128]{2,1,0:T(8,128)S(1)}, f32[2,72,128]{2,1,0:T(8,128)S(1)}, u32[]{:S(2)}, u32[]{:S(2)}) collective-permute-start(f32[2,72,128]{2,1,0:T(8,128)S(1)} %pad_maximum_fusion.refs_0_), channel_id=1, source_target_pairs={{0,2},{1,5},{2,0},{3,7},{4,6},{5,1},{6,4},{7,3},{8,10},{9,13},{10,... | collective-permute-start | bytes 221192 | tf_op jit(solution)/shard_map/ppermute | solution.py:313
  8.2 0.1 cosine_multiply_fusion
  8.2 0.5 %collective-permute-start.5 = (f32[2,72,128]{2,1,0:T(8,128)S(1)}, f32[2,72,128]{2,1,0:T(8,128)S(1)}, u32[]{:S(2)}, u32[]{:S(2)}) collective-permute-start(f32[2,72,128]{2,1,0:T(8,128)S(1)} %pad_maximum_fusion.refs_0_), channel_id=1, source_target_pairs={{0,6},{1,9},{2,4},{3,11},{4,2},{5,13},{6,0},{7,15},{8,14},{9,1},{1... | collective-permute-start | bytes 221192 | tf_op jit(solution)/shard_map/ppermute | solution.py:313
  8.8 2.1 %collective-permute-start.6 = (f32[2,72,128]{2,1,0:T(8,128)S(1)}, f32[2,72,128]{2,1,0:T(8,128)S(1)}, u32[]{:S(2)}, u32[]{:S(2)}) collective-permute-start(f32[2,72,128]{2,1,0:T(8,128)S(1)} %pad_maximum_fusion.refs_0_), channel_id=1, source_target_pairs={{0,10},{1,13},{2,8},{3,15},{4,14},{5,9},{6,12},{7,11},{8,2},{9,5},... | collective-permute-start | bytes 221192 | tf_op jit(solution)/shard_map/ppermute | solution.py:313
  10.9 0.0 collective-permute-done.3.refs_3_
  10.9 0.6 %collective-permute-start.4 = (f32[1,72,128]{2,1,0:T(8,128)S(1)}, f32[1,72,128]{2,1,0:T(8,128)S(1)}, u32[]{:S(2)}, u32[]{:S(2)}) collective-permute-start(f32[1,72,128]{2,1,0:T(8,128)S(1)} %collective-permute-done.3.refs_3_), channel_id=1, source_target_pairs={{0,1},{1,0},{2,3},{3,2},{4,5},{5,4},{6,7},{7,6},{8,9},{9,8},{10,11... | collective-permute-start | bytes 110600 | tf_op jit(solution)/shard_map/ppermute | solution.py:363
  11.5 0.5 %collective-permute-done.1.refs_1_ = f32[2,72,128]{2,1,0:T(8,128)S(1)} collective-permute-done((f32[2,72,128]{2,1,0:T(8,128)S(1)}, f32[2,72,128]{2,1,0:T(8,128)S(1)}, u32[]{:S(2)}, u32[]{:S(2)}) %collective-permute-start.1) | collective-permute-done | bytes 73760 | tf_op jit(solution)/shard_map/ppermute | solution.py:313
  12.0 0.0 collective-permute-start.2
  12.1 0.1 pad.3.clone
  12.1 0.2 collective-permute-done.4.refs_4_
  12.4 0.9 %collective-permute-done.2.refs_2_ = f32[2,72,128]{2,1,0:T(8,128)S(1)} collective-permute-done((f32[2,72,128]{2,1,0:T(8,128)S(1)}, f32[2,72,128]{2,1,0:T(8,128)S(1)}, u32[]{:S(2)}, u32[]{:S(2)}) %collective-permute-start.2) | collective-permute-done | bytes 73760 | tf_op jit(solution)/shard_map/ppermute | solution.py:363
  13.3 2.3 %strips0.1 = (bf16[10,256,256]{2,1,0:T(8,128)(2,1)S(1)}, f32[32,1024]{1,0:T(8,128)S(1)}, bf16[32,1024]{1,0:T(8,128)(2,1)S(1)}, bf16[32,1024]{1,0:T(8,128)(2,1)S(1)}) custom-call(f32[2,72,128]{2,1,0:T(8,128)S(1)} %pad_maximum_fusion.refs_0_, f32[2,72,128]{2,1,0:T(8,128)S(1)} %collective-permute-done.1.refs_1_, ...), custom_call_target="tpu_custom_call" | custom-call | flops 19660800 | bytes 1310720 | tf_op jit(solution)/shard_map/strips0/pallas_call | solution.py:343
  15.6 0.0 collective-permute-done.5.refs_0_.refs_5_
  15.6 0.0 collective-permute-done.6.refs_1_.refs_6_
  15.6 0.2 collective-permute-start.7
  15.8 0.4 %collective-permute-start.8 = (f32[2,72,128]{2,1,0:T(8,128)S(1)}, f32[2,72,128]{2,1,0:T(8,128)S(1)}, u32[]{:S(2)}, u32[]{:S(2)}) collective-permute-start(f32[2,72,128]{2,1,0:T(8,128)S(1)} %collective-permute-done.6.refs_1_.refs_6_), channel_id=1, source_target_pairs={{0,1},{1,0},{2,3},{3,2},{4,5},{5,4},{6,7},{7,6},{8,9},{9,8},{10,11... | collective-permute-start | bytes 221192 | tf_op jit(solution)/shard_map/ppermute | solution.py:363
  16.2 0.1 maximum_maximum_fusion.refs_9_
  16.2 2.4 %strips4.1 = (bf16[11,256,256]{2,1,0:T(8,128)(2,1)S(1)}, f32[32,1536]{1,0:T(8,128)S(1)}, bf16[32,1536]{1,0:T(8,128)(2,1)S(1)}, bf16[32,1536]{1,0:T(8,128)(2,1)S(1)}) custom-call(f32[2,72,128]{2,1,0:T(8,128)S(1)} %collective-permute-done.5.refs_0_.refs_5_, f32[2,72,128]{2,1,0:T(8,128)S(1)} %collective-permute-done.6.refs_1_.refs_6_, ...), custom_call_target="tpu_custom_call" | custom-call | flops 21626880 | bytes 1441792 | tf_op jit(solution)/shard_map/strips4/pallas_call | solution.py:343
  18.7 0.0 collective-permute-done.7.refs_7_
  18.7 0.0 collective-permute-done.8.refs_8_
  18.7 8.5 %iterate.1 = (f32[32,128]{1,0:T(8,128)}, f32[32,128]{1,0:T(8,128)}) custom-call(f32[2,72,128]{2,1,0:T(8,128)S(1)} %pad_maximum_fusion.refs_0_, f32[2,72,128]{2,1,0:T(8,128)S(1)} %collective-permute-done.1.refs_1_, f32[2,72,128]{2,1,0:T(8,128)S(1)} %collective-permute-done.2.refs_2_, f32[1,72,128]{2,1,0:T(8,128)S(1)} %collective-permute-done.3.refs_3_, ...), custom_call_target="tpu_custom_call" | custom-call | tf_op jit(solution)/shard_map/iterate/pallas_call | solution.py:375
  (3 shorter events, 0.0 us)
Async XLA Ops:
  1.5 6.1 %collective-permute-start = (f32[1,72,128]{2,1,0:T(8,128)S(1)}, f32[1,72,128]{2,1,0:T(8,128)S(1)}, u32[]{:S(2)}, u32[]{:S(2)}) collective-permute-start(f32[1,72,128]{2,1,0:T(8,128)S(1)} %bitcast.3), channel_id=1, source_target_pairs={{0,1},{1,0},{2,3},{3,2},{4,5},{5,4},{6,7},{7,6},{8,9},{9,8},{10,11... | collective-permute-start | bytes 110600 | tf_op jit(solution)/shard_map/ppermute | solution.py:316
  2.0 8.9 %collective-permute-start.3 = (f32[1,72,128]{2,1,0:T(8,128)S(1)}, f32[1,72,128]{2,1,0:T(8,128)S(1)}, u32[]{:S(2)}, u32[]{:S(2)}) collective-permute-start(f32[1,72,128]{2,1,0:T(8,128)S(1)} %bitcast.4), channel_id=1, source_target_pairs={{0,14},{1,15},{2,12},{3,13},{4,10},{5,11},{6,8},{7,9},{8,6},{9,7},... | collective-permute-start | bytes 110600 | tf_op jit(solution)/shard_map/ppermute | solution.py:313
  7.6 4.4 %collective-permute-start.1 = (f32[2,72,128]{2,1,0:T(8,128)S(1)}, f32[2,72,128]{2,1,0:T(8,128)S(1)}, u32[]{:S(2)}, u32[]{:S(2)}) collective-permute-start(f32[2,72,128]{2,1,0:T(8,128)S(1)} %pad_maximum_fusion.refs_0_), channel_id=1, source_target_pairs={{0,2},{1,5},{2,0},{3,7},{4,6},{5,1},{6,4},{7,3},{8,10},{9,13},{10,... | collective-permute-start | bytes 221192 | tf_op jit(solution)/shard_map/ppermute | solution.py:313
  8.2 7.3 %collective-permute-start.5 = (f32[2,72,128]{2,1,0:T(8,128)S(1)}, f32[2,72,128]{2,1,0:T(8,128)S(1)}, u32[]{:S(2)}, u32[]{:S(2)}) collective-permute-start(f32[2,72,128]{2,1,0:T(8,128)S(1)} %pad_maximum_fusion.refs_0_), channel_id=1, source_target_pairs={{0,6},{1,9},{2,4},{3,11},{4,2},{5,13},{6,0},{7,15},{8,14},{9,1},{1... | collective-permute-start | bytes 221192 | tf_op jit(solution)/shard_map/ppermute | solution.py:313
  8.8 6.8 %collective-permute-start.6 = (f32[2,72,128]{2,1,0:T(8,128)S(1)}, f32[2,72,128]{2,1,0:T(8,128)S(1)}, u32[]{:S(2)}, u32[]{:S(2)}) collective-permute-start(f32[2,72,128]{2,1,0:T(8,128)S(1)} %pad_maximum_fusion.refs_0_), channel_id=1, source_target_pairs={{0,10},{1,13},{2,8},{3,15},{4,14},{5,9},{6,12},{7,11},{8,2},{9,5},... | collective-permute-start | bytes 221192 | tf_op jit(solution)/shard_map/ppermute | solution.py:313
  10.9 1.5 %collective-permute-start.4 = (f32[1,72,128]{2,1,0:T(8,128)S(1)}, f32[1,72,128]{2,1,0:T(8,128)S(1)}, u32[]{:S(2)}, u32[]{:S(2)}) collective-permute-start(f32[1,72,128]{2,1,0:T(8,128)S(1)} %collective-permute-done.3.refs_3_), channel_id=1, source_target_pairs={{0,1},{1,0},{2,3},{3,2},{4,5},{5,4},{6,7},{7,6},{8,9},{9,8},{10,11... | collective-permute-start | bytes 110600 | tf_op jit(solution)/shard_map/ppermute | solution.py:363
  12.0 1.3 %collective-permute-start.2 = (f32[2,72,128]{2,1,0:T(8,128)S(1)}, f32[2,72,128]{2,1,0:T(8,128)S(1)}, u32[]{:S(2)}, u32[]{:S(2)}) collective-permute-start(f32[2,72,128]{2,1,0:T(8,128)S(1)} %collective-permute-done.1.refs_1_), channel_id=1, source_target_pairs={{0,1},{1,0},{2,3},{3,2},{4,5},{5,4},{6,7},{7,6},{8,9},{9,8},{10,11... | collective-permute-start | bytes 221192 | tf_op jit(solution)/shard_map/ppermute | solution.py:363
  15.6 3.1 %collective-permute-start.7 = (f32[2,72,128]{2,1,0:T(8,128)S(1)}, f32[2,72,128]{2,1,0:T(8,128)S(1)}, u32[]{:S(2)}, u32[]{:S(2)}) collective-permute-start(f32[2,72,128]{2,1,0:T(8,128)S(1)} %collective-permute-done.5.refs_0_.refs_5_), channel_id=1, source_target_pairs={{0,1},{1,0},{2,3},{3,2},{4,5},{5,4},{6,7},{7,6},{8,9},{9,8},{10,11... | collective-permute-start | bytes 221192 | tf_op jit(solution)/shard_map/ppermute | solution.py:363
  15.8 2.9 %collective-permute-start.8 = (f32[2,72,128]{2,1,0:T(8,128)S(1)}, f32[2,72,128]{2,1,0:T(8,128)S(1)}, u32[]{:S(2)}, u32[]{:S(2)}) collective-permute-start(f32[2,72,128]{2,1,0:T(8,128)S(1)} %collective-permute-done.6.refs_1_.refs_6_), channel_id=1, source_target_pairs={{0,1},{1,0},{2,3},{3,2},{4,5},{5,4},{6,7},{7,6},{8,9},{9,8},{10,11... | collective-permute-start | bytes 221192 | tf_op jit(solution)/shard_map/ppermute | solution.py:363

commit v9 on v8

--- a/solution.py
+++ b/solution.py
@@ -146,8 +146,8 @@
         )
 
     def fill(k, source):
-        for r in range(0, BLOCK, 32):
-            table[k, r : r + 32, :] = green(source[r : r + 32, :])
+        for r in range(0, BLOCK, 64):
+            table[k, r : r + 64, :] = green(source[r : r + 64, :])
 
     def products(k, valid=None):
         j, i = place(k)

time: 27.4 us -> 27.4 us (level)
  no operation moved by 1% of the time
where the time goes in v9:
time: 27.4 us; the launch traced here: 27.2 us
  Pallas kernels  14.1 us (51%)
  starting transfers between devices  10.5 us (38%)
  waiting for transfers between devices  1.68 us (6%)
  between operations  0.68 us (2%)
    ppermute x4, starting transfers between devices, fetch(): return lax.ppermute(array, names, pairs)  8.82 us
    pallas_call x1, Pallas kernels, replicated_shards(): pl.pallas_call(functools.partial(iterate_kernel, pieces, new, blocks, col...  8.54 us
    pallas_call x2, Pallas kernels, strips(): pl.pallas_call(functools.partial(strips_kernel, len(data), old, new, colu...  4.71 us
    ppermute x4, starting transfers between devices, swapped(): return lax.ppermute(array, 'sub', swap)  1.2 us
    ppermute x4, waiting for transfers between devices, swapped(): return lax.ppermute(array, 'sub', swap)  1.15 us
    pallas_call x1, Pallas kernels, replicated_shards(): pl.pallas_call(pack_kernel, out_shape=(jax.ShapeDtypeStruct((8 + 2 * colu...  0.81 us
  transfers between devices with their start and end apart: 9, of which 3 were waited for; matrix products, arithmetic and copies ran while one was open for 1% of the time, Pallas kernels for 17%

profile of v9, /device:TPU:0, one launch (start us, length us, event | category | flops | bytes accessed | tf_op | source)
XLA Modules:
  0.0 27.2 jit_solution(6399366165657831980)
XLA Ops:
  0.6 0.8 %pack.1 = (f32[72,128]{1,0:T(8,128)S(1)}, s32[1,128]{1,0:T(1,128)S(1)}) custom-call(f32[3,128]{1,0:T(4,128)} %points.1, f32[1,128]{1,0:T(1,128)} %bitcast.7, f32[32,128]{1,0:T(8,128)} %density.1, f32[32,128]{1,0:T(8,128)} %incident.1, s32[16,128]{1,0:T(8,128)} %bitcast.6), custom_call_target="tpu_custom_call" | custom-call | tf_op jit(solution)/shard_map/pack/pallas_call | solution.py:296
  1.5 0.5 %collective-permute-start = (f32[1,72,128]{2,1,0:T(8,128)S(1)}, f32[1,72,128]{2,1,0:T(8,128)S(1)}, u32[]{:S(2)}, u32[]{:S(2)}) collective-permute-start(f32[1,72,128]{2,1,0:T(8,128)S(1)} %bitcast.3), channel_id=1, source_target_pairs={{0,1},{1,0},{2,3},{3,2},{4,5},{5,4},{6,7},{7,6},{8,9},{9,8},{10,11... | collective-permute-start | bytes 110600 | tf_op jit(solution)/shard_map/ppermute | solution.py:316
  2.0 5.6 %collective-permute-start.3 = (f32[1,72,128]{2,1,0:T(8,128)S(1)}, f32[1,72,128]{2,1,0:T(8,128)S(1)}, u32[]{:S(2)}, u32[]{:S(2)}) collective-permute-start(f32[1,72,128]{2,1,0:T(8,128)S(1)} %bitcast.4), channel_id=1, source_target_pairs={{0,14},{1,15},{2,12},{3,13},{4,10},{5,11},{6,8},{7,9},{8,6},{9,7},... | collective-permute-start | bytes 110600 | tf_op jit(solution)/shard_map/ppermute | solution.py:313
  7.6 0.0 collective-permute-done
  7.6 0.6 %collective-permute-start.1 = (f32[2,72,128]{2,1,0:T(8,128)S(1)}, f32[2,72,128]{2,1,0:T(8,128)S(1)}, u32[]{:S(2)}, u32[]{:S(2)}) collective-permute-start(f32[2,72,128]{2,1,0:T(8,128)S(1)} %pad_maximum_fusion.refs_0_), channel_id=1, source_target_pairs={{0,2},{1,5},{2,0},{3,7},{4,6},{5,1},{6,4},{7,3},{8,10},{9,13},{10,... | collective-permute-start | bytes 221192 | tf_op jit(solution)/shard_map/ppermute | solution.py:313
  8.2 0.1 cosine_multiply_fusion
  8.2 0.5 %collective-permute-start.5 = (f32[2,72,128]{2,1,0:T(8,128)S(1)}, f32[2,72,128]{2,1,0:T(8,128)S(1)}, u32[]{:S(2)}, u32[]{:S(2)}) collective-permute-start(f32[2,72,128]{2,1,0:T(8,128)S(1)} %pad_maximum_fusion.refs_0_), channel_id=1, source_target_pairs={{0,6},{1,9},{2,4},{3,11},{4,2},{5,13},{6,0},{7,15},{8,14},{9,1},{1... | collective-permute-start | bytes 221192 | tf_op jit(solution)/shard_map/ppermute | solution.py:313
  8.8 2.1 %collective-permute-start.6 = (f32[2,72,128]{2,1,0:T(8,128)S(1)}, f32[2,72,128]{2,1,0:T(8,128)S(1)}, u32[]{:S(2)}, u32[]{:S(2)}) collective-permute-start(f32[2,72,128]{2,1,0:T(8,128)S(1)} %pad_maximum_fusion.refs_0_), channel_id=1, source_target_pairs={{0,10},{1,13},{2,8},{3,15},{4,14},{5,9},{6,12},{7,11},{8,2},{9,5},... | collective-permute-start | bytes 221192 | tf_op jit(solution)/shard_map/ppermute | solution.py:313
  10.9 0.0 collective-permute-done.3.refs_3_
  10.9 0.6 %collective-permute-start.4 = (f32[1,72,128]{2,1,0:T(8,128)S(1)}, f32[1,72,128]{2,1,0:T(8,128)S(1)}, u32[]{:S(2)}, u32[]{:S(2)}) collective-permute-start(f32[1,72,128]{2,1,0:T(8,128)S(1)} %collective-permute-done.3.refs_3_), channel_id=1, source_target_pairs={{0,1},{1,0},{2,3},{3,2},{4,5},{5,4},{6,7},{7,6},{8,9},{9,8},{10,11... | collective-permute-start | bytes 110600 | tf_op jit(solution)/shard_map/ppermute | solution.py:363
  11.5 0.5 %collective-permute-done.1.refs_1_ = f32[2,72,128]{2,1,0:T(8,128)S(1)} collective-permute-done((f32[2,72,128]{2,1,0:T(8,128)S(1)}, f32[2,72,128]{2,1,0:T(8,128)S(1)}, u32[]{:S(2)}, u32[]{:S(2)}) %collective-permute-start.1) | collective-permute-done | bytes 73760 | tf_op jit(solution)/shard_map/ppermute | solution.py:313
  12.0 0.0 collective-permute-start.2
  12.1 0.1 pad.3.clone
  12.1 0.2 collective-permute-done.4.refs_4_
  12.4 0.9 %collective-permute-done.2.refs_2_ = f32[2,72,128]{2,1,0:T(8,128)S(1)} collective-permute-done((f32[2,72,128]{2,1,0:T(8,128)S(1)}, f32[2,72,128]{2,1,0:T(8,128)S(1)}, u32[]{:S(2)}, u32[]{:S(2)}) %collective-permute-start.2) | collective-permute-done | bytes 73760 | tf_op jit(solution)/shard_map/ppermute | solution.py:363
  13.3 2.3 %strips0.1 = (bf16[10,256,256]{2,1,0:T(8,128)(2,1)S(1)}, f32[32,1024]{1,0:T(8,128)S(1)}, bf16[32,1024]{1,0:T(8,128)(2,1)S(1)}, bf16[32,1024]{1,0:T(8,128)(2,1)S(1)}) custom-call(f32[2,72,128]{2,1,0:T(8,128)S(1)} %pad_maximum_fusion.refs_0_, f32[2,72,128]{2,1,0:T(8,128)S(1)} %collective-permute-done.1.refs_1_, ...), custom_call_target="tpu_custom_call" | custom-call | flops 19660800 | bytes 1310720 | tf_op jit(solution)/shard_map/strips0/pallas_call | solution.py:343
  15.6 0.0 collective-permute-done.5.refs_0_.refs_5_
  15.6 0.0 collective-permute-done.6.refs_1_.refs_6_
  15.6 0.2 collective-permute-start.7
  15.8 0.4 %collective-permute-start.8 = (f32[2,72,128]{2,1,0:T(8,128)S(1)}, f32[2,72,128]{2,1,0:T(8,128)S(1)}, u32[]{:S(2)}, u32[]{:S(2)}) collective-permute-start(f32[2,72,128]{2,1,0:T(8,128)S(1)} %collective-permute-done.6.refs_1_.refs_6_), channel_id=1, source_target_pairs={{0,1},{1,0},{2,3},{3,2},{4,5},{5,4},{6,7},{7,6},{8,9},{9,8},{10,11... | collective-permute-start | bytes 221192 | tf_op jit(solution)/shard_map/ppermute | solution.py:363
  16.2 0.1 maximum_maximum_fusion.refs_9_
  16.2 2.4 %strips4.1 = (bf16[11,256,256]{2,1,0:T(8,128)(2,1)S(1)}, f32[32,1536]{1,0:T(8,128)S(1)}, bf16[32,1536]{1,0:T(8,128)(2,1)S(1)}, bf16[32,1536]{1,0:T(8,128)(2,1)S(1)}) custom-call(f32[2,72,128]{2,1,0:T(8,128)S(1)} %collective-permute-done.5.refs_0_.refs_5_, f32[2,72,128]{2,1,0:T(8,128)S(1)} %collective-permute-done.6.refs_1_.refs_6_, ...), custom_call_target="tpu_custom_call" | custom-call | flops 21626880 | bytes 1441792 | tf_op jit(solution)/shard_map/strips4/pallas_call | solution.py:343
  18.7 0.0 collective-permute-done.7.refs_7_
  18.7 0.0 collective-permute-done.8.refs_8_
  18.7 8.5 %iterate.1 = (f32[32,128]{1,0:T(8,128)}, f32[32,128]{1,0:T(8,128)}) custom-call(f32[2,72,128]{2,1,0:T(8,128)S(1)} %pad_maximum_fusion.refs_0_, f32[2,72,128]{2,1,0:T(8,128)S(1)} %collective-permute-done.1.refs_1_, f32[2,72,128]{2,1,0:T(8,128)S(1)} %collective-permute-done.2.refs_2_, f32[1,72,128]{2,1,0:T(8,128)S(1)} %collective-permute-done.3.refs_3_, ...), custom_call_target="tpu_custom_call" | custom-call | tf_op jit(solution)/shard_map/iterate/pallas_call | solution.py:375
  (3 shorter events, 0.0 us)
Async XLA Ops:
  1.5 6.1 %collective-permute-start = (f32[1,72,128]{2,1,0:T(8,128)S(1)}, f32[1,72,128]{2,1,0:T(8,128)S(1)}, u32[]{:S(2)}, u32[]{:S(2)}) collective-permute-start(f32[1,72,128]{2,1,0:T(8,128)S(1)} %bitcast.3), channel_id=1, source_target_pairs={{0,1},{1,0},{2,3},{3,2},{4,5},{5,4},{6,7},{7,6},{8,9},{9,8},{10,11... | collective-permute-start | bytes 110600 | tf_op jit(solution)/shard_map/ppermute | solution.py:316
  2.0 8.9 %collective-permute-start.3 = (f32[1,72,128]{2,1,0:T(8,128)S(1)}, f32[1,72,128]{2,1,0:T(8,128)S(1)}, u32[]{:S(2)}, u32[]{:S(2)}) collective-permute-start(f32[1,72,128]{2,1,0:T(8,128)S(1)} %bitcast.4), channel_id=1, source_target_pairs={{0,14},{1,15},{2,12},{3,13},{4,10},{5,11},{6,8},{7,9},{8,6},{9,7},... | collective-permute-start | bytes 110600 | tf_op jit(solution)/shard_map/ppermute | solution.py:313
  7.6 4.4 %collective-permute-start.1 = (f32[2,72,128]{2,1,0:T(8,128)S(1)}, f32[2,72,128]{2,1,0:T(8,128)S(1)}, u32[]{:S(2)}, u32[]{:S(2)}) collective-permute-start(f32[2,72,128]{2,1,0:T(8,128)S(1)} %pad_maximum_fusion.refs_0_), channel_id=1, source_target_pairs={{0,2},{1,5},{2,0},{3,7},{4,6},{5,1},{6,4},{7,3},{8,10},{9,13},{10,... | collective-permute-start | bytes 221192 | tf_op jit(solution)/shard_map/ppermute | solution.py:313
  8.2 7.3 %collective-permute-start.5 = (f32[2,72,128]{2,1,0:T(8,128)S(1)}, f32[2,72,128]{2,1,0:T(8,128)S(1)}, u32[]{:S(2)}, u32[]{:S(2)}) collective-permute-start(f32[2,72,128]{2,1,0:T(8,128)S(1)} %pad_maximum_fusion.refs_0_), channel_id=1, source_target_pairs={{0,6},{1,9},{2,4},{3,11},{4,2},{5,13},{6,0},{7,15},{8,14},{9,1},{1... | collective-permute-start | bytes 221192 | tf_op jit(solution)/shard_map/ppermute | solution.py:313
  8.8 6.8 %collective-permute-start.6 = (f32[2,72,128]{2,1,0:T(8,128)S(1)}, f32[2,72,128]{2,1,0:T(8,128)S(1)}, u32[]{:S(2)}, u32[]{:S(2)}) collective-permute-start(f32[2,72,128]{2,1,0:T(8,128)S(1)} %pad_maximum_fusion.refs_0_), channel_id=1, source_target_pairs={{0,10},{1,13},{2,8},{3,15},{4,14},{5,9},{6,12},{7,11},{8,2},{9,5},... | collective-permute-start | bytes 221192 | tf_op jit(solution)/shard_map/ppermute | solution.py:313
  10.9 1.5 %collective-permute-start.4 = (f32[1,72,128]{2,1,0:T(8,128)S(1)}, f32[1,72,128]{2,1,0:T(8,128)S(1)}, u32[]{:S(2)}, u32[]{:S(2)}) collective-permute-start(f32[1,72,128]{2,1,0:T(8,128)S(1)} %collective-permute-done.3.refs_3_), channel_id=1, source_target_pairs={{0,1},{1,0},{2,3},{3,2},{4,5},{5,4},{6,7},{7,6},{8,9},{9,8},{10,11... | collective-permute-start | bytes 110600 | tf_op jit(solution)/shard_map/ppermute | solution.py:363
  12.0 1.3 %collective-permute-start.2 = (f32[2,72,128]{2,1,0:T(8,128)S(1)}, f32[2,72,128]{2,1,0:T(8,128)S(1)}, u32[]{:S(2)}, u32[]{:S(2)}) collective-permute-start(f32[2,72,128]{2,1,0:T(8,128)S(1)} %collective-permute-done.1.refs_1_), channel_id=1, source_target_pairs={{0,1},{1,0},{2,3},{3,2},{4,5},{5,4},{6,7},{7,6},{8,9},{9,8},{10,11... | collective-permute-start | bytes 221192 | tf_op jit(solution)/shard_map/ppermute | solution.py:363
  15.6 3.1 %collective-permute-start.7 = (f32[2,72,128]{2,1,0:T(8,128)S(1)}, f32[2,72,128]{2,1,0:T(8,128)S(1)}, u32[]{:S(2)}, u32[]{:S(2)}) collective-permute-start(f32[2,72,128]{2,1,0:T(8,128)S(1)} %collective-permute-done.5.refs_0_.refs_5_), channel_id=1, source_target_pairs={{0,1},{1,0},{2,3},{3,2},{4,5},{5,4},{6,7},{7,6},{8,9},{9,8},{10,11... | collective-permute-start | bytes 221192 | tf_op jit(solution)/shard_map/ppermute | solution.py:363
  15.8 2.9 %collective-permute-start.8 = (f32[2,72,128]{2,1,0:T(8,128)S(1)}, f32[2,72,128]{2,1,0:T(8,128)S(1)}, u32[]{:S(2)}, u32[]{:S(2)}) collective-permute-start(f32[2,72,128]{2,1,0:T(8,128)S(1)} %collective-permute-done.6.refs_1_.refs_6_), channel_id=1, source_target_pairs={{0,1},{1,0},{2,3},{3,2},{4,5},{5,4},{6,7},{7,6},{8,9},{9,8},{10,11... | collective-permute-start | bytes 221192 | tf_op jit(solution)/shard_map/ppermute | solution.py:363
